TPU v7x, 32 devices: a whole 2x2x4 slice. The times are simulated.
32 devices in a mesh: freq: 2 (over core), depth: 16 (over z, y, x).
Axes of the slice: x: 2, y: 2, z: 4, core: 2. Of those that a mesh axis runs over, the one named last changes fastest.
Arguments:
- green_source: bfloat16 [4, 16, 384, 2, 256], P('freq', 'depth'), may hold values from -6 to 6
- green_receiver: bfloat16 [4, 16, 128, 2, 256], P('freq', 'depth'), may hold values from -6 to 6
- source_index: int32 [1024], replicated, may hold values from 0 to 383
- receiver_index: int32 [1024], replicated, may hold values from 0 to 127
- frequency_bins: int32 [4], P('freq'), may hold values from 0 to 127
- depth_profile: float32 [16], P('depth'), may hold values from 0.5 to 2
Outputs:
- kernels: float32 [4, 1024, 16], P(None, ('freq', 'depth'))
All inputs are finite; a program needn't handle non-finite values.
Results may differ from a plain program's by a relative error of at most 0.0015.
Values may be sent and summed in bfloat16 or wider, within the bound.
No kernel may reach another device: no remote copies, remote signals or barrier semaphores. Data moves between devices by JAX's collectives and lax.ppermute only.
A program may use at most 64 MiB of HBM per device.

v0:
```python
import math

import jax
import jax.numpy as jnp
from jax import lax
from jax.sharding import PartitionSpec as P

NBINS = 128
WX = 16
WY = 16


def extended(block, sides, width):
    for axis, dim in sides:
        count = lax.axis_size(axis)
        forward = [(i, i + 1) for i in range(count - 1)]
        backward = [(target, source) for source, target in forward]
        low = lax.ppermute(
            lax.slice_in_dim(block, block.shape[dim] - width, None, axis=dim), axis, forward
        )
        high = lax.ppermute(lax.slice_in_dim(block, 0, width, axis=dim), axis, backward)
        block = jnp.concatenate([low, block, high], axis=dim)
    return block


def window_slope(values, direction):
    window = values.reshape(values.shape[:-1] + (WX, WY))
    axis_index = window.ndim - 2 + direction
    extent = window.shape[axis_index]
    widths = [(0, 0)] * axis_index + [(1, 1)] + [(0, 0)] * (window.ndim - axis_index - 1)
    padded = jnp.pad(window, widths)
    upper = lax.slice_in_dim(padded, 2, extent + 2, axis=axis_index)
    lower = lax.slice_in_dim(padded, 0, extent, axis=axis_index)
    return (0.5 * (upper - lower)).reshape(values.shape)


def all_pairs(left, right, flat_index):
    full = jnp.einsum("sam,ram->sr", left, right, preferred_element_type=jnp.float32)
    return full.reshape(-1)[flat_index]


def on_device(
    green_source, green_receiver, source_index, receiver_index, frequency_bins, depth_profile
):
    local_freqs, local_depths, sources, _, cells = green_source.shape
    receivers = green_receiver.shape[2]
    pairs = source_index.shape[0]
    n_freq = lax.axis_size("freq")
    scaled_freq = 0.5 + frequency_bins.astype(jnp.float32) / NBINS
    kernel_scale = 1.0 / math.sqrt(2.0 * WX * WY * local_freqs * n_freq)
    flat_index = source_index * receivers + receiver_index
    sign_table = jnp.array([1.0, -1.0], jnp.bfloat16)[:, None]
    swapped = jnp.flip(green_receiver, axis=3)
    signed = green_receiver * sign_table
    wide_source = green_source.astype(jnp.float32)
    slope_x = window_slope(wide_source, 0).astype(jnp.bfloat16)
    slope_y = window_slope(wide_source, 1).astype(jnp.bfloat16)
    padded = extended(green_source, (("depth", 1),), 1)
    total = jnp.zeros((4, pairs), jnp.float32)
    for freq_slot in range(local_freqs):
        plain = all_pairs(green_source[freq_slot, 0], signed[freq_slot, 0], flat_index)
        along_x = all_pairs(slope_x[freq_slot, 0], swapped[freq_slot, 0], flat_index)
        along_y = all_pairs(slope_y[freq_slot, 0], swapped[freq_slot, 0], flat_index)
        upper = all_pairs(padded[freq_slot, 2], swapped[freq_slot, 0], flat_index)
        lower = all_pairs(padded[freq_slot, 0], swapped[freq_slot, 0], flat_index)
        weight = scaled_freq[freq_slot]
        first = plain * (weight * weight) * depth_profile[0]
        fourth = 0.5 * (upper - lower) * weight
        total = total + jnp.stack([first, along_x * weight, along_y * weight, fourth], axis=0)
    columns = [total * kernel_scale]
    partial_value = jnp.stack(columns, axis=-1)
    summed = lax.psum_scatter(partial_value, "freq", scatter_dimension=1, tiled=True)
    pair_tiles = lax.all_to_all(summed, "depth", split_axis=1, concat_axis=2, tiled=True)
    return pair_tiles


def solution(mesh):
    placed = (
        P("freq", "depth", None, None, None),
        P("freq", "depth", None, None, None),
        P(),
        P(),
        P("freq"),
        P("depth"),
    )
    return jax.shard_map(
        on_device,
        mesh=mesh,
        in_specs=placed,
        out_specs=P(None, ("freq", "depth"), None),
        check_vma=False,
    )
```

profile of v0, /device:TPU:0, one launch (start us, length us, event | category | flops | bytes accessed | tf_op | source)
XLA Modules:
  0.0 130.2 jit_solution(1545392108558428830)
XLA Ops:
  6.5 0.0 copy-start
  6.5 0.0 copy-start.5
  6.5 0.0 copy-start.1
  6.5 0.0 reduce-scatter.4.cloned.1.call-start
  6.5 1.3 %copy.44 = bf16[2,1,384,2,256]{4,2,3,1,0:T(8,128)(2,1)S(1)} copy(bf16[2,1,384,2,256]{4,3,2,1,0:T(2,128)(2,1)} %param.7) | data formatting | bytes 1572864 | tf_op args[0]
  7.9 1.3 collective-permute-start
  9.2 6.4 %collective-permute-start.1 = (bf16[2,1,384,2,256]{4,2,3,1,0:T(8,128)(2,1)S(1)}, bf16[2,1,384,2,256]{4,2,3,1,0:T(8,128)(2,1)}, u32[]{:S(2)}, u32[]{:S(2)}) collective-permute-start(bf16[2,1,384,2,256]{4,2,3,1,0:T(8,128)(2,1)S(1)} %copy.44), channel_id=1, source_target_pairs={{0,1},{1,2},{2,3},{3,4},{4,5},{5,6},{6,7},{7,8},{8,9},{9,10},{10,1... | collective-permute-start | bytes 2359304 | tf_op jit(solution)/shard_map/ppermute | solution.py:18
  15.6 0.0 copy-done
  15.6 0.6 copy.46
  16.2 0.0 copy-done.5
  16.2 0.6 fusion.19
  20.4 0.0 copy-done.1
  20.4 0.2 fusion.18
  20.6 0.7 slice.94
  21.4 0.7 slice.83
  22.1 0.1 convert.1
  22.2 0.6 fusion.2
  22.8 0.1 fusion.16
  22.9 0.0 copy-start.2
  22.9 0.0 copy-start.3
  22.9 0.1 fusion.17
  23.0 0.3 convolution_bitcast_fusion.3
  23.3 0.3 convolution_bitcast_fusion.2
  23.6 0.0 copy-done.2
  23.6 0.0 copy-done.3
  23.6 6.2 %gather_fusion.6 = f32[1024]{0:T(1024)S(1)} fusion(f32[49152]{0:T(1024)S(1)} %convolution_bitcast_fusion.3, s32[1024]{0:T(1024)S(1)} %fusion.15), kind=kCustom, calls=%fused_computation.6 | custom fusion | bytes 12288 | tf_op jit(solution)/shard_map/gather | solution.py:39
  29.8 6.2 %gather_fusion.7 = f32[1024]{0:T(1024)S(1)} fusion(f32[49152]{0:T(1024)S(1)} %convolution_bitcast_fusion.2, s32[1024]{0:T(1024)S(1)} %fusion.15), kind=kCustom, calls=%fused_computation.7 | custom fusion | bytes 12288 | tf_op jit(solution)/shard_map/gather | solution.py:39
  36.0 0.3 convolution_bitcast_fusion.7
  36.3 6.2 %gather_fusion.1 = f32[1024]{0:T(1024)S(1)} fusion(f32[49152]{0:T(1024)S(1)} %convolution_bitcast_fusion.7, s32[1024]{0:T(1024)S(1)} %fusion.15), kind=kCustom, calls=%fused_computation.1 | custom fusion | bytes 12288 | tf_op jit(solution)/shard_map/gather | solution.py:39
  42.4 0.3 convolution_bitcast_fusion.6
  42.7 0.0 copy-start.4
  42.7 6.2 %gather_fusion.2 = f32[1024]{0:T(1024)S(1)} fusion(f32[49152]{0:T(1024)S(1)} %convolution_bitcast_fusion.6, s32[1024]{0:T(1024)S(1)} %fusion.15), kind=kCustom, calls=%fused_computation.2 | custom fusion | bytes 12288 | tf_op jit(solution)/shard_map/gather | solution.py:39
  48.9 0.0 copy-done.4
  48.9 0.1 copy_multiply_fusion
  49.0 0.3 convolution_bitcast_fusion.9
  49.3 0.1 copy.45
  49.4 6.2 %gather_fusion = f32[1024]{0:T(1024)S(1)} fusion(f32[49152]{0:T(1024)S(1)} %bitcast.103, s32[1024]{0:T(1024)S(1)} %fusion.15), kind=kCustom, calls=%fused_computation | custom fusion | bytes 12288 | tf_op jit(solution)/shard_map/gather | solution.py:39
  55.6 0.3 convolution_bitcast_fusion.8
  55.9 0.1 copy.56
  56.0 6.2 %gather_fusion.5 = f32[1024]{0:T(1024)S(1)} fusion(f32[49152]{0:T(1024)S(1)} %bitcast.104, s32[1024]{0:T(1024)S(1)} %fusion.15), kind=kCustom, calls=%fused_computation.5 | custom fusion | bytes 12288 | tf_op jit(solution)/shard_map/gather | solution.py:39
  62.8 0.7 broadcast_multiply_fusion
  63.5 0.6 broadcast_multiply_fusion.2
  64.1 0.0 collective-permute-done
  64.1 1.3 convolution_bitcast_fusion.1
  65.3 6.2 %gather_fusion.8 = f32[1024]{0:T(1024)S(1)} fusion(f32[49152]{0:T(1024)S(1)} %convolution_bitcast_fusion.1, s32[1024]{0:T(1024)S(1)} %fusion.15), kind=kCustom, calls=%fused_computation.8 | custom fusion | bytes 12288 | tf_op jit(solution)/shard_map/gather | solution.py:39
  71.5 0.0 collective-permute-done.1
  71.5 1.3 convolution_bitcast_fusion
  72.8 6.2 %gather_fusion.9 = f32[1024]{0:T(1024)S(1)} fusion(f32[49152]{0:T(1024)S(1)} %convolution_bitcast_fusion, s32[1024]{0:T(1024)S(1)} %fusion.15), kind=kCustom, calls=%fused_computation.9 | custom fusion | bytes 12288 | tf_op jit(solution)/shard_map/gather | solution.py:39
  78.9 1.3 convolution_bitcast_fusion.5
  80.2 6.2 %gather_fusion.3 = f32[1024]{0:T(1024)S(1)} fusion(f32[49152]{0:T(1024)S(1)} %convolution_bitcast_fusion.5, s32[1024]{0:T(1024)S(1)} %fusion.15), kind=kCustom, calls=%fused_computation.3 | custom fusion | bytes 12288 | tf_op jit(solution)/shard_map/gather | solution.py:39
  86.3 1.3 convolution_bitcast_fusion.4
  87.6 6.2 %gather_fusion.4 = f32[1024]{0:T(1024)S(1)} fusion(f32[49152]{0:T(1024)S(1)} %convolution_bitcast_fusion.4, s32[1024]{0:T(1024)S(1)} %fusion.15), kind=kCustom, calls=%fused_computation.4 | custom fusion | bytes 12288 | tf_op jit(solution)/shard_map/gather | solution.py:39
  93.8 1.0 copy.69
  94.9 0.0 reduce-scatter.4.cloned.1.call-update
  94.9 9.8 %reduce-scatter.4.cloned.1.call-done = f32[512,4]{1,0:T(8,128)} async-done(((f32[1024,4]{1,0:T(8,128)}), f32[512,4]{1,0:T(8,128)}) %reduce-scatter.4.cloned.1.call-update) | async-done | bytes 8208
  104.7 0.5 broadcast.212
  105.2 2.2 %reduce = f32[512,4]{1,0:T(8,128)S(1)} reduce(f32[512,1,4]{2,1,0:T(1,128)} %bitcast.120, f32[]{:T(128)} %broadcast.212), dimensions={1}, to_apply=%bitcast.96.reduce_sub_computation | reduce | bytes 16388
  107.4 0.2 reshape.420
  107.6 13.8 %all_to_all.18 = f32[16,1,128]{2,1,0:T(1,128)S(1)} all-to-all(f32[16,1,128]{2,1,0:T(1,128)S(1)} %reshape.420), channel_id=1, replica_groups=mesh['freq'=2,'depth'=16] {'depth'}, dimensions={0} | all-to-all | bytes 16384 | tf_op jit(solution)/shard_map/all_to_all | solution.py:73
  121.4 0.7 reduce.1
  122.1 0.5 reshape.421
  122.6 0.8 copy.64
  (6 shorter events, 0.1 us)
Async XLA Ops:
  6.5 9.0 %copy-start = (bf16[2,1,384,2,256]{4,3,2,1,0:T(2,128)(2,1)S(1)}, bf16[2,1,384,2,256]{4,3,2,1,0:T(2,128)(2,1)}, u32[]{:S(2)}) copy-start(bf16[2,1,384,2,256]{4,3,2,1,0:T(2,128)(2,1)} %param.7) | copy-start | bytes 2359300
  6.5 9.7 %copy-start.5 = (s32[2]{0:T(128)S(1)}, s32[2]{0:T(128)}, u32[]{:S(2)}) copy-start(s32[2]{0:T(128)} %param.11) | copy-start | bytes 28
  6.5 13.9 %copy-start.1 = (bf16[2,1,128,2,256]{4,3,2,1,0:T(2,128)(2,1)S(1)}, bf16[2,1,128,2,256]{4,3,2,1,0:T(2,128)(2,1)}, u32[]{:S(2)}) copy-start(bf16[2,1,128,2,256]{4,3,2,1,0:T(2,128)(2,1)} %param.8) | copy-start | bytes 786436
  6.5 98.1 %reduce-scatter.4.cloned.1.call-start = ((), (), s32[]{:S(2)}) async-start(), calls=%async_computation.2 | async-start | bytes 786432
  7.9 56.2 %collective-permute-start = (bf16[2,1,384,2,256]{4,2,3,1,0:T(8,128)(2,1)S(1)}, bf16[2,1,384,2,256]{4,2,3,1,0:T(8,128)(2,1)}, u32[]{:S(2)}, u32[]{:S(2)}) collective-permute-start(bf16[2,1,384,2,256]{4,2,3,1,0:T(8,128)(2,1)S(1)} %copy.44), channel_id=1, source_target_pairs={{1,0},{2,1},{3,2},{4,3},{5,4},{6,5},{7,6},{8,7},{9,8},{10,9},{11,1... | collective-permute-start | bytes 2359304 | tf_op jit(solution)/shard_map/ppermute | solution.py:21
  9.2 62.3 %collective-permute-start.1 = (bf16[2,1,384,2,256]{4,2,3,1,0:T(8,128)(2,1)S(1)}, bf16[2,1,384,2,256]{4,2,3,1,0:T(8,128)(2,1)}, u32[]{:S(2)}, u32[]{:S(2)}) collective-permute-start(bf16[2,1,384,2,256]{4,2,3,1,0:T(8,128)(2,1)S(1)} %copy.44), channel_id=1, source_target_pairs={{0,1},{1,2},{2,3},{3,4},{4,5},{5,6},{6,7},{7,8},{8,9},{9,10},{10,1... | collective-permute-start | bytes 2359304 | tf_op jit(solution)/shard_map/ppermute | solution.py:18
  22.9 0.7 copy-start.2
  22.9 0.7 copy-start.3
  42.7 6.2 %copy-start.4 = (bf16[2]{0:T(256)(128)(2,1)S(1)}, bf16[2]{0:T(256)(128)(2,1)}, u32[]{:S(2)}) copy-start(bf16[2]{0:T(256)(128)(2,1)} %constant.20.clone) | copy-start | bytes 16
Sparse Core Ops, SparseCore 0:
  95.0 9.5 reduce-scatter.3
where the time goes:
time: 131 us; the launch traced here: 130 us
  local copies, waits for them, and re-layouts  69.1 us (53%)
  between operations  18 us (14%)
  blocking collectives  13.8 us (11%)
  waiting for transfers between devices  9.78 us (7%)
  starting transfers between devices  7.69 us (6%)
  matrix products  6.79 us (5%)
  other arithmetic  4.99 us (4%)
    gather x10, local copies, waits for them, and re-layouts, all_pairs(): return full.reshape(-1)[flat_index]  61.5 us
    all_to_all x1, blocking collectives, on_device(): lax.all_to_all(summed, 'depth', split_axis=1, concat_axis=2, tiled=True)  13.8 us
    unnamed x2, waiting for transfers between devices  9.77 us
    dot_general x10, matrix products, all_pairs(): jnp.einsum('sam,ram->sr', left, right, preferred_element_type=jnp.float32)  6.79 us
    ppermute x1, starting transfers between devices, extended(): lax.ppermute(lax.slice_in_dim(block, block.shape[dim] - width, None, axis...  6.4 us
    unnamed x18, local copies, waits for them, and re-layouts  4.18 us
  transfers between devices with their start and end apart: 3, of which 1 were waited for; matrix products, arithmetic and copies ran while one was open for 39% of the time, Pallas kernels for 0%

commit v1 on v0

v1 whole, which is shorter than its diff:
```python
import functools
import math

import jax
import jax.numpy as jnp
from jax import lax
from jax.experimental import pallas as pl
from jax.experimental.pallas import tpu as pltpu
from jax.sharding import PartitionSpec as P

NBINS = 128
WX = 16
WY = 16
LANES = 128
ROWS = 8
VMEM_BYTES = 48 * 1024 * 1024

TRANSPOSED = (((1,), (1,)), ((), ()))


def dot(left, right):
    return jnp.dot(left, right, preferred_element_type=jnp.float32)


def dot_t(left, right):
    return lax.dot_general(left, right, TRANSPOSED, preferred_element_type=jnp.float32)


def frequency_weight(bins_ref, slot):
    return 0.5 + bins_ref[slot].astype(jnp.float32) / NBINS


def slope_table(cells):
    source = lax.broadcasted_iota(jnp.int32, (cells, cells), 0)
    target = lax.broadcasted_iota(jnp.int32, (cells, cells), 1)
    column = lax.rem(target, WY)
    step = source - target
    half, zero = jnp.float32(0.5), jnp.float32(0.0)
    along_x = jnp.where(step == WY, half, zero) - jnp.where(step == -WY, half, zero)
    along_y = jnp.where((step == 1) & (column != WY - 1), half, zero) - jnp.where(
        (step == -1) & (column != 0), half, zero
    )
    return jnp.concatenate([along_x, along_y], axis=1).astype(jnp.bfloat16)


def pick_pairs(products, source_ref, receiver_ref, count, receivers):
    sources = products.shape[1]
    pairs = source_ref.shape[1]
    at_source = lax.broadcasted_iota(jnp.int32, (sources, pairs), 0) == source_ref[...]
    hot = jnp.where(at_source, jnp.float32(1), jnp.float32(0)).astype(jnp.bfloat16)
    high = products.astype(jnp.bfloat16)
    low = (products - high.astype(jnp.float32)).astype(jnp.bfloat16)
    picked = dot(high, hot) + dot(low, hot)
    at_receiver = lax.broadcasted_iota(jnp.int32, (receivers, pairs), 0) == receiver_ref[...]
    return [
        jnp.sum(
            jnp.where(at_receiver, picked[k * receivers : (k + 1) * receivers], 0.0),
            axis=0,
            keepdims=True,
        )
        for k in range(count)
    ]


def local_terms(
    scale, bins_ref, profile_ref, source_ref, receiver_ref, green_s, green_r, out_ref
):
    freqs, _, _, cells = green_s.shape
    receivers = green_r.shape[2]
    table = slope_table(cells)
    sound = along_x = along_y = 0.0
    for slot in range(freqs):
        weight = frequency_weight(bins_ref, slot)
        real, imag = green_s[slot, 0], green_s[slot, 1]
        slope_real = dot(real, table).astype(jnp.bfloat16)
        slope_imag = dot(imag, table).astype(jnp.bfloat16)
        near_real, near_imag = green_r[slot, 0], green_r[slot, 1]
        plain = dot_t(near_real, real) - dot_t(near_imag, imag)
        slope_x = dot_t(near_imag, slope_real[:, :cells]) + dot_t(near_real, slope_imag[:, :cells])
        slope_y = dot_t(near_imag, slope_real[:, cells:]) + dot_t(near_real, slope_imag[:, cells:])
        sound = sound + plain * (weight * weight * profile_ref[0] * scale)
        along_x = along_x + slope_x * (weight * scale)
        along_y = along_y + slope_y * (weight * scale)
    products = jnp.concatenate([sound, along_x, along_y], axis=0)
    rows = pick_pairs(products, source_ref, receiver_ref, 3, receivers)
    blank = jnp.zeros((ROWS - 3, rows[0].shape[1]), jnp.float32)
    out_ref[...] = jnp.concatenate(rows + [blank], axis=0)


def layer_terms(
    scale, share, bins_ref, source_ref, receiver_ref, green_s, lower_r, upper_r, terms, out_ref
):
    freqs = green_s.shape[0]
    receivers = lower_r.shape[2]
    total = 0.0
    for slot in range(freqs):
        weight = frequency_weight(bins_ref, slot)
        near_real = jnp.concatenate([lower_r[slot, 0], upper_r[slot, 0]], axis=0)
        near_imag = jnp.concatenate([lower_r[slot, 1], upper_r[slot, 1]], axis=0)
        both = dot_t(near_imag, green_s[slot, 0]) + dot_t(near_real, green_s[slot, 1])
        total = total + both * (0.5 * weight * scale)
    rows = pick_pairs(total, source_ref, receiver_ref, 2, receivers)
    blank = jnp.zeros((ROWS - 5, rows[0].shape[1]), jnp.float32)
    block = jnp.concatenate([terms[0:3, :]] + rows + [blank], axis=0)
    for owner in range(out_ref.shape[0]):
        tile = owner * share // LANES
        out_ref[owner] = block[:, tile * LANES : (tile + 1) * LANES]


def combine(freqs, depths, share, parts_ref, out_ref):
    owner = lax.axis_index("freq") * depths + lax.axis_index("depth")
    offset = lax.rem(owner * share, LANES)

    def term(k):
        total = parts_ref[pl.ds(0, depths), k, :]
        for group in range(1, freqs):
            total = total + parts_ref[pl.ds(group * depths, depths), k, :]
        return total

    blank = jnp.zeros((1, LANES), jnp.float32)
    from_above = jnp.concatenate([term(3)[1:], blank], axis=0)
    from_below = jnp.concatenate([blank, term(4)[:-1]], axis=0)
    for k, value in enumerate([term(0), term(1), term(2), from_above - from_below]):
        out_ref[k] = pltpu.roll(value, lax.rem(LANES - offset, LANES), 1)[:, :share]


def vmem(count):
    return [pl.BlockSpec(memory_space=pltpu.VMEM)] * count


def smem(count):
    return [pl.BlockSpec(memory_space=pltpu.SMEM)] * count


def on_device(
    green_source, green_receiver, source_index, receiver_index, frequency_bins, depth_profile
):
    local_freqs, _, sources, _, cells = green_source.shape
    receivers = green_receiver.shape[2]
    pairs = source_index.shape[0]
    n_freq, n_depth = lax.axis_size("freq"), lax.axis_size("depth")
    owners = n_freq * n_depth
    share = pairs // owners
    scale = 1.0 / math.sqrt(2.0 * WX * WY * local_freqs * n_freq)
    params = pltpu.CompilerParams(vmem_limit_bytes=VMEM_BYTES)

    near = jnp.swapaxes(green_receiver[:, 0], 1, 2)
    forward = [(i, i + 1) for i in range(n_depth - 1)]
    backward = [(target, source) for source, target in forward]
    lower = lax.ppermute(near, "depth", forward)
    upper = lax.ppermute(near, "depth", backward)

    far = jnp.swapaxes(green_source[:, 0], 1, 2)
    source_row = source_index.reshape(1, pairs)
    receiver_row = receiver_index.reshape(1, pairs)
    product = 2 * 2 * cells * local_freqs * sources * receivers
    picking = 2 * 2 * sources * receivers * pairs
    terms = pl.pallas_call(
        functools.partial(local_terms, scale),
        out_shape=jax.ShapeDtypeStruct((ROWS, pairs), jnp.float32),
        in_specs=smem(2) + vmem(4),
        out_specs=pl.BlockSpec(memory_space=pltpu.VMEM),
        compiler_params=params,
        cost_estimate=pl.CostEstimate(
            flops=3 * (product + picking), bytes_accessed=1 << 21, transcendentals=0
        ),
        name="local_terms",
    )(frequency_bins, depth_profile, source_row, receiver_row, far, near)
    parts = pl.pallas_call(
        functools.partial(layer_terms, scale, share),
        out_shape=jax.ShapeDtypeStruct((owners, ROWS, LANES), jnp.float32),
        in_specs=smem(1) + vmem(6),
        out_specs=pl.BlockSpec(memory_space=pltpu.VMEM),
        compiler_params=params,
        cost_estimate=pl.CostEstimate(
            flops=2 * (product + picking), bytes_accessed=1 << 21, transcendentals=0
        ),
        name="layer_terms",
    )(frequency_bins, source_row, receiver_row, far, lower, upper, terms)
    parts = lax.all_to_all(parts, ("freq", "depth"), split_axis=0, concat_axis=0, tiled=True)
    kernels = pl.pallas_call(
        functools.partial(combine, n_freq, n_depth, share),
        out_shape=jax.ShapeDtypeStruct((4, n_depth, share), jnp.float32),
        in_specs=vmem(1),
        out_specs=pl.BlockSpec(memory_space=pltpu.VMEM),
        compiler_params=params,
        name="combine",
    )(parts)
    return jnp.swapaxes(kernels, 1, 2)


def solution(mesh):
    placed = (
        P("freq", "depth", None, None, None),
        P("freq", "depth", None, None, None),
        P(),
        P(),
        P("freq"),
        P("depth"),
    )
    return jax.shard_map(
        on_device,
        mesh=mesh,
        in_specs=placed,
        out_specs=P(None, ("freq", "depth"), None),
        check_vma=False,
    )
```

time: 131 us -> 34.1 us (0.26)
  local copies, waits for them, and re-layouts: 69.1 us -> 2.89 us
  between operations: 18 us -> 0.73 us
  matrix products: 6.79 us -> 0 us
  Pallas kernels: 0 us -> 5.11 us
  other arithmetic: 4.99 us -> 0 us
  waiting for transfers between devices: 9.78 us -> 5.72 us
    gather x10 -> x0, local copies, waits for them, and re-layouts: 61.5 us -> none  [all_pairs(): return full.reshape(-1)[flat_index]]
    unnamed x2 -> x0, waiting for transfers between devices: 9.77 us -> none
    dot_general x10 -> x0, matrix products: 6.79 us -> none  [all_pairs(): jnp.einsum('sam,ram->sr', left, right, preferred_element_type=jnp.float32)]
    ppermute x2, waiting for transfers between devices: 0.01 us -> 5.72 us  [the longest x1 5.72 us: on_device(): lower = lax.ppermute(near, 'depth', forward)]
    pallas_call x0 -> x3, Pallas kernels: none -> 5.11 us  [the longest x1 2.74 us: on_device(): pl.pallas_call(functools.partial(local_terms, scale), out_shape=jax.Shape...]
    slice x6 -> x0, local copies, waits for them, and re-layouts: 2.37 us -> none  [the longest x3 1.62 us: on_device(): swapped[freq_slot, 0]]
    unnamed x1 -> x0, other arithmetic: 2.25 us -> none
    mul x7 -> x0, other arithmetic: 1.36 us -> none  [the longest x2 1.2 us: on_device(): along_y * weight]
  transfers between devices with their start and end apart: 3 -> 2, of which waited for: 1 -> 1; matrix products, arithmetic and copies ran while one was open for 39% -> 4% of each run, Pallas kernels for 0% -> 8%
where the time goes in v1:
time: 34.1 us; the launch traced here: 33.9 us
  blocking collectives  12.7 us (37%)
  starting transfers between devices  6.78 us (20%)
  waiting for transfers between devices  5.72 us (17%)
  Pallas kernels  5.11 us (15%)
  local copies, waits for them, and re-layouts  2.89 us (8%)
  between operations  0.73 us (2%)
    all_to_all x1, blocking collectives, on_device(): lax.all_to_all(parts, ('freq', 'depth'), split_axis=0, concat_axis=0, til...  12.7 us
    ppermute x1, waiting for transfers between devices, on_device(): lower = lax.ppermute(near, 'depth', forward)  5.72 us
    ppermute x1, starting transfers between devices, on_device(): lower = lax.ppermute(near, 'depth', forward)  5.49 us
    unnamed x8, local copies, waits for them, and re-layouts  2.89 us
    pallas_call x1, Pallas kernels, on_device(): pl.pallas_call(functools.partial(local_terms, scale), out_shape=jax.Shape...  2.74 us
    pallas_call x1, Pallas kernels, on_device(): pl.pallas_call(functools.partial(layer_terms, scale, share), out_shape=ja...  1.65 us
    ppermute x1, starting transfers between devices, on_device(): upper = lax.ppermute(near, 'depth', backward)  1.29 us
    pallas_call x1, Pallas kernels, on_device(): pl.pallas_call(functools.partial(combine, n_freq, n_depth, share), out_sh...  0.72 us
  transfers between devices with their start and end apart: 2, of which 1 were waited for; matrix products, arithmetic and copies ran while one was open for 4% of the time, Pallas kernels for 8%

profile of v1, /device:TPU:0, one launch (start us, length us, event | category | flops | bytes accessed | tf_op | source)
XLA Modules:
  0.0 33.9 jit_solution(3323867615798388497)
XLA Ops:
  0.0 1.0 %copy.12 = bf16[2,1,128,2,256]{4,2,3,0,1:T(8,128)(2,1)S(1)} copy(bf16[2,1,128,2,256]{4,3,2,1,0:T(2,128)(2,1)} %param.7) | data formatting | bytes 524288 | tf_op args[1]
  1.0 1.3 %collective-permute-start.1 = (bf16[2,2,128,256]{3,2,1,0:T(8,128)(2,1)S(1)}, bf16[2,2,128,256]{3,2,1,0:T(8,128)(2,1)S(1)}, u32[]{:S(2)}, u32[]{:S(2)}) collective-permute-start(bf16[2,2,128,256]{3,2,1,0:T(8,128)(2,1)S(1)} %bitcast.15), channel_id=1, source_target_pairs={{1,0},{2,1},{3,2},{4,3},{5,4},{6,5},{7,6},{8,7},{9,8},{10,9},{11,1... | collective-permute-start | bytes 786440 | tf_op jit(solution)/shard_map/ppermute | solution.py:151
  2.3 5.5 %collective-permute-start = (bf16[2,2,128,256]{3,2,1,0:T(8,128)(2,1)S(1)}, bf16[2,2,128,256]{3,2,1,0:T(8,128)(2,1)S(1)}, u32[]{:S(2)}, u32[]{:S(2)}) collective-permute-start(bf16[2,2,128,256]{3,2,1,0:T(8,128)(2,1)S(1)} %bitcast.16), channel_id=1, source_target_pairs={{0,1},{1,2},{2,3},{3,4},{4,5},{5,6},{6,7},{7,8},{8,9},{9,10},{10,1... | collective-permute-start | bytes 786440 | tf_op jit(solution)/shard_map/ppermute | solution.py:150
  8.4 0.0 copy-start.1
  8.4 1.2 %copy.11 = bf16[2,1,384,2,256]{4,2,3,0,1:T(8,128)(2,1)S(1)} copy(bf16[2,1,384,2,256]{4,3,2,1,0:T(2,128)(2,1)} %param.6) | data formatting | bytes 1572864 | tf_op args[0]
  9.7 0.0 copy-start
  9.7 0.0 copy-start.2
  9.7 0.0 copy-done.1
  9.7 0.7 %copy-done = s32[1024]{0:T(1024)S(1)} copy-done((s32[1024]{0:T(1024)S(1)}, s32[1024]{0:T(1024)}, u32[]{:S(2)}) %copy-start) | copy-done | bytes 4120
  10.4 0.0 copy-done.2
  10.4 2.7 %local_terms.1.terms = f32[8,1024]{1,0:T(8,128)S(1)} custom-call(s32[2]{0:T(128)S(1)} %copy-done.2, f32[1]{0:T(128)S(6)} %copy.13.profile_ref, s32[1,1024]{1,0:T(1,128)S(1)} %bitcast.18, s32[1,1024]{1,0:T(1,128)S(1)} %bitcast.20, bf16[2,2,384,256]{3,2,1,0:T(8,128)(2,1)S(1)} %bitcast.13, bf16[2,2,128,256]{3,2,1,0:T(8,128)(2,1)S(1)} %bitcast.17), custom_call_target="tpu_custom_call" | custom-call | flops 905969664 | bytes 2097152 | tf_op jit(solution)/shard_map/local_terms/pallas_call | solution.py:158
  13.1 0.0 collective-permute-done.1.upper_r
  13.1 5.7 %collective-permute-done.lower_r = bf16[2,2,128,256]{3,2,1,0:T(8,128)(2,1)S(1)} collective-permute-done((bf16[2,2,128,256]{3,2,1,0:T(8,128)(2,1)S(1)}, bf16[2,2,128,256]{3,2,1,0:T(8,128)(2,1)S(1)}, u32[]{:S(2)}, u32[]{:S(2)}) %collective-permute-start) | collective-permute-done | bytes 262176 | tf_op jit(solution)/shard_map/ppermute | solution.py:150
  18.9 1.6 %layer_terms.1 = f32[32,8,128]{2,1,0:T(8,128)S(1)} custom-call(s32[2]{0:T(128)S(1)} %copy-done.2, s32[1,1024]{1,0:T(1,128)S(1)} %bitcast.19, s32[1,1024]{1,0:T(1,128)S(1)} %bitcast.21, bf16[2,2,384,256]{3,2,1,0:T(8,128)(2,1)S(1)} %bitcast.14, bf16[2,2,128,256]{3,2,1,0:T(8,128)(2,1)S(1)} %collective-permute-done.lower_r, ...), custom_call_target="tpu_custom_call" | custom-call | flops 603979776 | bytes 2097152 | tf_op jit(solution)/shard_map/layer_terms/pallas_call | solution.py:169
  20.5 12.7 %all_to_all.5.parts_ref = f32[32,8,128]{2,1,0:T(8,128)S(1)} all-to-all(f32[32,8,128]{2,1,0:T(8,128)S(1)} %layer_terms.1), channel_id=1, replica_groups=mesh['freq'=2,'depth'=16] {'freq','depth'}, dimensions={0} | all-to-all | bytes 262144 | tf_op jit(solution)/shard_map/all_to_all | solution.py:180
  33.2 0.7 %combine.1 = f32[4,16,32]{2,1,0:T(8,128)} custom-call(f32[32,8,128]{2,1,0:T(8,128)S(1)} %all_to_all.5.parts_ref), custom_call_target="tpu_custom_call" | custom-call | tf_op jit(solution)/shard_map/combine/pallas_call | solution.py:181
Async XLA Ops:
  1.0 12.1 %collective-permute-start.1 = (bf16[2,2,128,256]{3,2,1,0:T(8,128)(2,1)S(1)}, bf16[2,2,128,256]{3,2,1,0:T(8,128)(2,1)S(1)}, u32[]{:S(2)}, u32[]{:S(2)}) collective-permute-start(bf16[2,2,128,256]{3,2,1,0:T(8,128)(2,1)S(1)} %bitcast.15), channel_id=1, source_target_pairs={{1,0},{2,1},{3,2},{4,3},{5,4},{6,5},{7,6},{8,7},{9,8},{10,9},{11,1... | collective-permute-start | bytes 786440 | tf_op jit(solution)/shard_map/ppermute | solution.py:151
  2.3 16.6 %collective-permute-start = (bf16[2,2,128,256]{3,2,1,0:T(8,128)(2,1)S(1)}, bf16[2,2,128,256]{3,2,1,0:T(8,128)(2,1)S(1)}, u32[]{:S(2)}, u32[]{:S(2)}) collective-permute-start(bf16[2,2,128,256]{3,2,1,0:T(8,128)(2,1)S(1)} %bitcast.16), channel_id=1, source_target_pairs={{0,1},{1,2},{2,3},{3,4},{4,5},{5,6},{6,7},{7,8},{8,9},{9,10},{10,1... | collective-permute-start | bytes 786440 | tf_op jit(solution)/shard_map/ppermute | solution.py:150
  8.4 1.3 %copy-start.1 = (s32[1024]{0:T(1024)S(1)}, s32[1024]{0:T(1024)}, u32[]{:S(2)}) copy-start(s32[1024]{0:T(1024)} %param.9) | copy-start | bytes 12292
  9.7 0.7 %copy-start = (s32[1024]{0:T(1024)S(1)}, s32[1024]{0:T(1024)}, u32[]{:S(2)}) copy-start(s32[1024]{0:T(1024)} %param.8) | copy-start | bytes 12292
  9.7 0.7 %copy-start.2 = (s32[2]{0:T(128)S(1)}, s32[2]{0:T(128)}, u32[]{:S(2)}) copy-start(s32[2]{0:T(128)} %bins_ref.3) | copy-start | bytes 28

commit v2 on v1

v2 whole, which is shorter than its diff:
```python
import functools
import math

import jax
import jax.numpy as jnp
from jax import lax
from jax.experimental import pallas as pl
from jax.experimental.pallas import tpu as pltpu
from jax.sharding import PartitionSpec as P

NBINS = 128
WX = 16
WY = 16
LANES = 128
VMEM_BYTES = 48 * 1024 * 1024


def dot(left, right):
    return jnp.dot(left, right, preferred_element_type=jnp.float32)


def frequency_weight(bins_ref, slot):
    return 0.5 + bins_ref[slot].astype(jnp.float32) / NBINS


def slope_table(cells):
    target = lax.broadcasted_iota(jnp.int32, (cells, cells), 0)
    source = lax.broadcasted_iota(jnp.int32, (cells, cells), 1)
    column = lax.rem(target, WY)
    step = source - target
    half, zero = jnp.float32(0.5), jnp.float32(0.0)
    along_x = jnp.where(step == WY, half, zero) - jnp.where(step == -WY, half, zero)
    along_y = jnp.where((step == 1) & (column != WY - 1), half, zero) - jnp.where(
        (step == -1) & (column != 0), half, zero
    )
    return jnp.concatenate([along_x, along_y], axis=0).astype(jnp.bfloat16)


def pick_pairs(products, hot, receiver_ref):
    receivers = products.shape[0]
    pairs = receiver_ref.shape[1]
    high = products.astype(jnp.bfloat16)
    low = (products - high.astype(jnp.float32)).astype(jnp.bfloat16)
    both = dot(jnp.concatenate([high, low], axis=0), hot)
    picked = both[:receivers] + both[receivers:]
    at_receiver = lax.broadcasted_iota(jnp.int32, (receivers, pairs), 0) == receiver_ref[...]
    row = jnp.sum(jnp.where(at_receiver, picked, 0.0), axis=0, keepdims=True)
    return jnp.concatenate(
        [row[:, at : at + LANES] for at in range(0, pairs, LANES)], axis=0
    )


def local_terms(
    scale, bins_ref, profile_ref, source_ref, receiver_ref, green_s, green_r, out_ref, hot_ref
):
    freqs, _, cells, sources = green_s.shape
    pairs = source_ref.shape[1]
    at_source = lax.broadcasted_iota(jnp.int32, (sources, pairs), 0) == source_ref[...]
    hot_ref[...] = jnp.where(at_source, jnp.float32(1), jnp.float32(0)).astype(jnp.bfloat16)
    table = slope_table(cells)
    sound = along_x = along_y = 0.0
    for slot in range(freqs):
        weight = frequency_weight(bins_ref, slot)
        real, imag = green_s[slot, 0], green_s[slot, 1]
        slope_real = dot(table, real).astype(jnp.bfloat16)
        slope_imag = dot(table, imag).astype(jnp.bfloat16)
        near_real, near_imag = green_r[slot, 0], green_r[slot, 1]
        plain = dot(near_real, real) - dot(near_imag, imag)
        slope_x = dot(near_imag, slope_real[:cells]) + dot(near_real, slope_imag[:cells])
        slope_y = dot(near_imag, slope_real[cells:]) + dot(near_real, slope_imag[cells:])
        sound = sound + plain * (weight * weight * profile_ref[0] * scale)
        along_x = along_x + slope_x * (weight * scale)
        along_y = along_y + slope_y * (weight * scale)
    hot = hot_ref[...]
    for k, products in enumerate([sound, along_x, along_y]):
        out_ref[k] = pick_pairs(products, hot, receiver_ref)


def layer_term(scale, bins_ref, receiver_ref, hot, green_s, other_r):
    total = 0.0
    for slot in range(green_s.shape[0]):
        both = dot(other_r[slot, 1], green_s[slot, 0]) + dot(other_r[slot, 0], green_s[slot, 1])
        total = total + both * (0.5 * frequency_weight(bins_ref, slot) * scale)
    return pick_pairs(total, hot, receiver_ref)


def near_term(scale, bins_ref, receiver_ref, hot_ref, green_s, near_r, out_ref):
    out_ref[...] = layer_term(scale, bins_ref, receiver_ref, hot_ref[...], green_s, near_r)


def far_term(
    scale, share, bins_ref, receiver_ref, hot_ref, green_s, far_r, terms, near_ref, out_ref
):
    far = layer_term(scale, bins_ref, receiver_ref, hot_ref[...], green_s, far_r)
    near = near_ref[...]
    odd = lax.rem(lax.axis_index("depth"), 2) == 1
    below = jnp.where(odd, near, far)
    above = jnp.where(odd, far, near)
    tiles = far.shape[0]
    group = lax.broadcasted_iota(jnp.int32, (tiles, LANES), 1) // share
    in_tile = LANES // share

    def moved(value, to, part):
        return pltpu.roll(value, (to - part) * share % LANES, 1) if to != part else value

    for part in range(in_tile):
        first = moved(below, 3, part)
        for k in range(3):
            first = jnp.where(group == k, moved(terms[k], k, part), first)
        out_ref[pl.ds(2 * part, tiles, stride=2 * in_tile), :] = first
        out_ref[pl.ds(2 * part + 1, tiles, stride=2 * in_tile), :] = moved(above, 0, part)


def combine(freqs, depths, share, parts_ref, out_ref):
    def row(which):
        total = parts_ref[pl.ds(which, depths, stride=2), :]
        for group in range(1, freqs):
            total = total + parts_ref[pl.ds(2 * group * depths + which, depths, stride=2), :]
        return total

    first = row(0)
    above = row(1)[:, :share]
    for k in range(3):
        out_ref[k] = first[:, k * share : (k + 1) * share]
    below = first[:, 3 * share : 4 * share]
    blank = jnp.zeros((1, share), jnp.float32)
    out_ref[3] = jnp.concatenate([below[1:], blank], axis=0) - jnp.concatenate(
        [blank, above[:-1]], axis=0
    )


def vmem(count):
    return [pl.BlockSpec(memory_space=pltpu.VMEM)] * count


def smem(count):
    return [pl.BlockSpec(memory_space=pltpu.SMEM)] * count


def on_device(
    green_source, green_receiver, source_index, receiver_index, frequency_bins, depth_profile
):
    local_freqs, _, sources, _, cells = green_source.shape
    receivers = green_receiver.shape[2]
    pairs = source_index.shape[0]
    n_freq, n_depth = lax.axis_size("freq"), lax.axis_size("depth")
    owners = n_freq * n_depth
    share = pairs // owners
    tiles = pairs // LANES
    scale = 1.0 / math.sqrt(2.0 * WX * WY * local_freqs * n_freq)
    params = pltpu.CompilerParams(vmem_limit_bytes=VMEM_BYTES)

    own = jnp.swapaxes(green_receiver[:, 0], 1, 2)
    paired = [(i, i ^ 1) for i in range(n_depth)]
    crossed = [(i, i + 1) for i in range(1, n_depth - 1, 2)]
    crossed += [(target, source) for source, target in crossed]
    near_r = lax.ppermute(own, "depth", paired)
    far_r = lax.ppermute(own, "depth", crossed)

    green_s = jnp.transpose(green_source[:, 0], (0, 2, 3, 1))
    source_row = source_index.reshape(1, pairs)
    receiver_row = receiver_index.reshape(1, pairs)
    product = 2 * 2 * cells * local_freqs * sources * receivers
    picking = 2 * 2 * sources * receivers * pairs

    def call(body, name, shapes, n_smem, n_vmem, terms):
        return pl.pallas_call(
            body,
            out_shape=shapes,
            in_specs=smem(n_smem) + vmem(n_vmem),
            out_specs=jax.tree.map(lambda _: pl.BlockSpec(memory_space=pltpu.VMEM), shapes),
            compiler_params=params,
            cost_estimate=pl.CostEstimate(
                flops=terms * (product + picking), bytes_accessed=1 << 21, transcendentals=0
            ),
            name=name,
        )

    term_shape = jax.ShapeDtypeStruct((tiles, LANES), jnp.float32)
    terms, hot = call(
        functools.partial(local_terms, scale),
        "local_terms",
        [
            jax.ShapeDtypeStruct((3, tiles, LANES), jnp.float32),
            jax.ShapeDtypeStruct((sources, pairs), jnp.bfloat16),
        ],
        2, 4, 3,
    )(frequency_bins, depth_profile, source_row, receiver_row, green_s, own)
    near = call(functools.partial(near_term, scale), "near_term", term_shape, 1, 4, 1)(
        frequency_bins, receiver_row, hot, green_s, near_r
    )
    parts = call(
        functools.partial(far_term, scale, share),
        "far_term",
        jax.ShapeDtypeStruct((2 * owners, LANES), jnp.float32),
        1, 6, 1,
    )(frequency_bins, receiver_row, hot, green_s, far_r, terms, near)
    parts = lax.all_to_all(parts, ("freq", "depth"), split_axis=0, concat_axis=0, tiled=True)
    kernels = call(
        functools.partial(combine, n_freq, n_depth, share),
        "combine",
        jax.ShapeDtypeStruct((4, n_depth, share), jnp.float32),
        0, 1, 0,
    )(parts)
    return jnp.swapaxes(kernels, 1, 2)


def solution(mesh):
    placed = (
        P("freq", "depth", None, None, None),
        P("freq", "depth", None, None, None),
        P(),
        P(),
        P("freq"),
        P("depth"),
    )
    return jax.shard_map(
        on_device,
        mesh=mesh,
        in_specs=placed,
        out_specs=P(None, ("freq", "depth"), None),
        check_vma=False,
    )
```

time: 34.1 us -> 31.6 us (0.927)
  starting transfers between devices: 6.78 us -> 3.67 us
  waiting for transfers between devices: 5.72 us -> 4.15 us
  local copies, waits for them, and re-layouts: 2.89 us -> 3.91 us
  Pallas kernels: 5.11 us -> 5.99 us
    ppermute x2, starting transfers between devices: 6.78 us -> 3.67 us  [the longest x1 3 us: on_device(): near_r = lax.ppermute(own, 'depth', paired)]
    ppermute x2, waiting for transfers between devices: 5.72 us -> 4.15 us  [the longest x1 4.15 us: on_device(): near_r = lax.ppermute(own, 'depth', paired)]
    unnamed x8, local copies, waits for them, and re-layouts: 2.89 us -> 3.91 us
    pallas_call x3 -> x4, Pallas kernels: 5.11 us -> 5.99 us  [the longest x1 2.71 us: on_device(): call(functools.partial(local_terms, scale), 'local_terms', [jax.ShapeDtyp...]
  transfers between devices with their start and end apart: 2 -> 2, of which waited for: 1 -> 1; matrix products, arithmetic and copies ran while one was open for 4% -> 7% of each run, Pallas kernels for 8% -> 13%
where the time goes in v2:
time: 31.6 us; the launch traced here: 31.4 us
  blocking collectives  12.9 us (41%)
  Pallas kernels  5.99 us (19%)
  waiting for transfers between devices  4.15 us (13%)
  local copies, waits for them, and re-layouts  3.91 us (12%)
  starting transfers between devices  3.67 us (12%)
  between operations  0.74 us (2%)
    all_to_all x1, blocking collectives, on_device(): lax.all_to_all(parts, ('freq', 'depth'), split_axis=0, concat_axis=0, til...  12.9 us
    ppermute x1, waiting for transfers between devices, on_device(): near_r = lax.ppermute(own, 'depth', paired)  4.15 us
    unnamed x8, local copies, waits for them, and re-layouts  3.91 us
    ppermute x1, starting transfers between devices, on_device(): near_r = lax.ppermute(own, 'depth', paired)  3 us
    pallas_call x1, Pallas kernels, on_device(): call(functools.partial(local_terms, scale), 'local_terms', [jax.ShapeDtyp...  2.71 us
    pallas_call x1, Pallas kernels, on_device(): call(functools.partial(far_term, scale, share), 'far_term', jax.ShapeDtyp...  1.29 us
    pallas_call x1, Pallas kernels, on_device(): call(functools.partial(near_term, scale), 'near_term', term_shape, 1, 4, 1)  1.22 us
    pallas_call x1, Pallas kernels, on_device(): call(functools.partial(combine, n_freq, n_depth, share), 'combine', jax.S...  0.76 us
  transfers between devices with their start and end apart: 2, of which 1 were waited for; matrix products, arithmetic and copies ran while one was open for 7% of the time, Pallas kernels for 13%

profile of v2, /device:TPU:0, one launch (start us, length us, event | category | flops | bytes accessed | tf_op | source)
XLA Modules:
  0.0 31.4 jit_solution(12734252791914381296)
XLA Ops:
  0.0 1.0 %copy.10 = bf16[2,1,128,2,256]{4,2,3,0,1:T(8,128)(2,1)S(1)} copy(bf16[2,1,128,2,256]{4,3,2,1,0:T(2,128)(2,1)} %param.7) | data formatting | bytes 524288 | tf_op args[1]
  1.0 3.0 %collective-permute-start.1 = (bf16[2,2,128,256]{3,2,1,0:T(8,128)(2,1)S(1)}, bf16[2,2,128,256]{3,2,1,0:T(8,128)(2,1)S(1)}, u32[]{:S(2)}, u32[]{:S(2)}) collective-permute-start(bf16[2,2,128,256]{3,2,1,0:T(8,128)(2,1)S(1)} %bitcast.16), channel_id=1, source_target_pairs={{0,1},{1,0},{2,3},{3,2},{4,5},{5,4},{6,7},{7,6},{8,9},{9,8},{10,11... | collective-permute-start | bytes 786440 | tf_op jit(solution)/shard_map/ppermute | solution.py:157
  4.0 0.7 %collective-permute-start = (bf16[2,2,128,256]{3,2,1,0:T(8,128)(2,1)S(1)}, bf16[2,2,128,256]{3,2,1,0:T(8,128)(2,1)S(1)}, u32[]{:S(2)}, u32[]{:S(2)}) collective-permute-start(bf16[2,2,128,256]{3,2,1,0:T(8,128)(2,1)S(1)} %bitcast.17), channel_id=1, source_target_pairs={{1,2},{3,4},{5,6},{7,8},{9,10},{11,12},{13,14},{2,1},{4,3},{6,5},{... | collective-permute-start | bytes 786440 | tf_op jit(solution)/shard_map/ppermute | solution.py:158
  4.7 0.0 copy-start.2
  4.7 2.3 %copy.7 = bf16[2,1,384,2,256]{2,4,3,0,1:T(8,128)(2,1)S(1)} copy(bf16[2,1,384,2,256]{4,3,2,1,0:T(2,128)(2,1)} %param.6) | data formatting | bytes 1572864 | tf_op args[0]
  7.0 0.0 copy-start
  7.6 0.0 copy-start.1
  7.7 0.0 copy-done.2
  7.7 0.0 copy-done
  7.7 0.6 %copy-done.1 = s32[2]{0:T(128)S(1)} copy-done((s32[2]{0:T(128)S(1)}, s32[2]{0:T(128)}, u32[]{:S(2)}) %copy-start.1) | copy-done | bytes 32
  8.3 2.7 %local_terms.1 = (f32[3,8,128]{2,1,0:T(8,128)S(1)}, bf16[384,1024]{1,0:T(8,128)(2,1)S(1)}) custom-call(s32[2]{0:T(128)S(1)} %copy-done.1, f32[1]{0:T(128)S(6)} %copy.11.profile_ref, s32[1,1024]{1,0:T(1,128)S(1)} %bitcast.24, s32[1,1024]{1,0:T(1,128)S(1)} %bitcast.21, bf16[2,2,256,384]{3,2,1,0:T(8,128)(2,1)S(1)} %bitcast.13, bf16[2,2,128,256]{3,2,1,0:T(8,128)(2,1)S(1)} %bitcast.18), custom_call_target="tpu_custom_call" | custom-call | flops 905969664 | bytes 2097152 | tf_op jit(solution)/shard_map/local_terms/pallas_call | solution.py:180
  11.0 4.1 %collective-permute-done.1.near_r = bf16[2,2,128,256]{3,2,1,0:T(8,128)(2,1)S(1)} collective-permute-done((bf16[2,2,128,256]{3,2,1,0:T(8,128)(2,1)S(1)}, bf16[2,2,128,256]{3,2,1,0:T(8,128)(2,1)S(1)}, u32[]{:S(2)}, u32[]{:S(2)}) %collective-permute-start.1) | collective-permute-done | bytes 262176 | tf_op jit(solution)/shard_map/ppermute | solution.py:157
  15.2 1.2 %near_term.1.near_ref = f32[8,128]{1,0:T(8,128)S(1)} custom-call(s32[2]{0:T(128)S(1)} %copy-done.1, s32[1,1024]{1,0:T(1,128)S(1)} %bitcast.22, bf16[384,1024]{1,0:T(8,128)(2,1)S(1)} %get-tuple-element.7.hot_ref, bf16[2,2,256,384]{3,2,1,0:T(8,128)(2,1)S(1)} %bitcast.14, bf16[2,2,128,256]{3,2,1,0:T(8,128)(2,1)S(1)} %collective-permute-done.1.near_r), custom_call_target="tpu_custom_call" | custom-call | flops 301989888 | bytes 2097152 | tf_op jit(solution)/shard_map/near_term/pallas_call | solution.py:189
  16.4 0.0 collective-permute-done.far_r
  16.4 1.3 %far_term.1 = f32[64,128]{1,0:T(8,128)S(1)} custom-call(s32[2]{0:T(128)S(1)} %copy-done.1, s32[1,1024]{1,0:T(1,128)S(1)} %bitcast.23, bf16[384,1024]{1,0:T(8,128)(2,1)S(1)} %get-tuple-element.7.hot_ref, bf16[2,2,256,384]{3,2,1,0:T(8,128)(2,1)S(1)} %bitcast.15, bf16[2,2,128,256]{3,2,1,0:T(8,128)(2,1)S(1)} %collective-permute-done.far_r, ...), custom_call_target="tpu_custom_call" | custom-call | flops 301989888 | bytes 2097152 | tf_op jit(solution)/shard_map/far_term/pallas_call | solution.py:192
  17.7 12.9 %all_to_all.11 = f32[32,2,128]{2,1,0:T(2,128)S(1)} all-to-all(f32[32,2,128]{2,1,0:T(2,128)S(1)} %bitcast.19), channel_id=1, replica_groups=mesh['freq'=2,'depth'=16] {'freq','depth'}, dimensions={0} | all-to-all | bytes 65536 | tf_op jit(solution)/shard_map/all_to_all | solution.py:198
  30.6 0.8 %combine.1 = f32[4,16,32]{2,1,0:T(8,128)} custom-call(f32[64,128]{1,0:T(8,128)S(1)} %bitcast.20), custom_call_target="tpu_custom_call" | custom-call | bytes 2097152 | tf_op jit(solution)/shard_map/combine/pallas_call | solution.py:199
Async XLA Ops:
  1.0 14.2 %collective-permute-start.1 = (bf16[2,2,128,256]{3,2,1,0:T(8,128)(2,1)S(1)}, bf16[2,2,128,256]{3,2,1,0:T(8,128)(2,1)S(1)}, u32[]{:S(2)}, u32[]{:S(2)}) collective-permute-start(bf16[2,2,128,256]{3,2,1,0:T(8,128)(2,1)S(1)} %bitcast.16), channel_id=1, source_target_pairs={{0,1},{1,0},{2,3},{3,2},{4,5},{5,4},{6,7},{7,6},{8,9},{9,8},{10,11... | collective-permute-start | bytes 786440 | tf_op jit(solution)/shard_map/ppermute | solution.py:157
  4.0 12.4 %collective-permute-start = (bf16[2,2,128,256]{3,2,1,0:T(8,128)(2,1)S(1)}, bf16[2,2,128,256]{3,2,1,0:T(8,128)(2,1)S(1)}, u32[]{:S(2)}, u32[]{:S(2)}) collective-permute-start(bf16[2,2,128,256]{3,2,1,0:T(8,128)(2,1)S(1)} %bitcast.17), channel_id=1, source_target_pairs={{1,2},{3,4},{5,6},{7,8},{9,10},{11,12},{13,14},{2,1},{4,3},{6,5},{... | collective-permute-start | bytes 786440 | tf_op jit(solution)/shard_map/ppermute | solution.py:158
  4.7 3.0 %copy-start.2 = (s32[1024]{0:T(1024)S(1)}, s32[1024]{0:T(1024)}, u32[]{:S(2)}) copy-start(s32[1024]{0:T(1024)} %param.8) | copy-start | bytes 12292
  7.0 0.7 %copy-start = (s32[1024]{0:T(1024)S(1)}, s32[1024]{0:T(1024)}, u32[]{:S(2)}) copy-start(s32[1024]{0:T(1024)} %param.9) | copy-start | bytes 12292
  7.6 0.7 %copy-start.1 = (s32[2]{0:T(128)S(1)}, s32[2]{0:T(128)}, u32[]{:S(2)}) copy-start(s32[2]{0:T(128)} %bins_ref.5) | copy-start | bytes 28

commit v3 on v2

--- a/solution.py
+++ b/solution.py
@@ -51,7 +51,16 @@
 
 
 def local_terms(
-    scale, bins_ref, profile_ref, source_ref, receiver_ref, green_s, green_r, out_ref, hot_ref
+    scale,
+    bins_ref,
+    profile_ref,
+    source_ref,
+    receiver_ref,
+    green_s,
+    green_r,
+    out_ref,
+    hot_ref,
+    weight_ref,
 ):
     freqs, _, cells, sources = green_s.shape
     pairs = source_ref.shape[1]
@@ -61,6 +70,7 @@
     sound = along_x = along_y = 0.0
     for slot in range(freqs):
         weight = frequency_weight(bins_ref, slot)
+        weight_ref[slot] = jnp.full(weight_ref.shape[1:], 0.5 * weight * scale, jnp.float32)
         real, imag = green_s[slot, 0], green_s[slot, 1]
         slope_real = dot(table, real).astype(jnp.bfloat16)
         slope_imag = dot(table, imag).astype(jnp.bfloat16)
@@ -76,22 +86,22 @@
         out_ref[k] = pick_pairs(products, hot, receiver_ref)
 
 
-def layer_term(scale, bins_ref, receiver_ref, hot, green_s, other_r):
+def layer_term(weight_ref, receiver_ref, hot, green_s, other_r):
     total = 0.0
     for slot in range(green_s.shape[0]):
         both = dot(other_r[slot, 1], green_s[slot, 0]) + dot(other_r[slot, 0], green_s[slot, 1])
-        total = total + both * (0.5 * frequency_weight(bins_ref, slot) * scale)
+        total = total + both * weight_ref[slot]
     return pick_pairs(total, hot, receiver_ref)
 
 
-def near_term(scale, bins_ref, receiver_ref, hot_ref, green_s, near_r, out_ref):
-    out_ref[...] = layer_term(scale, bins_ref, receiver_ref, hot_ref[...], green_s, near_r)
+def near_term(weight_ref, receiver_ref, hot_ref, green_s, near_r, out_ref):
+    out_ref[...] = layer_term(weight_ref, receiver_ref, hot_ref[...], green_s, near_r)
 
 
 def far_term(
-    scale, share, bins_ref, receiver_ref, hot_ref, green_s, far_r, terms, near_ref, out_ref
+    share, weight_ref, receiver_ref, hot_ref, green_s, far_r, terms, near_ref, out_ref
 ):
-    far = layer_term(scale, bins_ref, receiver_ref, hot_ref[...], green_s, far_r)
+    far = layer_term(weight_ref, receiver_ref, hot_ref[...], green_s, far_r)
     near = near_ref[...]
     odd = lax.rem(lax.axis_index("depth"), 2) == 1
     below = jnp.where(odd, near, far)
@@ -177,24 +187,25 @@
         )
 
     term_shape = jax.ShapeDtypeStruct((tiles, LANES), jnp.float32)
-    terms, hot = call(
+    terms, hot, weights = call(
         functools.partial(local_terms, scale),
         "local_terms",
         [
             jax.ShapeDtypeStruct((3, tiles, LANES), jnp.float32),
             jax.ShapeDtypeStruct((sources, pairs), jnp.bfloat16),
+            jax.ShapeDtypeStruct((local_freqs, 1, sources), jnp.float32),
         ],
         2, 4, 3,
     )(frequency_bins, depth_profile, source_row, receiver_row, green_s, own)
-    near = call(functools.partial(near_term, scale), "near_term", term_shape, 1, 4, 1)(
-        frequency_bins, receiver_row, hot, green_s, near_r
+    near = call(near_term, "near_term", term_shape, 0, 5, 1)(
+        weights, receiver_row, hot, green_s, near_r
     )
     parts = call(
-        functools.partial(far_term, scale, share),
+        functools.partial(far_term, share),
         "far_term",
         jax.ShapeDtypeStruct((2 * owners, LANES), jnp.float32),
-        1, 6, 1,
-    )(frequency_bins, receiver_row, hot, green_s, far_r, terms, near)
+        0, 7, 1,
+    )(weights, receiver_row, hot, green_s, far_r, terms, near)
     parts = lax.all_to_all(parts, ("freq", "depth"), split_axis=0, concat_axis=0, tiled=True)
     kernels = call(
         functools.partial(combine, n_freq, n_depth, share),

time: 31.6 us -> 30.8 us (0.975)
  Pallas kernels: 5.99 us -> 4.89 us
    pallas_call x2, Pallas kernels: 2.52 us -> 1.43 us  [the longest x1 0.75 us: on_device(): call(functools.partial(far_term, share), 'far_term', jax.ShapeDtypeStruct...]
  transfers between devices with their start and end apart: 2 -> 2, of which waited for: 1 -> 1; matrix products, arithmetic and copies ran while one was open for 7% -> 8% of each run, Pallas kernels for 13% -> 11%
where the time goes in v3:
time: 30.8 us; the launch traced here: 30.5 us
  blocking collectives  13.2 us (43%)
  Pallas kernels  4.89 us (16%)
  waiting for transfers between devices  4.16 us (14%)
  local copies, waits for them, and re-layouts  3.91 us (13%)
  starting transfers between devices  3.67 us (12%)
  between operations  0.74 us (2%)
    all_to_all x1, blocking collectives, on_device(): lax.all_to_all(parts, ('freq', 'depth'), split_axis=0, concat_axis=0, til...  13.2 us
    ppermute x1, waiting for transfers between devices, on_device(): near_r = lax.ppermute(own, 'depth', paired)  4.16 us
    unnamed x8, local copies, waits for them, and re-layouts  3.91 us
    ppermute x1, starting transfers between devices, on_device(): near_r = lax.ppermute(own, 'depth', paired)  3 us
    pallas_call x1, Pallas kernels, on_device(): call(functools.partial(local_terms, scale), 'local_terms', [jax.ShapeDtyp...  2.7 us
    pallas_call x1, Pallas kernels, on_device(): call(functools.partial(combine, n_freq, n_depth, share), 'combine', jax.S...  0.76 us
    pallas_call x1, Pallas kernels, on_device(): call(functools.partial(far_term, share), 'far_term', jax.ShapeDtypeStruct...  0.75 us
    pallas_call x1, Pallas kernels, on_device(): call(near_term, 'near_term', term_shape, 0, 5, 1)  0.68 us
  transfers between devices with their start and end apart: 2, of which 1 were waited for; matrix products, arithmetic and copies ran while one was open for 8% of the time, Pallas kernels for 11%

profile of v3, /device:TPU:0, one launch (start us, length us, event | category | flops | bytes accessed | tf_op | source)
XLA Modules:
  0.0 30.5 jit_solution(2445513790451184192)
XLA Ops:
  0.0 1.0 %copy.10 = bf16[2,1,128,2,256]{4,2,3,0,1:T(8,128)(2,1)S(1)} copy(bf16[2,1,128,2,256]{4,3,2,1,0:T(2,128)(2,1)} %param.7) | data formatting | bytes 524288 | tf_op args[1]
  1.0 3.0 %collective-permute-start.1 = (bf16[2,2,128,256]{3,2,1,0:T(8,128)(2,1)S(1)}, bf16[2,2,128,256]{3,2,1,0:T(8,128)(2,1)S(1)}, u32[]{:S(2)}, u32[]{:S(2)}) collective-permute-start(bf16[2,2,128,256]{3,2,1,0:T(8,128)(2,1)S(1)} %bitcast.16), channel_id=1, source_target_pairs={{0,1},{1,0},{2,3},{3,2},{4,5},{5,4},{6,7},{7,6},{8,9},{9,8},{10,11... | collective-permute-start | bytes 786440 | tf_op jit(solution)/shard_map/ppermute | solution.py:167
  4.0 0.7 %collective-permute-start = (bf16[2,2,128,256]{3,2,1,0:T(8,128)(2,1)S(1)}, bf16[2,2,128,256]{3,2,1,0:T(8,128)(2,1)S(1)}, u32[]{:S(2)}, u32[]{:S(2)}) collective-permute-start(bf16[2,2,128,256]{3,2,1,0:T(8,128)(2,1)S(1)} %bitcast.17), channel_id=1, source_target_pairs={{1,2},{3,4},{5,6},{7,8},{9,10},{11,12},{13,14},{2,1},{4,3},{6,5},{... | collective-permute-start | bytes 786440 | tf_op jit(solution)/shard_map/ppermute | solution.py:168
  4.7 0.0 copy-start.1
  4.7 2.3 %copy.7 = bf16[2,1,384,2,256]{2,4,3,0,1:T(8,128)(2,1)S(1)} copy(bf16[2,1,384,2,256]{4,3,2,1,0:T(2,128)(2,1)} %param.6) | data formatting | bytes 1572864 | tf_op args[0]
  7.0 0.0 copy-start
  7.6 0.0 copy-start.2
  7.7 0.0 copy-done.1
  7.7 0.0 copy-done
  7.7 0.6 %copy-done.2 = s32[2]{0:T(128)S(1)} copy-done((s32[2]{0:T(128)S(1)}, s32[2]{0:T(128)}, u32[]{:S(2)}) %copy-start.2) | copy-done | bytes 32
  8.3 2.7 %local_terms.1 = (f32[3,8,128]{2,1,0:T(8,128)S(1)}, bf16[384,1024]{1,0:T(8,128)(2,1)S(1)}, f32[2,1,384]{2,1,0:T(1,128)S(1)}) custom-call(s32[2]{0:T(128)S(1)} %copy-done.2, f32[1]{0:T(128)S(6)} %copy.11.profile_ref, s32[1,1024]{1,0:T(1,128)S(1)} %bitcast.24, s32[1,1024]{1,0:T(1,128)S(1)} %bitcast.21, bf16[2,2,256,384]{3,2,1,0:T(8,128)(2,1)S(1)} %bitcast.13, ...), custom_call_target="tpu_custom_call" | custom-call | flops 905969664 | bytes 2097152 | tf_op jit(solution)/shard_map/local_terms/pallas_call | solution.py:190
  11.0 4.2 %collective-permute-done.1.near_r = bf16[2,2,128,256]{3,2,1,0:T(8,128)(2,1)S(1)} collective-permute-done((bf16[2,2,128,256]{3,2,1,0:T(8,128)(2,1)S(1)}, bf16[2,2,128,256]{3,2,1,0:T(8,128)(2,1)S(1)}, u32[]{:S(2)}, u32[]{:S(2)}) %collective-permute-start.1) | collective-permute-done | bytes 262176 | tf_op jit(solution)/shard_map/ppermute | solution.py:167
  15.2 0.7 %near_term.1.near_ref = f32[8,128]{1,0:T(8,128)S(1)} custom-call(f32[2,1,384]{2,1,0:T(1,128)S(1)} %get-tuple-element.8.weight_ref, s32[1,1024]{1,0:T(1,128)S(1)} %bitcast.22, bf16[384,1024]{1,0:T(8,128)(2,1)S(1)} %get-tuple-element.9.hot_ref, bf16[2,2,256,384]{3,2,1,0:T(8,128)(2,1)S(1)} %bitcast.14, bf16[2,2,128,256]{3,2,1,0:T(8,128)(2,1)S(1)} %collective-permute-done.1.near_r), custom_call_target="tpu_custom_call" | custom-call | flops 301989888 | bytes 2097152 | tf_op jit(solution)/shard_map/near_term/pallas_call | solution.py:200
  15.9 0.0 collective-permute-done.far_r
  15.9 0.8 %far_term.1 = f32[64,128]{1,0:T(8,128)S(1)} custom-call(f32[2,1,384]{2,1,0:T(1,128)S(1)} %get-tuple-element.8.weight_ref, s32[1,1024]{1,0:T(1,128)S(1)} %bitcast.23, bf16[384,1024]{1,0:T(8,128)(2,1)S(1)} %get-tuple-element.9.hot_ref, bf16[2,2,256,384]{3,2,1,0:T(8,128)(2,1)S(1)} %bitcast.15, bf16[2,2,128,256]{3,2,1,0:T(8,128)(2,1)S(1)} %collective-permute-done.far_r, ...), custom_call_target="tpu_custom_call" | custom-call | flops 301989888 | bytes 2097152 | tf_op jit(solution)/shard_map/far_term/pallas_call | solution.py:203
  16.6 13.2 %all_to_all.11 = f32[32,2,128]{2,1,0:T(2,128)S(1)} all-to-all(f32[32,2,128]{2,1,0:T(2,128)S(1)} %bitcast.19), channel_id=1, replica_groups=mesh['freq'=2,'depth'=16] {'freq','depth'}, dimensions={0} | all-to-all | bytes 65536 | tf_op jit(solution)/shard_map/all_to_all | solution.py:209
  29.8 0.8 %combine.1 = f32[4,16,32]{2,1,0:T(8,128)} custom-call(f32[64,128]{1,0:T(8,128)S(1)} %bitcast.20), custom_call_target="tpu_custom_call" | custom-call | bytes 2097152 | tf_op jit(solution)/shard_map/combine/pallas_call | solution.py:210
Async XLA Ops:
  1.0 14.2 %collective-permute-start.1 = (bf16[2,2,128,256]{3,2,1,0:T(8,128)(2,1)S(1)}, bf16[2,2,128,256]{3,2,1,0:T(8,128)(2,1)S(1)}, u32[]{:S(2)}, u32[]{:S(2)}) collective-permute-start(bf16[2,2,128,256]{3,2,1,0:T(8,128)(2,1)S(1)} %bitcast.16), channel_id=1, source_target_pairs={{0,1},{1,0},{2,3},{3,2},{4,5},{5,4},{6,7},{7,6},{8,9},{9,8},{10,11... | collective-permute-start | bytes 786440 | tf_op jit(solution)/shard_map/ppermute | solution.py:167
  4.0 11.9 %collective-permute-start = (bf16[2,2,128,256]{3,2,1,0:T(8,128)(2,1)S(1)}, bf16[2,2,128,256]{3,2,1,0:T(8,128)(2,1)S(1)}, u32[]{:S(2)}, u32[]{:S(2)}) collective-permute-start(bf16[2,2,128,256]{3,2,1,0:T(8,128)(2,1)S(1)} %bitcast.17), channel_id=1, source_target_pairs={{1,2},{3,4},{5,6},{7,8},{9,10},{11,12},{13,14},{2,1},{4,3},{6,5},{... | collective-permute-start | bytes 786440 | tf_op jit(solution)/shard_map/ppermute | solution.py:168
  4.7 3.0 %copy-start.1 = (s32[1024]{0:T(1024)S(1)}, s32[1024]{0:T(1024)}, u32[]{:S(2)}) copy-start(s32[1024]{0:T(1024)} %param.8) | copy-start | bytes 12292
  7.0 0.7 %copy-start = (s32[1024]{0:T(1024)S(1)}, s32[1024]{0:T(1024)}, u32[]{:S(2)}) copy-start(s32[1024]{0:T(1024)} %param.9) | copy-start | bytes 12292
  7.6 0.7 %copy-start.2 = (s32[2]{0:T(128)S(1)}, s32[2]{0:T(128)}, u32[]{:S(2)}) copy-start(s32[2]{0:T(128)} %bins_ref.1) | copy-start | bytes 28

commit v4 on v3

--- a/solution.py
+++ b/solution.py
@@ -74,7 +74,7 @@
         real, imag = green_s[slot, 0], green_s[slot, 1]
         slope_real = dot(table, real).astype(jnp.bfloat16)
         slope_imag = dot(table, imag).astype(jnp.bfloat16)
-        near_real, near_imag = green_r[slot, 0], green_r[slot, 1]
+        near_real, near_imag = parts_of(green_r[slot])
         plain = dot(near_real, real) - dot(near_imag, imag)
         slope_x = dot(near_imag, slope_real[:cells]) + dot(near_real, slope_imag[:cells])
         slope_y = dot(near_imag, slope_real[cells:]) + dot(near_real, slope_imag[cells:])
@@ -86,10 +86,16 @@
         out_ref[k] = pick_pairs(products, hot, receiver_ref)
 
 
+def parts_of(rows):
+    parts = jnp.swapaxes(rows, 0, 1)
+    return parts[0], parts[1]
+
+
 def layer_term(weight_ref, receiver_ref, hot, green_s, other_r):
     total = 0.0
     for slot in range(green_s.shape[0]):
-        both = dot(other_r[slot, 1], green_s[slot, 0]) + dot(other_r[slot, 0], green_s[slot, 1])
+        real, imag = parts_of(other_r[slot])
+        both = dot(imag, green_s[slot, 0]) + dot(real, green_s[slot, 1])
         total = total + both * weight_ref[slot]
     return pick_pairs(total, hot, receiver_ref)
 
@@ -160,12 +166,22 @@
     scale = 1.0 / math.sqrt(2.0 * WX * WY * local_freqs * n_freq)
     params = pltpu.CompilerParams(vmem_limit_bytes=VMEM_BYTES)
 
-    own = jnp.swapaxes(green_receiver[:, 0], 1, 2)
+    own = green_receiver[:, 0]
     paired = [(i, i ^ 1) for i in range(n_depth)]
     crossed = [(i, i + 1) for i in range(1, n_depth - 1, 2)]
     crossed += [(target, source) for source, target in crossed]
+    everywhere = [
+        (group * n_depth + source, group * n_depth + target)
+        for group in range(n_freq)
+        for source, target in crossed
+    ]
+    everywhere += [
+        (group * n_depth + end, (group ^ 1) * n_depth + end)
+        for group in range(n_freq)
+        for end in (0, n_depth - 1)
+    ]
     near_r = lax.ppermute(own, "depth", paired)
-    far_r = lax.ppermute(own, "depth", crossed)
+    far_r = lax.ppermute(own, ("freq", "depth"), everywhere)
 
     green_s = jnp.transpose(green_source[:, 0], (0, 2, 3, 1))
     source_row = source_index.reshape(1, pairs)

time: 30.8 us -> 29.9 us (0.971)
  waiting for transfers between devices: 4.16 us -> 5.15 us
  local copies, waits for them, and re-layouts: 3.91 us -> 2.93 us
  starting transfers between devices: 3.67 us -> 2.94 us
    ppermute x1, waiting for transfers between devices: 4.16 us -> 5.15 us  [on_device(): near_r = lax.ppermute(own, 'depth', paired)]
    unnamed x8 -> x9, local copies, waits for them, and re-layouts: 3.91 us -> 2.93 us
    ppermute x1, starting transfers between devices: 0.67 us -> 0.01 us  [on_device(): far_r = lax.ppermute(own, ('freq', 'depth'), everywhere)]
where the time goes in v4:
time: 29.9 us; the launch traced here: 29.7 us
  blocking collectives  13 us (43%)
  waiting for transfers between devices  5.15 us (17%)
  Pallas kernels  4.92 us (16%)
  starting transfers between devices  2.94 us (10%)
  local copies, waits for them, and re-layouts  2.93 us (10%)
  between operations  0.73 us (2%)
    all_to_all x1, blocking collectives, on_device(): lax.all_to_all(parts, ('freq', 'depth'), split_axis=0, concat_axis=0, til...  13 us
    ppermute x1, waiting for transfers between devices, on_device(): near_r = lax.ppermute(own, 'depth', paired)  5.15 us
    ppermute x1, starting transfers between devices, on_device(): near_r = lax.ppermute(own, 'depth', paired)  2.94 us
    unnamed x9, local copies, waits for them, and re-layouts  2.93 us
    pallas_call x1, Pallas kernels, on_device(): call(functools.partial(local_terms, scale), 'local_terms', [jax.ShapeDtyp...  2.7 us
    pallas_call x1, Pallas kernels, on_device(): call(functools.partial(far_term, share), 'far_term', jax.ShapeDtypeStruct...  0.77 us
    pallas_call x1, Pallas kernels, on_device(): call(functools.partial(combine, n_freq, n_depth, share), 'combine', jax.S...  0.76 us
    pallas_call x1, Pallas kernels, on_device(): call(near_term, 'near_term', term_shape, 0, 5, 1)  0.69 us
  transfers between devices with their start and end apart: 2, of which 1 were waited for; matrix products, arithmetic and copies ran while one was open for 8% of the time, Pallas kernels for 11%

profile of v4, /device:TPU:0, one launch (start us, length us, event | category | flops | bytes accessed | tf_op | source)
XLA Modules:
  0.0 29.7 jit_solution(9703269845591544907)
XLA Ops:
  0.0 0.0 copy-start.1
  0.0 2.9 %collective-permute-start.1 = (bf16[2,128,2,256]{3,2,1,0:T(2,128)(2,1)}, bf16[2,128,2,256]{3,2,1,0:T(2,128)(2,1)S(1)}, u32[]{:S(2)}, u32[]{:S(2)}) collective-permute-start(bf16[2,128,2,256]{3,2,1,0:T(2,128)(2,1)} %bitcast.17), channel_id=1, source_target_pairs={{0,1},{1,0},{2,3},{3,2},{4,5},{5,4},{6,7},{7,6},{8,9},{9,8},{10,11... | collective-permute-start | bytes 786440 | tf_op jit(solution)/shard_map/ppermute | solution.py:183
  2.9 0.0 collective-permute-start
  2.9 0.0 copy-start.2
  2.9 2.3 %copy.7 = bf16[2,1,384,2,256]{2,4,3,0,1:T(8,128)(2,1)S(1)} copy(bf16[2,1,384,2,256]{4,3,2,1,0:T(2,128)(2,1)} %param.6) | data formatting | bytes 1572864 | tf_op args[0]
  5.2 0.0 copy-start
  5.9 0.0 copy-start.3
  5.9 0.0 copy-done.1
  5.9 0.0 copy-done.2
  6.0 0.0 copy-done
  6.0 0.6 %copy-done.3 = s32[2]{0:T(128)S(1)} copy-done((s32[2]{0:T(128)S(1)}, s32[2]{0:T(128)}, u32[]{:S(2)}) %copy-start.3) | copy-done | bytes 32
  6.6 2.7 %local_terms.1 = (f32[3,8,128]{2,1,0:T(8,128)S(1)}, bf16[384,1024]{1,0:T(8,128)(2,1)S(1)}, f32[2,1,384]{2,1,0:T(1,128)S(1)}) custom-call(s32[2]{0:T(128)S(1)} %copy-done.3, f32[1]{0:T(128)S(6)} %copy.8.profile_ref, s32[1,1024]{1,0:T(1,128)S(1)} %bitcast.20, s32[1,1024]{1,0:T(1,128)S(1)} %bitcast.14, bf16[2,2,256,384]{3,2,1,0:T(8,128)(2,1)S(1)} %bitcast.9, ...), custom_call_target="tpu_custom_call" | custom-call | flops 905969664 | bytes 2097152 | tf_op jit(solution)/shard_map/local_terms/pallas_call | solution.py:206
  9.3 5.2 %collective-permute-done.1.near_r = bf16[2,128,2,256]{3,2,1,0:T(2,128)(2,1)S(1)} collective-permute-done((bf16[2,128,2,256]{3,2,1,0:T(2,128)(2,1)}, bf16[2,128,2,256]{3,2,1,0:T(2,128)(2,1)S(1)}, u32[]{:S(2)}, u32[]{:S(2)}) %collective-permute-start.1) | collective-permute-done | bytes 262176 | tf_op jit(solution)/shard_map/ppermute | solution.py:183
  14.4 0.7 %near_term.1.near_ref = f32[8,128]{1,0:T(8,128)S(1)} custom-call(f32[2,1,384]{2,1,0:T(1,128)S(1)} %get-tuple-element.8.weight_ref, s32[1,1024]{1,0:T(1,128)S(1)} %bitcast.15, bf16[384,1024]{1,0:T(8,128)(2,1)S(1)} %get-tuple-element.9.hot_ref, bf16[2,2,256,384]{3,2,1,0:T(8,128)(2,1)S(1)} %bitcast.10, bf16[2,128,2,256]{3,2,1,0:T(2,128)(2,1)S(1)} %collective-permute-done.1.near_r), custom_call_target="tpu_custom_call" | custom-call | flops 301989888 | bytes 2097152 | tf_op jit(solution)/shard_map/near_term/pallas_call | solution.py:216
  15.1 0.0 collective-permute-done.far_r
  15.2 0.8 %far_term.1 = f32[64,128]{1,0:T(8,128)S(1)} custom-call(f32[2,1,384]{2,1,0:T(1,128)S(1)} %get-tuple-element.8.weight_ref, s32[1,1024]{1,0:T(1,128)S(1)} %bitcast.16, bf16[384,1024]{1,0:T(8,128)(2,1)S(1)} %get-tuple-element.9.hot_ref, bf16[2,2,256,384]{3,2,1,0:T(8,128)(2,1)S(1)} %bitcast.11, bf16[2,128,2,256]{3,2,1,0:T(2,128)(2,1)S(1)} %collective-permute-done.far_r, ...), custom_call_target="tpu_custom_call" | custom-call | flops 301989888 | bytes 2097152 | tf_op jit(solution)/shard_map/far_term/pallas_call | solution.py:219
  15.9 13.0 %all_to_all.11 = f32[32,2,128]{2,1,0:T(2,128)S(1)} all-to-all(f32[32,2,128]{2,1,0:T(2,128)S(1)} %bitcast.12), channel_id=1, replica_groups=mesh['freq'=2,'depth'=16] {'freq','depth'}, dimensions={0} | all-to-all | bytes 65536 | tf_op jit(solution)/shard_map/all_to_all | solution.py:225
  29.0 0.8 %combine.1 = f32[4,16,32]{2,1,0:T(8,128)} custom-call(f32[64,128]{1,0:T(8,128)S(1)} %bitcast.13), custom_call_target="tpu_custom_call" | custom-call | bytes 2097152 | tf_op jit(solution)/shard_map/combine/pallas_call | solution.py:226
Async XLA Ops:
  0.0 5.9 %copy-start.1 = (bf16[2,1,128,2,256]{4,3,2,1,0:T(2,128)(2,1)S(1)}, bf16[2,1,128,2,256]{4,3,2,1,0:T(2,128)(2,1)}, u32[]{:S(2)}) copy-start(bf16[2,1,128,2,256]{4,3,2,1,0:T(2,128)(2,1)} %param.7) | copy-start | bytes 786436
  0.0 14.4 %collective-permute-start.1 = (bf16[2,128,2,256]{3,2,1,0:T(2,128)(2,1)}, bf16[2,128,2,256]{3,2,1,0:T(2,128)(2,1)S(1)}, u32[]{:S(2)}, u32[]{:S(2)}) collective-permute-start(bf16[2,128,2,256]{3,2,1,0:T(2,128)(2,1)} %bitcast.17), channel_id=1, source_target_pairs={{0,1},{1,0},{2,3},{3,2},{4,5},{5,4},{6,7},{7,6},{8,9},{9,8},{10,11... | collective-permute-start | bytes 786440 | tf_op jit(solution)/shard_map/ppermute | solution.py:183
  2.9 12.2 %collective-permute-start = (bf16[2,128,2,256]{3,2,1,0:T(2,128)(2,1)}, bf16[2,128,2,256]{3,2,1,0:T(2,128)(2,1)S(1)}, u32[]{:S(2)}, u32[]{:S(2)}) collective-permute-start(bf16[2,128,2,256]{3,2,1,0:T(2,128)(2,1)} %bitcast.18), channel_id=1, source_target_pairs={{1,2},{3,4},{5,6},{7,8},{9,10},{11,12},{13,14},{2,1},{4,3},{6,5},{... | collective-permute-start | bytes 786440 | tf_op jit(solution)/shard_map/ppermute | solution.py:184
  2.9 3.0 %copy-start.2 = (s32[1024]{0:T(1024)S(1)}, s32[1024]{0:T(1024)}, u32[]{:S(2)}) copy-start(s32[1024]{0:T(1024)} %param.8) | copy-start | bytes 12292
  5.2 0.7 %copy-start = (s32[1024]{0:T(1024)S(1)}, s32[1024]{0:T(1024)}, u32[]{:S(2)}) copy-start(s32[1024]{0:T(1024)} %param.9) | copy-start | bytes 12292
  5.9 0.7 %copy-start.3 = (s32[2]{0:T(128)S(1)}, s32[2]{0:T(128)}, u32[]{:S(2)}) copy-start(s32[2]{0:T(128)} %bins_ref.1) | copy-start | bytes 28

commit v5 on v4

--- a/solution.py
+++ b/solution.py
@@ -36,13 +36,16 @@
     return jnp.concatenate([along_x, along_y], axis=0).astype(jnp.bfloat16)
 
 
-def pick_pairs(products, hot, receiver_ref):
+def pick_sources(products, hot):
     receivers = products.shape[0]
-    pairs = receiver_ref.shape[1]
     high = products.astype(jnp.bfloat16)
     low = (products - high.astype(jnp.float32)).astype(jnp.bfloat16)
     both = dot(jnp.concatenate([high, low], axis=0), hot)
-    picked = both[:receivers] + both[receivers:]
+    return both[:receivers] + both[receivers:]
+
+
+def pick_receivers(picked, receiver_ref):
+    receivers, pairs = picked.shape
     at_receiver = lax.broadcasted_iota(jnp.int32, (receivers, pairs), 0) == receiver_ref[...]
     row = jnp.sum(jnp.where(at_receiver, picked, 0.0), axis=0, keepdims=True)
     return jnp.concatenate(
@@ -59,19 +62,21 @@
     green_s,
     green_r,
     out_ref,
-    hot_ref,
+    column_ref,
     weight_ref,
 ):
     freqs, _, cells, sources = green_s.shape
     pairs = source_ref.shape[1]
     at_source = lax.broadcasted_iota(jnp.int32, (sources, pairs), 0) == source_ref[...]
-    hot_ref[...] = jnp.where(at_source, jnp.float32(1), jnp.float32(0)).astype(jnp.bfloat16)
+    hot = jnp.where(at_source, jnp.float32(1), jnp.float32(0)).astype(jnp.bfloat16)
     table = slope_table(cells)
     sound = along_x = along_y = 0.0
     for slot in range(freqs):
         weight = frequency_weight(bins_ref, slot)
         weight_ref[slot] = jnp.full(weight_ref.shape[1:], 0.5 * weight * scale, jnp.float32)
         real, imag = green_s[slot, 0], green_s[slot, 1]
+        column_ref[slot, 0] = dot(real, hot).astype(jnp.bfloat16)
+        column_ref[slot, 1] = dot(imag, hot).astype(jnp.bfloat16)
         slope_real = dot(table, real).astype(jnp.bfloat16)
         slope_imag = dot(table, imag).astype(jnp.bfloat16)
         near_real, near_imag = parts_of(green_r[slot])
@@ -81,9 +86,8 @@
         sound = sound + plain * (weight * weight * profile_ref[0] * scale)
         along_x = along_x + slope_x * (weight * scale)
         along_y = along_y + slope_y * (weight * scale)
-    hot = hot_ref[...]
     for k, products in enumerate([sound, along_x, along_y]):
-        out_ref[k] = pick_pairs(products, hot, receiver_ref)
+        out_ref[k] = pick_receivers(pick_sources(products, hot), receiver_ref)
 
 
 def parts_of(rows):
@@ -91,23 +95,23 @@
     return parts[0], parts[1]
 
 
-def layer_term(weight_ref, receiver_ref, hot, green_s, other_r):
+def layer_term(weight_ref, receiver_ref, column_ref, other_r):
     total = 0.0
-    for slot in range(green_s.shape[0]):
+    for slot in range(column_ref.shape[0]):
         real, imag = parts_of(other_r[slot])
-        both = dot(imag, green_s[slot, 0]) + dot(real, green_s[slot, 1])
+        both = dot(imag, column_ref[slot, 0]) + dot(real, column_ref[slot, 1])
         total = total + both * weight_ref[slot]
-    return pick_pairs(total, hot, receiver_ref)
-
-
-def near_term(weight_ref, receiver_ref, hot_ref, green_s, near_r, out_ref):
-    out_ref[...] = layer_term(weight_ref, receiver_ref, hot_ref[...], green_s, near_r)
+    return pick_receivers(total, receiver_ref)
+
+
+def near_term(weight_ref, receiver_ref, column_ref, near_r, out_ref):
+    out_ref[...] = layer_term(weight_ref, receiver_ref, column_ref, near_r)
 
 
 def far_term(
-    share, weight_ref, receiver_ref, hot_ref, green_s, far_r, terms, near_ref, out_ref
+    share, weight_ref, receiver_ref, column_ref, far_r, terms, near_ref, out_ref
 ):
-    far = layer_term(weight_ref, receiver_ref, hot_ref[...], green_s, far_r)
+    far = layer_term(weight_ref, receiver_ref, column_ref, far_r)
     near = near_ref[...]
     odd = lax.rem(lax.axis_index("depth"), 2) == 1
     below = jnp.where(odd, near, far)
@@ -203,25 +207,25 @@
         )
 
     term_shape = jax.ShapeDtypeStruct((tiles, LANES), jnp.float32)
-    terms, hot, weights = call(
+    terms, columns, weights = call(
         functools.partial(local_terms, scale),
         "local_terms",
         [
             jax.ShapeDtypeStruct((3, tiles, LANES), jnp.float32),
-            jax.ShapeDtypeStruct((sources, pairs), jnp.bfloat16),
-            jax.ShapeDtypeStruct((local_freqs, 1, sources), jnp.float32),
+            jax.ShapeDtypeStruct((local_freqs, 2, cells, pairs), jnp.bfloat16),
+            jax.ShapeDtypeStruct((local_freqs, 1, pairs), jnp.float32),
         ],
         2, 4, 3,
     )(frequency_bins, depth_profile, source_row, receiver_row, green_s, own)
-    near = call(near_term, "near_term", term_shape, 0, 5, 1)(
-        weights, receiver_row, hot, green_s, near_r
+    near = call(near_term, "near_term", term_shape, 0, 4, 1)(
+        weights, receiver_row, columns, near_r
     )
     parts = call(
         functools.partial(far_term, share),
         "far_term",
         jax.ShapeDtypeStruct((2 * owners, LANES), jnp.float32),
-        0, 7, 1,
-    )(weights, receiver_row, hot, green_s, far_r, terms, near)
+        0, 6, 1,
+    )(weights, receiver_row, columns, far_r, terms, near)
     parts = lax.all_to_all(parts, ("freq", "depth"), split_axis=0, concat_axis=0, tiled=True)
     kernels = call(
         functools.partial(combine, n_freq, n_depth, share),

time: 29.9 us -> 29.8 us (level)
  waiting for transfers between devices: 5.15 us -> 1.9 us
  local copies, waits for them, and re-layouts: 2.93 us -> 5.26 us
  Pallas kernels: 4.92 us -> 5.53 us
    ppermute x1, waiting for transfers between devices: 5.15 us -> 1.9 us  [on_device(): near_r = lax.ppermute(own, 'depth', paired)]
    unnamed x9 -> x11, local copies, waits for them, and re-layouts: 2.93 us -> 5.26 us
    pallas_call x1, Pallas kernels: 2.7 us -> 3.67 us  [on_device(): call(functools.partial(local_terms, scale), 'local_terms', [jax.ShapeDtyp...]
  transfers between devices with their start and end apart: 2 -> 2, of which waited for: 1 -> 1; matrix products, arithmetic and copies ran while one was open for 8% -> 8% of each run, Pallas kernels for 11% -> 14%
where the time goes in v5:
time: 29.8 us; the launch traced here: 29.5 us
  blocking collectives  13.2 us (44%)
  Pallas kernels  5.53 us (19%)
  local copies, waits for them, and re-layouts  5.26 us (18%)
  starting transfers between devices  2.94 us (10%)
  waiting for transfers between devices  1.9 us (6%)
  between operations  0.7 us (2%)
    all_to_all x1, blocking collectives, on_device(): lax.all_to_all(parts, ('freq', 'depth'), split_axis=0, concat_axis=0, til...  13.2 us
    unnamed x11, local copies, waits for them, and re-layouts  5.26 us
    pallas_call x1, Pallas kernels, on_device(): call(functools.partial(local_terms, scale), 'local_terms', [jax.ShapeDtyp...  3.67 us
    ppermute x1, starting transfers between devices, on_device(): near_r = lax.ppermute(own, 'depth', paired)  2.94 us
    ppermute x1, waiting for transfers between devices, on_device(): near_r = lax.ppermute(own, 'depth', paired)  1.9 us
    pallas_call x1, Pallas kernels, on_device(): call(functools.partial(combine, n_freq, n_depth, share), 'combine', jax.S...  0.76 us
  transfers between devices with their start and end apart: 2, of which 1 were waited for; matrix products, arithmetic and copies ran while one was open for 8% of the time, Pallas kernels for 14%

profile of v5, /device:TPU:0, one launch (start us, length us, event | category | flops | bytes accessed | tf_op | source)
XLA Modules:
  0.0 29.5 jit_solution(9268770580876612541)
XLA Ops:
  0.0 2.9 %collective-permute-start.1 = (bf16[2,128,2,256]{3,2,1,0:T(2,128)(2,1)}, bf16[2,128,2,256]{3,2,1,0:T(2,128)(2,1)S(1)}, u32[]{:S(2)}, u32[]{:S(2)}) collective-permute-start(bf16[2,128,2,256]{3,2,1,0:T(2,128)(2,1)} %bitcast.15), channel_id=1, source_target_pairs={{0,1},{1,0},{2,3},{3,2},{4,5},{5,4},{6,7},{7,6},{8,9},{9,8},{10,11... | collective-permute-start | bytes 786440 | tf_op jit(solution)/shard_map/ppermute | solution.py:187
  2.9 0.0 collective-permute-start
  2.9 2.3 %copy.7 = bf16[2,1,384,2,256]{2,4,3,0,1:T(8,128)(2,1)S(1)} copy(bf16[2,1,384,2,256]{4,3,2,1,0:T(2,128)(2,1)} %param.6) | data formatting | bytes 1572864 | tf_op args[0]
  5.9 0.0 copy-start
  5.9 0.7 %copy-done = s32[1024]{0:T(1024)S(1)} copy-done((s32[1024]{0:T(1024)S(1)}, s32[1024]{0:T(1024)}, u32[]{:S(2)}) %copy-start) | copy-done | bytes 4120
  6.6 0.0 copy-start.2
  6.6 0.9 %copy-done.2 = bf16[2,1,128,2,256]{4,3,2,1,0:T(2,128)(2,1)S(1)} copy-done((bf16[2,1,128,2,256]{4,3,2,1,0:T(2,128)(2,1)S(1)}, bf16[2,1,128,2,256]{4,3,2,1,0:T(2,128)(2,1)}, u32[]{:S(2)}) %copy-start.2) | copy-done | bytes 262168
  7.5 0.0 copy-start.3
  7.5 0.7 %copy-done.3 = s32[1024]{0:T(1024)S(1)} copy-done((s32[1024]{0:T(1024)S(1)}, s32[1024]{0:T(1024)}, u32[]{:S(2)}) %copy-start.3) | copy-done | bytes 4120
  8.2 0.0 copy-start.4
  8.2 0.7 %copy-done.4 = s32[2]{0:T(128)S(1)} copy-done((s32[2]{0:T(128)S(1)}, s32[2]{0:T(128)}, u32[]{:S(2)}) %copy-start.4) | copy-done | bytes 32
  8.9 0.0 copy-start.1
  8.9 3.7 %local_terms.1 = (f32[3,8,128]{2,1,0:T(8,128)S(1)}, bf16[2,2,256,1024]{3,2,1,0:T(8,128)(2,1)S(1)}, f32[2,1,1024]{2,1,0:T(1,128)S(1)}) custom-call(s32[2]{0:T(128)S(1)} %copy-done.4, f32[1]{0:T(128)S(6)} %copy.8.profile_ref, s32[1,1024]{1,0:T(1,128)S(1)} %bitcast.18, s32[1,1024]{1,0:T(1,128)S(1)} %bitcast.12, bf16[2,2,256,384]{3,2,1,0:T(8,128)(2,1)S(1)} %bitcast.9, ...), custom_call_target="tpu_custom_call" | custom-call | flops 905969664 | bytes 2097152 | tf_op jit(solution)/shard_map/local_terms/pallas_call | solution.py:210
  12.5 1.9 %collective-permute-done.1.near_r = bf16[2,128,2,256]{3,2,1,0:T(2,128)(2,1)S(1)} collective-permute-done((bf16[2,128,2,256]{3,2,1,0:T(2,128)(2,1)}, bf16[2,128,2,256]{3,2,1,0:T(2,128)(2,1)S(1)}, u32[]{:S(2)}, u32[]{:S(2)}) %collective-permute-start.1) | collective-permute-done | bytes 262176 | tf_op jit(solution)/shard_map/ppermute | solution.py:187
  14.4 0.5 %near_term.1.near_ref = f32[8,128]{1,0:T(8,128)S(1)} custom-call(f32[2,1,1024]{2,1,0:T(1,128)S(1)} %get-tuple-element.8.weight_ref, s32[1,1024]{1,0:T(1,128)S(1)} %bitcast.13, bf16[2,2,256,1024]{3,2,1,0:T(8,128)(2,1)S(1)} %get-tuple-element.9.column_ref, bf16[2,128,2,256]{3,2,1,0:T(2,128)(2,1)S(1)} %collective-permute-done.1.near_r), custom_call_target="tpu_custom_call" | custom-call | flops 301989888 | bytes 2097152 | tf_op jit(solution)/shard_map/near_term/pallas_call | solution.py:220
  15.0 0.0 collective-permute-done.far_r
  15.0 0.0 copy-done.1
  15.0 0.6 %far_term.1 = f32[64,128]{1,0:T(8,128)S(1)} custom-call(f32[2,1,1024]{2,1,0:T(1,128)S(1)} %get-tuple-element.8.weight_ref, s32[1,1024]{1,0:T(1,128)S(1)} %bitcast.14, bf16[2,2,256,1024]{3,2,1,0:T(8,128)(2,1)S(1)} %get-tuple-element.9.column_ref, bf16[2,128,2,256]{3,2,1,0:T(2,128)(2,1)S(1)} %collective-permute-done.far_r, ...), custom_call_target="tpu_custom_call" | custom-call | flops 301989888 | bytes 2097152 | tf_op jit(solution)/shard_map/far_term/pallas_call | solution.py:223
  15.6 13.2 %all_to_all.11 = f32[32,2,128]{2,1,0:T(2,128)S(1)} all-to-all(f32[32,2,128]{2,1,0:T(2,128)S(1)} %bitcast.10), channel_id=1, replica_groups=mesh['freq'=2,'depth'=16] {'freq','depth'}, dimensions={0} | all-to-all | bytes 65536 | tf_op jit(solution)/shard_map/all_to_all | solution.py:229
  28.8 0.8 %combine.1 = f32[4,16,32]{2,1,0:T(8,128)} custom-call(f32[64,128]{1,0:T(8,128)S(1)} %bitcast.11), custom_call_target="tpu_custom_call" | custom-call | bytes 2097152 | tf_op jit(solution)/shard_map/combine/pallas_call | solution.py:230
Async XLA Ops:
  0.0 14.4 %collective-permute-start.1 = (bf16[2,128,2,256]{3,2,1,0:T(2,128)(2,1)}, bf16[2,128,2,256]{3,2,1,0:T(2,128)(2,1)S(1)}, u32[]{:S(2)}, u32[]{:S(2)}) collective-permute-start(bf16[2,128,2,256]{3,2,1,0:T(2,128)(2,1)} %bitcast.15), channel_id=1, source_target_pairs={{0,1},{1,0},{2,3},{3,2},{4,5},{5,4},{6,7},{7,6},{8,9},{9,8},{10,11... | collective-permute-start | bytes 786440 | tf_op jit(solution)/shard_map/ppermute | solution.py:187
  2.9 12.0 %collective-permute-start = (bf16[2,128,2,256]{3,2,1,0:T(2,128)(2,1)}, bf16[2,128,2,256]{3,2,1,0:T(2,128)(2,1)S(1)}, u32[]{:S(2)}, u32[]{:S(2)}) collective-permute-start(bf16[2,128,2,256]{3,2,1,0:T(2,128)(2,1)} %bitcast.16), channel_id=1, source_target_pairs={{1,2},{3,4},{5,6},{7,8},{9,10},{11,12},{13,14},{2,1},{4,3},{6,5},{... | collective-permute-start | bytes 786440 | tf_op jit(solution)/shard_map/ppermute | solution.py:188
  5.9 0.7 %copy-start = (s32[1024]{0:T(1024)S(1)}, s32[1024]{0:T(1024)}, u32[]{:S(2)}) copy-start(s32[1024]{0:T(1024)} %param.9) | copy-start | bytes 12292
  6.6 0.9 %copy-start.2 = (bf16[2,1,128,2,256]{4,3,2,1,0:T(2,128)(2,1)S(1)}, bf16[2,1,128,2,256]{4,3,2,1,0:T(2,128)(2,1)}, u32[]{:S(2)}) copy-start(bf16[2,1,128,2,256]{4,3,2,1,0:T(2,128)(2,1)} %param.7) | copy-start | bytes 786436
  7.5 0.7 %copy-start.3 = (s32[1024]{0:T(1024)S(1)}, s32[1024]{0:T(1024)}, u32[]{:S(2)}) copy-start(s32[1024]{0:T(1024)} %param.8) | copy-start | bytes 12292
  8.2 0.7 %copy-start.4 = (s32[2]{0:T(128)S(1)}, s32[2]{0:T(128)}, u32[]{:S(2)}) copy-start(s32[2]{0:T(128)} %bins_ref.1) | copy-start | bytes 28
  8.9 6.1 %copy-start.1 = (s32[1024]{0:T(1024)S(1)}, s32[1024]{0:T(1024)}, u32[]{:S(2)}) copy-start(s32[1024]{0:T(1024)} %param.9) | copy-start | bytes 12292

commit v6 on v5

--- a/solution.py
+++ b/solution.py
@@ -138,15 +138,13 @@
             total = total + parts_ref[pl.ds(2 * group * depths + which, depths, stride=2), :]
         return total
 
-    first = row(0)
-    above = row(1)[:, :share]
+    first, second = row(0), row(1)
+    depth = lax.broadcasted_iota(jnp.int32, first.shape, 0)
+    above = jnp.where(depth == depths - 1, 0.0, pltpu.roll(first, depths - 1, 0))
+    below = jnp.where(depth == 0, 0.0, pltpu.roll(second, 1, 0))
     for k in range(3):
-        out_ref[k] = first[:, k * share : (k + 1) * share]
-    below = first[:, 3 * share : 4 * share]
-    blank = jnp.zeros((1, share), jnp.float32)
-    out_ref[3] = jnp.concatenate([below[1:], blank], axis=0) - jnp.concatenate(
-        [blank, above[:-1]], axis=0
-    )
+        out_ref[k] = pltpu.roll(first, (LANES - k * share) % LANES, 1)[:, :share]
+    out_ref[3] = (pltpu.roll(above, LANES - 3 * share, 1) - below)[:, :share]
 
 
 def vmem(count):

time: 29.8 us -> 29.8 us (level)
  no operation moved by 1% of the time
where the time goes in v6:
time: 29.8 us; the launch traced here: 29.5 us
  blocking collectives  13.2 us (44%)
  Pallas kernels  5.46 us (18%)
  local copies, waits for them, and re-layouts  5.26 us (18%)
  starting transfers between devices  2.94 us (10%)
  waiting for transfers between devices  1.9 us (6%)
  between operations  0.7 us (2%)
    all_to_all x1, blocking collectives, on_device(): lax.all_to_all(parts, ('freq', 'depth'), split_axis=0, concat_axis=0, til...  13.2 us
    unnamed x11, local copies, waits for them, and re-layouts  5.26 us
    pallas_call x1, Pallas kernels, on_device(): call(functools.partial(local_terms, scale), 'local_terms', [jax.ShapeDtyp...  3.67 us
    ppermute x1, starting transfers between devices, on_device(): near_r = lax.ppermute(own, 'depth', paired)  2.94 us
    ppermute x1, waiting for transfers between devices, on_device(): near_r = lax.ppermute(own, 'depth', paired)  1.9 us
    pallas_call x1, Pallas kernels, on_device(): call(functools.partial(combine, n_freq, n_depth, share), 'combine', jax.S...  0.69 us
  transfers between devices with their start and end apart: 2, of which 1 were waited for; matrix products, arithmetic and copies ran while one was open for 8% of the time, Pallas kernels for 14%

profile of v6, /device:TPU:0, one launch (start us, length us, event | category | flops | bytes accessed | tf_op | source)
XLA Modules:
  0.0 29.5 jit_solution(6389325940205661650)
XLA Ops:
  0.0 2.9 %collective-permute-start.1 = (bf16[2,128,2,256]{3,2,1,0:T(2,128)(2,1)}, bf16[2,128,2,256]{3,2,1,0:T(2,128)(2,1)S(1)}, u32[]{:S(2)}, u32[]{:S(2)}) collective-permute-start(bf16[2,128,2,256]{3,2,1,0:T(2,128)(2,1)} %bitcast.15), channel_id=1, source_target_pairs={{0,1},{1,0},{2,3},{3,2},{4,5},{5,4},{6,7},{7,6},{8,9},{9,8},{10,11... | collective-permute-start | bytes 786440 | tf_op jit(solution)/shard_map/ppermute | solution.py:185
  2.9 0.0 collective-permute-start
  2.9 2.3 %copy.7 = bf16[2,1,384,2,256]{2,4,3,0,1:T(8,128)(2,1)S(1)} copy(bf16[2,1,384,2,256]{4,3,2,1,0:T(2,128)(2,1)} %param.6) | data formatting | bytes 1572864 | tf_op args[0]
  5.9 0.0 copy-start
  5.9 0.7 %copy-done = s32[1024]{0:T(1024)S(1)} copy-done((s32[1024]{0:T(1024)S(1)}, s32[1024]{0:T(1024)}, u32[]{:S(2)}) %copy-start) | copy-done | bytes 4120
  6.6 0.0 copy-start.2
  6.6 0.9 %copy-done.2 = bf16[2,1,128,2,256]{4,3,2,1,0:T(2,128)(2,1)S(1)} copy-done((bf16[2,1,128,2,256]{4,3,2,1,0:T(2,128)(2,1)S(1)}, bf16[2,1,128,2,256]{4,3,2,1,0:T(2,128)(2,1)}, u32[]{:S(2)}) %copy-start.2) | copy-done | bytes 262168
  7.5 0.0 copy-start.3
  7.5 0.7 %copy-done.3 = s32[1024]{0:T(1024)S(1)} copy-done((s32[1024]{0:T(1024)S(1)}, s32[1024]{0:T(1024)}, u32[]{:S(2)}) %copy-start.3) | copy-done | bytes 4120
  8.2 0.0 copy-start.4
  8.2 0.7 %copy-done.4 = s32[2]{0:T(128)S(1)} copy-done((s32[2]{0:T(128)S(1)}, s32[2]{0:T(128)}, u32[]{:S(2)}) %copy-start.4) | copy-done | bytes 32
  8.9 0.0 copy-start.1
  8.9 3.7 %local_terms.1 = (f32[3,8,128]{2,1,0:T(8,128)S(1)}, bf16[2,2,256,1024]{3,2,1,0:T(8,128)(2,1)S(1)}, f32[2,1,1024]{2,1,0:T(1,128)S(1)}) custom-call(s32[2]{0:T(128)S(1)} %copy-done.4, f32[1]{0:T(128)S(6)} %copy.8.profile_ref, s32[1,1024]{1,0:T(1,128)S(1)} %bitcast.18, s32[1,1024]{1,0:T(1,128)S(1)} %bitcast.12, bf16[2,2,256,384]{3,2,1,0:T(8,128)(2,1)S(1)} %bitcast.9, ...), custom_call_target="tpu_custom_call" | custom-call | flops 905969664 | bytes 2097152 | tf_op jit(solution)/shard_map/local_terms/pallas_call | solution.py:208
  12.5 1.9 %collective-permute-done.1.near_r = bf16[2,128,2,256]{3,2,1,0:T(2,128)(2,1)S(1)} collective-permute-done((bf16[2,128,2,256]{3,2,1,0:T(2,128)(2,1)}, bf16[2,128,2,256]{3,2,1,0:T(2,128)(2,1)S(1)}, u32[]{:S(2)}, u32[]{:S(2)}) %collective-permute-start.1) | collective-permute-done | bytes 262176 | tf_op jit(solution)/shard_map/ppermute | solution.py:185
  14.4 0.5 %near_term.1.near_ref = f32[8,128]{1,0:T(8,128)S(1)} custom-call(f32[2,1,1024]{2,1,0:T(1,128)S(1)} %get-tuple-element.8.weight_ref, s32[1,1024]{1,0:T(1,128)S(1)} %bitcast.13, bf16[2,2,256,1024]{3,2,1,0:T(8,128)(2,1)S(1)} %get-tuple-element.9.column_ref, bf16[2,128,2,256]{3,2,1,0:T(2,128)(2,1)S(1)} %collective-permute-done.1.near_r), custom_call_target="tpu_custom_call" | custom-call | flops 301989888 | bytes 2097152 | tf_op jit(solution)/shard_map/near_term/pallas_call | solution.py:218
  15.0 0.0 collective-permute-done.far_r
  15.0 0.0 copy-done.1
  15.0 0.6 %far_term.1 = f32[64,128]{1,0:T(8,128)S(1)} custom-call(f32[2,1,1024]{2,1,0:T(1,128)S(1)} %get-tuple-element.8.weight_ref, s32[1,1024]{1,0:T(1,128)S(1)} %bitcast.14, bf16[2,2,256,1024]{3,2,1,0:T(8,128)(2,1)S(1)} %get-tuple-element.9.column_ref, bf16[2,128,2,256]{3,2,1,0:T(2,128)(2,1)S(1)} %collective-permute-done.far_r, ...), custom_call_target="tpu_custom_call" | custom-call | flops 301989888 | bytes 2097152 | tf_op jit(solution)/shard_map/far_term/pallas_call | solution.py:221
  15.6 13.2 %all_to_all.11 = f32[32,2,128]{2,1,0:T(2,128)S(1)} all-to-all(f32[32,2,128]{2,1,0:T(2,128)S(1)} %bitcast.10), channel_id=1, replica_groups=mesh['freq'=2,'depth'=16] {'freq','depth'}, dimensions={0} | all-to-all | bytes 65536 | tf_op jit(solution)/shard_map/all_to_all | solution.py:227
  28.8 0.7 %combine.1 = f32[4,16,32]{2,1,0:T(8,128)} custom-call(f32[64,128]{1,0:T(8,128)S(1)} %bitcast.11), custom_call_target="tpu_custom_call" | custom-call | bytes 2097152 | tf_op jit(solution)/shard_map/combine/pallas_call | solution.py:228
Async XLA Ops:
  0.0 14.4 %collective-permute-start.1 = (bf16[2,128,2,256]{3,2,1,0:T(2,128)(2,1)}, bf16[2,128,2,256]{3,2,1,0:T(2,128)(2,1)S(1)}, u32[]{:S(2)}, u32[]{:S(2)}) collective-permute-start(bf16[2,128,2,256]{3,2,1,0:T(2,128)(2,1)} %bitcast.15), channel_id=1, source_target_pairs={{0,1},{1,0},{2,3},{3,2},{4,5},{5,4},{6,7},{7,6},{8,9},{9,8},{10,11... | collective-permute-start | bytes 786440 | tf_op jit(solution)/shard_map/ppermute | solution.py:185
  2.9 12.0 %collective-permute-start = (bf16[2,128,2,256]{3,2,1,0:T(2,128)(2,1)}, bf16[2,128,2,256]{3,2,1,0:T(2,128)(2,1)S(1)}, u32[]{:S(2)}, u32[]{:S(2)}) collective-permute-start(bf16[2,128,2,256]{3,2,1,0:T(2,128)(2,1)} %bitcast.16), channel_id=1, source_target_pairs={{1,2},{3,4},{5,6},{7,8},{9,10},{11,12},{13,14},{2,1},{4,3},{6,5},{... | collective-permute-start | bytes 786440 | tf_op jit(solution)/shard_map/ppermute | solution.py:186
  5.9 0.7 %copy-start = (s32[1024]{0:T(1024)S(1)}, s32[1024]{0:T(1024)}, u32[]{:S(2)}) copy-start(s32[1024]{0:T(1024)} %param.9) | copy-start | bytes 12292
  6.6 0.9 %copy-start.2 = (bf16[2,1,128,2,256]{4,3,2,1,0:T(2,128)(2,1)S(1)}, bf16[2,1,128,2,256]{4,3,2,1,0:T(2,128)(2,1)}, u32[]{:S(2)}) copy-start(bf16[2,1,128,2,256]{4,3,2,1,0:T(2,128)(2,1)} %param.7) | copy-start | bytes 786436
  7.5 0.7 %copy-start.3 = (s32[1024]{0:T(1024)S(1)}, s32[1024]{0:T(1024)}, u32[]{:S(2)}) copy-start(s32[1024]{0:T(1024)} %param.8) | copy-start | bytes 12292
  8.2 0.7 %copy-start.4 = (s32[2]{0:T(128)S(1)}, s32[2]{0:T(128)}, u32[]{:S(2)}) copy-start(s32[2]{0:T(128)} %bins_ref.1) | copy-start | bytes 28
  8.9 6.1 %copy-start.1 = (s32[1024]{0:T(1024)S(1)}, s32[1024]{0:T(1024)}, u32[]{:S(2)}) copy-start(s32[1024]{0:T(1024)} %param.9) | copy-start | bytes 12292

commit v7 on v6

--- a/solution.py
+++ b/solution.py
@@ -95,10 +95,10 @@
     return parts[0], parts[1]
 
 
-def layer_term(weight_ref, receiver_ref, column_ref, other_r):
+def layer_term(weight_ref, receiver_ref, column_ref, other_r, first=0):
     total = 0.0
-    for slot in range(column_ref.shape[0]):
-        real, imag = parts_of(other_r[slot])
+    for slot in range(first, first + other_r.shape[0]):
+        real, imag = parts_of(other_r[slot - first])
         both = dot(imag, column_ref[slot, 0]) + dot(real, column_ref[slot, 1])
         total = total + both * weight_ref[slot]
     return pick_receivers(total, receiver_ref)
@@ -109,9 +109,10 @@
 
 
 def far_term(
-    share, weight_ref, receiver_ref, column_ref, far_r, terms, near_ref, out_ref
+    share, weight_ref, receiver_ref, column_ref, far_r, terms, near_ref, half_ref, out_ref
 ):
-    far = layer_term(weight_ref, receiver_ref, column_ref, far_r)
+    first = column_ref.shape[0] - far_r.shape[0]
+    far = half_ref[...] + layer_term(weight_ref, receiver_ref, column_ref, far_r, first)
     near = near_ref[...]
     odd = lax.rem(lax.axis_index("depth"), 2) == 1
     below = jnp.where(odd, near, far)
@@ -183,7 +184,9 @@
         for end in (0, n_depth - 1)
     ]
     near_r = lax.ppermute(own, "depth", paired)
-    far_r = lax.ppermute(own, ("freq", "depth"), everywhere)
+    half = local_freqs // 2
+    far_a = lax.ppermute(own[:half], ("freq", "depth"), everywhere)
+    far_b = lax.ppermute(own[half:], ("freq", "depth"), everywhere)
 
     green_s = jnp.transpose(green_source[:, 0], (0, 2, 3, 1))
     source_row = source_index.reshape(1, pairs)
@@ -199,7 +202,7 @@
             out_specs=jax.tree.map(lambda _: pl.BlockSpec(memory_space=pltpu.VMEM), shapes),
             compiler_params=params,
             cost_estimate=pl.CostEstimate(
-                flops=terms * (product + picking), bytes_accessed=1 << 21, transcendentals=0
+                flops=int(terms * (product + picking)), bytes_accessed=1 << 21, transcendentals=0
             ),
             name=name,
         )
@@ -218,12 +221,15 @@
     near = call(near_term, "near_term", term_shape, 0, 4, 1)(
         weights, receiver_row, columns, near_r
     )
+    halved = call(near_term, "half_term", term_shape, 0, 4, 0.5)(
+        weights, receiver_row, columns, far_a
+    )
     parts = call(
         functools.partial(far_term, share),
         "far_term",
         jax.ShapeDtypeStruct((2 * owners, LANES), jnp.float32),
-        0, 6, 1,
-    )(weights, receiver_row, columns, far_r, terms, near)
+        0, 7, 1,
+    )(weights, receiver_row, columns, far_b, terms, near, halved)
     parts = lax.all_to_all(parts, ("freq", "depth"), split_axis=0, concat_axis=0, tiled=True)
     kernels = call(
         functools.partial(combine, n_freq, n_depth, share),

time: 29.8 us -> 29.6 us (level)
  local copies, waits for them, and re-layouts: 5.26 us -> 3.45 us
  waiting for transfers between devices: 1.9 us -> 2.76 us
  starting transfers between devices: 2.94 us -> 3.58 us
    unnamed x11 -> x9, local copies, waits for them, and re-layouts: 5.26 us -> 2.3 us
    slice x0 -> x1, local copies, waits for them, and re-layouts: none -> 1.16 us  [on_device(): far_a = lax.ppermute(own[:half], ('freq', 'depth'), everywhere)]
    ppermute x1, waiting for transfers between devices: 1.9 us -> 2.76 us  [on_device(): near_r = lax.ppermute(own, 'depth', paired)]
    ppermute x1 -> x2, starting transfers between devices: 0.01 us -> 0.57 us  [the longest x1 0.5 us: on_device(): far_b = lax.ppermute(own[half:], ('freq', 'depth'), everywhere)]
    pallas_call x0 -> x1, Pallas kernels: none -> 0.34 us  [on_device(): call(near_term, 'half_term', term_shape, 0, 4, 0.5)]
  transfers between devices with their start and end apart: 2 -> 3, of which waited for: 1 -> 1; matrix products, arithmetic and copies ran while one was open for 8% -> 12% of each run, Pallas kernels for 14% -> 15%
where the time goes in v7:
time: 29.6 us; the launch traced here: 29.4 us
  blocking collectives  13.2 us (45%)
  Pallas kernels  5.62 us (19%)
  starting transfers between devices  3.58 us (12%)
  local copies, waits for them, and re-layouts  3.45 us (12%)
  waiting for transfers between devices  2.76 us (9%)
  between operations  0.74 us (2%)
    all_to_all x1, blocking collectives, on_device(): lax.all_to_all(parts, ('freq', 'depth'), split_axis=0, concat_axis=0, til...  13.2 us
    pallas_call x1, Pallas kernels, on_device(): call(functools.partial(local_terms, scale), 'local_terms', [jax.ShapeDtyp...  3.66 us
    ppermute x1, starting transfers between devices, on_device(): near_r = lax.ppermute(own, 'depth', paired)  3.01 us
    ppermute x1, waiting for transfers between devices, on_device(): near_r = lax.ppermute(own, 'depth', paired)  2.76 us
    unnamed x9, local copies, waits for them, and re-layouts  2.3 us
    slice x1, local copies, waits for them, and re-layouts, on_device(): far_a = lax.ppermute(own[:half], ('freq', 'depth'), everywhere)  1.16 us
    pallas_call x1, Pallas kernels, on_device(): call(functools.partial(combine, n_freq, n_depth, share), 'combine', jax.S...  0.69 us
  transfers between devices with their start and end apart: 3, of which 1 were waited for; matrix products, arithmetic and copies ran while one was open for 12% of the time, Pallas kernels for 15%

profile of v7, /device:TPU:0, one launch (start us, length us, event | category | flops | bytes accessed | tf_op | source)
XLA Modules:
  0.0 29.4 jit_solution(3995941243880203487)
XLA Ops:
  0.0 0.0 copy-start
  0.0 0.0 copy-start.1
  0.0 0.0 copy-start.2
  0.0 0.0 copy-start.3
  0.0 3.0 %collective-permute-start.1 = (bf16[2,128,2,256]{3,2,1,0:T(2,128)(2,1)}, bf16[2,128,2,256]{3,2,1,0:T(2,128)(2,1)S(1)}, u32[]{:S(2)}, u32[]{:S(2)}) collective-permute-start(bf16[2,128,2,256]{3,2,1,0:T(2,128)(2,1)} %bitcast.14), channel_id=1, source_target_pairs={{0,1},{1,0},{2,3},{3,2},{4,5},{5,4},{6,7},{7,6},{8,9},{9,8},{10,11... | collective-permute-start | bytes 786440 | tf_op jit(solution)/shard_map/ppermute | solution.py:186
  3.0 1.2 %slice_bitcast_fusion = (bf16[1,128,2,256]{3,2,1,0:T(2,128)(2,1)S(1)}, bf16[1,128,2,256]{3,2,1,0:T(2,128)(2,1)S(1)}) fusion(bf16[2,1,128,2,256]{4,3,2,1,0:T(2,128)(2,1)} %param.7), kind=kLoop, calls=%fused_computation | loop fusion | bytes 524288 | tf_op jit(solution)/shard_map/slice | solution.py:188
  4.2 0.1 collective-permute-start.2
  4.3 0.5 %collective-permute-start = (bf16[1,128,2,256]{3,2,1,0:T(2,128)(2,1)S(1)}, bf16[1,128,2,256]{3,2,1,0:T(2,128)(2,1)S(1)}, u32[]{:S(2)}, u32[]{:S(2)}) collective-permute-start(bf16[1,128,2,256]{3,2,1,0:T(2,128)(2,1)S(1)} %get-tuple-element.12), channel_id=1, source_target_pairs={{1,2},{3,4},{5,6},{7,8},{9,10},{11,12},{13,14},{2,1},{4,3},{6,5},{... | collective-permute-start | bytes 393224 | tf_op jit(solution)/shard_map/ppermute | solution.py:189
  4.8 2.3 %copy.7 = bf16[2,1,384,2,256]{2,4,3,0,1:T(8,128)(2,1)S(1)} copy(bf16[2,1,384,2,256]{4,3,2,1,0:T(2,128)(2,1)} %param.6) | data formatting | bytes 1572864 | tf_op args[0]
  7.7 0.0 copy-done
  7.7 0.0 copy-done.1
  7.7 0.0 copy-done.2
  7.7 0.0 copy-done.3
  7.7 3.7 %local_terms.1 = (f32[3,8,128]{2,1,0:T(8,128)S(1)}, bf16[2,2,256,1024]{3,2,1,0:T(8,128)(2,1)S(1)}, f32[2,1,1024]{2,1,0:T(1,128)S(1)}) custom-call(s32[2]{0:T(128)S(1)} %copy-done.3, f32[1]{0:T(128)S(6)} %copy.8.profile_ref, s32[1,1024]{1,0:T(1,128)S(1)} %bitcast.22, s32[1,1024]{1,0:T(1,128)S(1)} %bitcast.18, bf16[2,2,256,384]{3,2,1,0:T(8,128)(2,1)S(1)} %bitcast.13, ...), custom_call_target="tpu_custom_call" | custom-call | flops 905969664 | bytes 2097152 | tf_op jit(solution)/shard_map/local_terms/pallas_call | solution.py:211
  11.4 0.0 collective-permute-done.2.near_r
  11.4 0.3 %half_term.1.half_ref = f32[8,128]{1,0:T(8,128)S(1)} custom-call(f32[2,1,1024]{2,1,0:T(1,128)S(1)} %get-tuple-element.8.weight_ref, s32[1,1024]{1,0:T(1,128)S(1)} %bitcast.19, bf16[2,2,256,1024]{3,2,1,0:T(8,128)(2,1)S(1)} %get-tuple-element.9.column_ref, bf16[1,128,2,256]{3,2,1,0:T(2,128)(2,1)S(1)} %collective-permute-done.2.near_r), custom_call_target="tpu_custom_call" | custom-call | flops 150994944 | bytes 2097152 | tf_op jit(solution)/shard_map/half_term/pallas_call | solution.py:224
  11.8 2.8 %collective-permute-done.1.near_r = bf16[2,128,2,256]{3,2,1,0:T(2,128)(2,1)S(1)} collective-permute-done((bf16[2,128,2,256]{3,2,1,0:T(2,128)(2,1)}, bf16[2,128,2,256]{3,2,1,0:T(2,128)(2,1)S(1)}, u32[]{:S(2)}, u32[]{:S(2)}) %collective-permute-start.1) | collective-permute-done | bytes 262176 | tf_op jit(solution)/shard_map/ppermute | solution.py:186
  14.5 0.5 %near_term.1.near_ref = f32[8,128]{1,0:T(8,128)S(1)} custom-call(f32[2,1,1024]{2,1,0:T(1,128)S(1)} %get-tuple-element.8.weight_ref, s32[1,1024]{1,0:T(1,128)S(1)} %bitcast.20, bf16[2,2,256,1024]{3,2,1,0:T(8,128)(2,1)S(1)} %get-tuple-element.9.column_ref, bf16[2,128,2,256]{3,2,1,0:T(2,128)(2,1)S(1)} %collective-permute-done.1.near_r), custom_call_target="tpu_custom_call" | custom-call | flops 301989888 | bytes 2097152 | tf_op jit(solution)/shard_map/near_term/pallas_call | solution.py:221
  15.0 0.0 collective-permute-done.far_r
  15.1 0.4 %far_term.1 = f32[64,128]{1,0:T(8,128)S(1)} custom-call(f32[2,1,1024]{2,1,0:T(1,128)S(1)} %get-tuple-element.8.weight_ref, s32[1,1024]{1,0:T(1,128)S(1)} %bitcast.21, bf16[2,2,256,1024]{3,2,1,0:T(8,128)(2,1)S(1)} %get-tuple-element.9.column_ref, bf16[1,128,2,256]{3,2,1,0:T(2,128)(2,1)S(1)} %collective-permute-done.far_r, ...), custom_call_target="tpu_custom_call" | custom-call | flops 301989888 | bytes 2097152 | tf_op jit(solution)/shard_map/far_term/pallas_call | solution.py:227
  15.5 13.2 %all_to_all.11 = f32[32,2,128]{2,1,0:T(2,128)S(1)} all-to-all(f32[32,2,128]{2,1,0:T(2,128)S(1)} %bitcast.16), channel_id=1, replica_groups=mesh['freq'=2,'depth'=16] {'freq','depth'}, dimensions={0} | all-to-all | bytes 65536 | tf_op jit(solution)/shard_map/all_to_all | solution.py:233
  28.7 0.7 %combine.1 = f32[4,16,32]{2,1,0:T(8,128)} custom-call(f32[64,128]{1,0:T(8,128)S(1)} %bitcast.17), custom_call_target="tpu_custom_call" | custom-call | bytes 2097152 | tf_op jit(solution)/shard_map/combine/pallas_call | solution.py:234
Async XLA Ops:
  0.0 7.7 %copy-start = (bf16[2,1,128,2,256]{4,3,2,1,0:T(2,128)(2,1)S(1)}, bf16[2,1,128,2,256]{4,3,2,1,0:T(2,128)(2,1)}, u32[]{:S(2)}) copy-start(bf16[2,1,128,2,256]{4,3,2,1,0:T(2,128)(2,1)} %param.7) | copy-start | bytes 786436
  0.0 7.7 %copy-start.1 = (s32[1024]{0:T(1024)S(1)}, s32[1024]{0:T(1024)}, u32[]{:S(2)}) copy-start(s32[1024]{0:T(1024)} %param.9) | copy-start | bytes 12292
  0.0 7.7 %copy-start.2 = (s32[1024]{0:T(1024)S(1)}, s32[1024]{0:T(1024)}, u32[]{:S(2)}) copy-start(s32[1024]{0:T(1024)} %param.8) | copy-start | bytes 12292
  0.0 7.7 %copy-start.3 = (s32[2]{0:T(128)S(1)}, s32[2]{0:T(128)}, u32[]{:S(2)}) copy-start(s32[2]{0:T(128)} %bins_ref.1) | copy-start | bytes 28
  0.0 14.5 %collective-permute-start.1 = (bf16[2,128,2,256]{3,2,1,0:T(2,128)(2,1)}, bf16[2,128,2,256]{3,2,1,0:T(2,128)(2,1)S(1)}, u32[]{:S(2)}, u32[]{:S(2)}) collective-permute-start(bf16[2,128,2,256]{3,2,1,0:T(2,128)(2,1)} %bitcast.14), channel_id=1, source_target_pairs={{0,1},{1,0},{2,3},{3,2},{4,5},{5,4},{6,7},{7,6},{8,9},{9,8},{10,11... | collective-permute-start | bytes 786440 | tf_op jit(solution)/shard_map/ppermute | solution.py:186
  4.2 7.2 %collective-permute-start.2 = (bf16[1,128,2,256]{3,2,1,0:T(2,128)(2,1)S(1)}, bf16[1,128,2,256]{3,2,1,0:T(2,128)(2,1)S(1)}, u32[]{:S(2)}, u32[]{:S(2)}) collective-permute-start(bf16[1,128,2,256]{3,2,1,0:T(2,128)(2,1)S(1)} %get-tuple-element.11), channel_id=1, source_target_pairs={{1,2},{3,4},{5,6},{7,8},{9,10},{11,12},{13,14},{2,1},{4,3},{6,5},{... | collective-permute-start | bytes 393224 | tf_op jit(solution)/shard_map/ppermute | solution.py:188
  4.3 10.8 %collective-permute-start = (bf16[1,128,2,256]{3,2,1,0:T(2,128)(2,1)S(1)}, bf16[1,128,2,256]{3,2,1,0:T(2,128)(2,1)S(1)}, u32[]{:S(2)}, u32[]{:S(2)}) collective-permute-start(bf16[1,128,2,256]{3,2,1,0:T(2,128)(2,1)S(1)} %get-tuple-element.12), channel_id=1, source_target_pairs={{1,2},{3,4},{5,6},{7,8},{9,10},{11,12},{13,14},{2,1},{4,3},{6,5},{... | collective-permute-start | bytes 393224 | tf_op jit(solution)/shard_map/ppermute | solution.py:189

commit v8 on v7

--- a/solution.py
+++ b/solution.py
@@ -115,8 +115,8 @@
     far = half_ref[...] + layer_term(weight_ref, receiver_ref, column_ref, far_r, first)
     near = near_ref[...]
     odd = lax.rem(lax.axis_index("depth"), 2) == 1
-    below = jnp.where(odd, near, far)
-    above = jnp.where(odd, far, near)
+    below = jnp.where(odd, far, near)
+    above = jnp.where(odd, near, far)
     tiles = far.shape[0]
     group = lax.broadcasted_iota(jnp.int32, (tiles, LANES), 1) // share
     in_tile = LANES // share
@@ -183,10 +183,10 @@
         for group in range(n_freq)
         for end in (0, n_depth - 1)
     ]
-    near_r = lax.ppermute(own, "depth", paired)
     half = local_freqs // 2
-    far_a = lax.ppermute(own[:half], ("freq", "depth"), everywhere)
-    far_b = lax.ppermute(own[half:], ("freq", "depth"), everywhere)
+    far_r = lax.ppermute(own, ("freq", "depth"), everywhere)
+    near_a = lax.ppermute(own[:half], "depth", paired)
+    near_b = lax.ppermute(own[half:], "depth", paired)
 
     green_s = jnp.transpose(green_source[:, 0], (0, 2, 3, 1))
     source_row = source_index.reshape(1, pairs)
@@ -219,17 +219,17 @@
         2, 4, 3,
     )(frequency_bins, depth_profile, source_row, receiver_row, green_s, own)
     near = call(near_term, "near_term", term_shape, 0, 4, 1)(
-        weights, receiver_row, columns, near_r
+        weights, receiver_row, columns, far_r
     )
     halved = call(near_term, "half_term", term_shape, 0, 4, 0.5)(
-        weights, receiver_row, columns, far_a
+        weights, receiver_row, columns, near_a
     )
     parts = call(
         functools.partial(far_term, share),
         "far_term",
         jax.ShapeDtypeStruct((2 * owners, LANES), jnp.float32),
         0, 7, 1,
-    )(weights, receiver_row, columns, far_b, terms, near, halved)
+    )(weights, receiver_row, columns, near_b, terms, near, halved)
     parts = lax.all_to_all(parts, ("freq", "depth"), split_axis=0, concat_axis=0, tiled=True)
     kernels = call(
         functools.partial(combine, n_freq, n_depth, share),

time: 29.6 us -> 29.5 us (level)
  blocking collectives: 13.2 us -> 11.9 us
  starting transfers between devices: 3.58 us -> 4.66 us
    all_to_all x1, blocking collectives: 13.2 us -> 11.9 us  [on_device(): lax.all_to_all(parts, ('freq', 'depth'), split_axis=0, concat_axis=0, til...]
    ppermute x3, starting transfers between devices: 3.58 us -> 4.66 us  [the longest x1 4.05 us: on_device(): near_a = lax.ppermute(own[:half], 'depth', paired)]
  transfers between devices with their start and end apart: 3 -> 3, of which waited for: 1 -> 2; matrix products, arithmetic and copies ran while one was open for 12% -> 12% of each run, Pallas kernels for 15% -> 15%
where the time goes in v8:
time: 29.5 us; the launch traced here: 29.3 us
  blocking collectives  11.9 us (40%)
  Pallas kernels  5.61 us (19%)
  starting transfers between devices  4.66 us (16%)
  local copies, waits for them, and re-layouts  3.44 us (12%)
  waiting for transfers between devices  3.02 us (10%)
  between operations  0.73 us (2%)
    all_to_all x1, blocking collectives, on_device(): lax.all_to_all(parts, ('freq', 'depth'), split_axis=0, concat_axis=0, til...  11.9 us
    ppermute x1, starting transfers between devices, on_device(): near_a = lax.ppermute(own[:half], 'depth', paired)  4.05 us
    pallas_call x1, Pallas kernels, on_device(): call(functools.partial(local_terms, scale), 'local_terms', [jax.ShapeDtyp...  3.66 us
    unnamed x9, local copies, waits for them, and re-layouts  2.3 us
    ppermute x1, waiting for transfers between devices, on_device(): near_a = lax.ppermute(own[:half], 'depth', paired)  2.24 us
    slice x1, local copies, waits for them, and re-layouts, on_device(): near_a = lax.ppermute(own[:half], 'depth', paired)  1.15 us
    ppermute x1, waiting for transfers between devices, on_device(): near_b = lax.ppermute(own[half:], 'depth', paired)  0.78 us
    pallas_call x1, Pallas kernels, on_device(): call(functools.partial(combine, n_freq, n_depth, share), 'combine', jax.S...  0.69 us
  transfers between devices with their start and end apart: 3, of which 2 were waited for; matrix products, arithmetic and copies ran while one was open for 12% of the time, Pallas kernels for 15%

profile of v8, /device:TPU:0, one launch (start us, length us, event | category | flops | bytes accessed | tf_op | source)
XLA Modules:
  0.0 29.3 jit_solution(6360949913242216637)
XLA Ops:
  0.0 0.0 copy-start
  0.0 0.0 copy-start.1
  0.0 0.0 copy-start.2
  0.0 0.0 copy-start.3
  0.0 0.5 %collective-permute-start.1 = (bf16[2,128,2,256]{3,2,1,0:T(2,128)(2,1)}, bf16[2,128,2,256]{3,2,1,0:T(2,128)(2,1)S(1)}, u32[]{:S(2)}, u32[]{:S(2)}) collective-permute-start(bf16[2,128,2,256]{3,2,1,0:T(2,128)(2,1)} %bitcast.14), channel_id=1, source_target_pairs={{1,2},{3,4},{5,6},{7,8},{9,10},{11,12},{13,14},{2,1},{4,3},{6,5},{... | collective-permute-start | bytes 786440 | tf_op jit(solution)/shard_map/ppermute | solution.py:187
  0.5 1.1 %slice_bitcast_fusion = (bf16[1,128,2,256]{3,2,1,0:T(2,128)(2,1)S(1)}, bf16[1,128,2,256]{3,2,1,0:T(2,128)(2,1)S(1)}) fusion(bf16[2,1,128,2,256]{4,3,2,1,0:T(2,128)(2,1)} %param.7), kind=kLoop, calls=%fused_computation | loop fusion | bytes 524288 | tf_op jit(solution)/shard_map/slice | solution.py:188
  1.7 4.1 %collective-permute-start.2 = (bf16[1,128,2,256]{3,2,1,0:T(2,128)(2,1)S(1)}, bf16[1,128,2,256]{3,2,1,0:T(2,128)(2,1)S(1)}, u32[]{:S(2)}, u32[]{:S(2)}) collective-permute-start(bf16[1,128,2,256]{3,2,1,0:T(2,128)(2,1)S(1)} %get-tuple-element.11), channel_id=1, source_target_pairs={{0,1},{1,0},{2,3},{3,2},{4,5},{5,4},{6,7},{7,6},{8,9},{9,8},{10,11... | collective-permute-start | bytes 393224 | tf_op jit(solution)/shard_map/ppermute | solution.py:188
  5.7 0.1 collective-permute-start
  5.8 2.3 %copy.7 = bf16[2,1,384,2,256]{2,4,3,0,1:T(8,128)(2,1)S(1)} copy(bf16[2,1,384,2,256]{4,3,2,1,0:T(2,128)(2,1)} %param.6) | data formatting | bytes 1572864 | tf_op args[0]
  8.8 0.0 copy-done
  8.8 0.0 copy-done.1
  8.8 0.0 copy-done.2
  8.8 0.0 copy-done.3
  8.8 3.7 %local_terms.1 = (f32[3,8,128]{2,1,0:T(8,128)S(1)}, bf16[2,2,256,1024]{3,2,1,0:T(8,128)(2,1)S(1)}, f32[2,1,1024]{2,1,0:T(1,128)S(1)}) custom-call(s32[2]{0:T(128)S(1)} %copy-done.3, f32[1]{0:T(128)S(6)} %copy.8.profile_ref, s32[1,1024]{1,0:T(1,128)S(1)} %bitcast.22, s32[1,1024]{1,0:T(1,128)S(1)} %bitcast.18, bf16[2,2,256,384]{3,2,1,0:T(8,128)(2,1)S(1)} %bitcast.13, ...), custom_call_target="tpu_custom_call" | custom-call | flops 905969664 | bytes 2097152 | tf_op jit(solution)/shard_map/local_terms/pallas_call | solution.py:211
  12.5 2.2 %collective-permute-done.2.near_r = bf16[1,128,2,256]{3,2,1,0:T(2,128)(2,1)S(1)} collective-permute-done((bf16[1,128,2,256]{3,2,1,0:T(2,128)(2,1)S(1)}, bf16[1,128,2,256]{3,2,1,0:T(2,128)(2,1)S(1)}, u32[]{:S(2)}, u32[]{:S(2)}) %collective-permute-start.2) | collective-permute-done | bytes 131104 | tf_op jit(solution)/shard_map/ppermute | solution.py:188
  14.7 0.3 %half_term.1.half_ref = f32[8,128]{1,0:T(8,128)S(1)} custom-call(f32[2,1,1024]{2,1,0:T(1,128)S(1)} %get-tuple-element.8.weight_ref, s32[1,1024]{1,0:T(1,128)S(1)} %bitcast.19, bf16[2,2,256,1024]{3,2,1,0:T(8,128)(2,1)S(1)} %get-tuple-element.9.column_ref, bf16[1,128,2,256]{3,2,1,0:T(2,128)(2,1)S(1)} %collective-permute-done.2.near_r), custom_call_target="tpu_custom_call" | custom-call | flops 150994944 | bytes 2097152 | tf_op jit(solution)/shard_map/half_term/pallas_call | solution.py:224
  15.0 0.0 collective-permute-done.1.near_r
  15.1 0.5 %near_term.1.near_ref = f32[8,128]{1,0:T(8,128)S(1)} custom-call(f32[2,1,1024]{2,1,0:T(1,128)S(1)} %get-tuple-element.8.weight_ref, s32[1,1024]{1,0:T(1,128)S(1)} %bitcast.20, bf16[2,2,256,1024]{3,2,1,0:T(8,128)(2,1)S(1)} %get-tuple-element.9.column_ref, bf16[2,128,2,256]{3,2,1,0:T(2,128)(2,1)S(1)} %collective-permute-done.1.near_r), custom_call_target="tpu_custom_call" | custom-call | flops 301989888 | bytes 2097152 | tf_op jit(solution)/shard_map/near_term/pallas_call | solution.py:221
  15.6 0.8 %collective-permute-done.far_r = bf16[1,128,2,256]{3,2,1,0:T(2,128)(2,1)S(1)} collective-permute-done((bf16[1,128,2,256]{3,2,1,0:T(2,128)(2,1)S(1)}, bf16[1,128,2,256]{3,2,1,0:T(2,128)(2,1)S(1)}, u32[]{:S(2)}, u32[]{:S(2)}) %collective-permute-start) | collective-permute-done | bytes 131104 | tf_op jit(solution)/shard_map/ppermute | solution.py:189
  16.4 0.4 %far_term.1 = f32[64,128]{1,0:T(8,128)S(1)} custom-call(f32[2,1,1024]{2,1,0:T(1,128)S(1)} %get-tuple-element.8.weight_ref, s32[1,1024]{1,0:T(1,128)S(1)} %bitcast.21, bf16[2,2,256,1024]{3,2,1,0:T(8,128)(2,1)S(1)} %get-tuple-element.9.column_ref, bf16[1,128,2,256]{3,2,1,0:T(2,128)(2,1)S(1)} %collective-permute-done.far_r, ...), custom_call_target="tpu_custom_call" | custom-call | flops 301989888 | bytes 2097152 | tf_op jit(solution)/shard_map/far_term/pallas_call | solution.py:227
  16.8 11.9 %all_to_all.11 = f32[32,2,128]{2,1,0:T(2,128)S(1)} all-to-all(f32[32,2,128]{2,1,0:T(2,128)S(1)} %bitcast.16), channel_id=1, replica_groups=mesh['freq'=2,'depth'=16] {'freq','depth'}, dimensions={0} | all-to-all | bytes 65536 | tf_op jit(solution)/shard_map/all_to_all | solution.py:233
  28.6 0.7 %combine.1 = f32[4,16,32]{2,1,0:T(8,128)} custom-call(f32[64,128]{1,0:T(8,128)S(1)} %bitcast.17), custom_call_target="tpu_custom_call" | custom-call | bytes 2097152 | tf_op jit(solution)/shard_map/combine/pallas_call | solution.py:234
Async XLA Ops:
  0.0 8.8 %copy-start = (bf16[2,1,128,2,256]{4,3,2,1,0:T(2,128)(2,1)S(1)}, bf16[2,1,128,2,256]{4,3,2,1,0:T(2,128)(2,1)}, u32[]{:S(2)}) copy-start(bf16[2,1,128,2,256]{4,3,2,1,0:T(2,128)(2,1)} %param.7) | copy-start | bytes 786436
  0.0 8.8 %copy-start.1 = (s32[1024]{0:T(1024)S(1)}, s32[1024]{0:T(1024)}, u32[]{:S(2)}) copy-start(s32[1024]{0:T(1024)} %param.9) | copy-start | bytes 12292
  0.0 8.8 %copy-start.2 = (s32[1024]{0:T(1024)S(1)}, s32[1024]{0:T(1024)}, u32[]{:S(2)}) copy-start(s32[1024]{0:T(1024)} %param.8) | copy-start | bytes 12292
  0.0 8.8 %copy-start.3 = (s32[2]{0:T(128)S(1)}, s32[2]{0:T(128)}, u32[]{:S(2)}) copy-start(s32[2]{0:T(128)} %bins_ref.1) | copy-start | bytes 28
  0.0 15.0 %collective-permute-start.1 = (bf16[2,128,2,256]{3,2,1,0:T(2,128)(2,1)}, bf16[2,128,2,256]{3,2,1,0:T(2,128)(2,1)S(1)}, u32[]{:S(2)}, u32[]{:S(2)}) collective-permute-start(bf16[2,128,2,256]{3,2,1,0:T(2,128)(2,1)} %bitcast.14), channel_id=1, source_target_pairs={{1,2},{3,4},{5,6},{7,8},{9,10},{11,12},{13,14},{2,1},{4,3},{6,5},{... | collective-permute-start | bytes 786440 | tf_op jit(solution)/shard_map/ppermute | solution.py:187
  1.7 13.0 %collective-permute-start.2 = (bf16[1,128,2,256]{3,2,1,0:T(2,128)(2,1)S(1)}, bf16[1,128,2,256]{3,2,1,0:T(2,128)(2,1)S(1)}, u32[]{:S(2)}, u32[]{:S(2)}) collective-permute-start(bf16[1,128,2,256]{3,2,1,0:T(2,128)(2,1)S(1)} %get-tuple-element.11), channel_id=1, source_target_pairs={{0,1},{1,0},{2,3},{3,2},{4,5},{5,4},{6,7},{7,6},{8,9},{9,8},{10,11... | collective-permute-start | bytes 393224 | tf_op jit(solution)/shard_map/ppermute | solution.py:188
  5.7 10.6 %collective-permute-start = (bf16[1,128,2,256]{3,2,1,0:T(2,128)(2,1)S(1)}, bf16[1,128,2,256]{3,2,1,0:T(2,128)(2,1)S(1)}, u32[]{:S(2)}, u32[]{:S(2)}) collective-permute-start(bf16[1,128,2,256]{3,2,1,0:T(2,128)(2,1)S(1)} %get-tuple-element.12), channel_id=1, source_target_pairs={{0,1},{1,0},{2,3},{3,2},{4,5},{5,4},{6,7},{7,6},{8,9},{9,8},{10,11... | collective-permute-start | bytes 393224 | tf_op jit(solution)/shard_map/ppermute | solution.py:189

commit v9 on v7

--- a/solution.py
+++ b/solution.py
@@ -104,32 +104,45 @@
     return pick_receivers(total, receiver_ref)
 
 
-def near_term(weight_ref, receiver_ref, column_ref, near_r, out_ref):
+def half_term(weight_ref, receiver_ref, column_ref, near_r, out_ref):
     out_ref[...] = layer_term(weight_ref, receiver_ref, column_ref, near_r)
 
 
-def far_term(
-    share, weight_ref, receiver_ref, column_ref, far_r, terms, near_ref, half_ref, out_ref
-):
+def moved(value, share, to, part):
+    return pltpu.roll(value, (to - part) * share % LANES, 1) if to != part else value
+
+
+def base_rows(share, weight_ref, receiver_ref, column_ref, near_r, terms, out_ref):
+    near = layer_term(weight_ref, receiver_ref, column_ref, near_r)
+    odd = lax.rem(lax.axis_index("depth"), 2) == 1
+    below = jnp.where(odd, near, 0.0)
+    above = jnp.where(odd, 0.0, near)
+    tiles = near.shape[0]
+    group = lax.broadcasted_iota(jnp.int32, (tiles, LANES), 1) // share
+    in_tile = LANES // share
+    for part in range(in_tile):
+        first = moved(below, share, 3, part)
+        for k in range(3):
+            first = jnp.where(group == k, moved(terms[k], share, k, part), first)
+        out_ref[part] = first
+        out_ref[in_tile + part] = moved(above, share, 0, part)
+
+
+def far_term(share, weight_ref, receiver_ref, column_ref, far_r, base, half_ref, out_ref):
     first = column_ref.shape[0] - far_r.shape[0]
     far = half_ref[...] + layer_term(weight_ref, receiver_ref, column_ref, far_r, first)
-    near = near_ref[...]
     odd = lax.rem(lax.axis_index("depth"), 2) == 1
-    below = jnp.where(odd, near, far)
-    above = jnp.where(odd, far, near)
+    below = jnp.where(odd, 0.0, far)
+    above = jnp.where(odd, far, 0.0)
     tiles = far.shape[0]
-    group = lax.broadcasted_iota(jnp.int32, (tiles, LANES), 1) // share
+    last = lax.broadcasted_iota(jnp.int32, (tiles, LANES), 1) // share == 3
     in_tile = LANES // share
-
-    def moved(value, to, part):
-        return pltpu.roll(value, (to - part) * share % LANES, 1) if to != part else value
-
     for part in range(in_tile):
-        first = moved(below, 3, part)
-        for k in range(3):
-            first = jnp.where(group == k, moved(terms[k], k, part), first)
-        out_ref[pl.ds(2 * part, tiles, stride=2 * in_tile), :] = first
-        out_ref[pl.ds(2 * part + 1, tiles, stride=2 * in_tile), :] = moved(above, 0, part)
+        own = jnp.where(last, moved(below, share, 3, part), 0.0)
+        out_ref[pl.ds(2 * part, tiles, stride=2 * in_tile), :] = base[part] + own
+        out_ref[pl.ds(2 * part + 1, tiles, stride=2 * in_tile), :] = base[
+            in_tile + part
+        ] + moved(above, share, 0, part)
 
 
 def combine(freqs, depths, share, parts_ref, out_ref):
@@ -218,18 +231,21 @@
         ],
         2, 4, 3,
     )(frequency_bins, depth_profile, source_row, receiver_row, green_s, own)
-    near = call(near_term, "near_term", term_shape, 0, 4, 1)(
-        weights, receiver_row, columns, near_r
-    )
-    halved = call(near_term, "half_term", term_shape, 0, 4, 0.5)(
+    base = call(
+        functools.partial(base_rows, share),
+        "base_rows",
+        jax.ShapeDtypeStruct((2 * LANES // share, tiles, LANES), jnp.float32),
+        0, 5, 1,
+    )(weights, receiver_row, columns, near_r, terms)
+    halved = call(half_term, "half_term", term_shape, 0, 4, 0.5)(
         weights, receiver_row, columns, far_a
     )
     parts = call(
         functools.partial(far_term, share),
         "far_term",
         jax.ShapeDtypeStruct((2 * owners, LANES), jnp.float32),
-        0, 7, 1,
-    )(weights, receiver_row, columns, far_b, terms, near, halved)
+        0, 6, 1,
+    )(weights, receiver_row, columns, far_b, base, halved)
     parts = lax.all_to_all(parts, ("freq", "depth"), split_axis=0, concat_axis=0, tiled=True)
     kernels = call(
         functools.partial(combine, n_freq, n_depth, share),

time: 29.6 us -> 29.6 us (level)
  transfers between devices with their start and end apart: 3 -> 3, of which waited for: 1 -> 1; matrix products, arithmetic and copies ran while one was open for 12% -> 12% of each run, Pallas kernels for 15% -> 16%
where the time goes in v9:
time: 29.6 us; the launch traced here: 29.4 us
  blocking collectives  13.1 us (44%)
  Pallas kernels  5.69 us (19%)
  starting transfers between devices  3.58 us (12%)
  local copies, waits for them, and re-layouts  3.45 us (12%)
  waiting for transfers between devices  2.76 us (9%)
  between operations  0.73 us (2%)
    all_to_all x1, blocking collectives, on_device(): lax.all_to_all(parts, ('freq', 'depth'), split_axis=0, concat_axis=0, til...  13.1 us
    pallas_call x1, Pallas kernels, on_device(): call(functools.partial(local_terms, scale), 'local_terms', [jax.ShapeDtyp...  3.66 us
    ppermute x1, starting transfers between devices, on_device(): near_r = lax.ppermute(own, 'depth', paired)  3.01 us
    ppermute x1, waiting for transfers between devices, on_device(): near_r = lax.ppermute(own, 'depth', paired)  2.76 us
    unnamed x9, local copies, waits for them, and re-layouts  2.3 us
    slice x1, local copies, waits for them, and re-layouts, on_device(): far_a = lax.ppermute(own[:half], ('freq', 'depth'), everywhere)  1.16 us
    pallas_call x1, Pallas kernels, on_device(): call(functools.partial(combine, n_freq, n_depth, share), 'combine', jax.S...  0.69 us
  transfers between devices with their start and end apart: 3, of which 1 were waited for; matrix products, arithmetic and copies ran while one was open for 12% of the time, Pallas kernels for 16%

profile of v9, /device:TPU:0, one launch (start us, length us, event | category | flops | bytes accessed | tf_op | source)
XLA Modules:
  0.0 29.4 jit_solution(11256572578138105901)
XLA Ops:
  0.0 0.0 copy-start
  0.0 0.0 copy-start.1
  0.0 0.0 copy-start.2
  0.0 0.0 copy-start.3
  0.0 3.0 %collective-permute-start.1 = (bf16[2,128,2,256]{3,2,1,0:T(2,128)(2,1)}, bf16[2,128,2,256]{3,2,1,0:T(2,128)(2,1)S(1)}, u32[]{:S(2)}, u32[]{:S(2)}) collective-permute-start(bf16[2,128,2,256]{3,2,1,0:T(2,128)(2,1)} %bitcast.14), channel_id=1, source_target_pairs={{0,1},{1,0},{2,3},{3,2},{4,5},{5,4},{6,7},{7,6},{8,9},{9,8},{10,11... | collective-permute-start | bytes 786440 | tf_op jit(solution)/shard_map/ppermute | solution.py:199
  3.0 1.2 %slice_bitcast_fusion = (bf16[1,128,2,256]{3,2,1,0:T(2,128)(2,1)S(1)}, bf16[1,128,2,256]{3,2,1,0:T(2,128)(2,1)S(1)}) fusion(bf16[2,1,128,2,256]{4,3,2,1,0:T(2,128)(2,1)} %param.7), kind=kLoop, calls=%fused_computation | loop fusion | bytes 524288 | tf_op jit(solution)/shard_map/slice | solution.py:201
  4.2 0.1 collective-permute-start.2
  4.3 0.5 %collective-permute-start = (bf16[1,128,2,256]{3,2,1,0:T(2,128)(2,1)S(1)}, bf16[1,128,2,256]{3,2,1,0:T(2,128)(2,1)S(1)}, u32[]{:S(2)}, u32[]{:S(2)}) collective-permute-start(bf16[1,128,2,256]{3,2,1,0:T(2,128)(2,1)S(1)} %get-tuple-element.12), channel_id=1, source_target_pairs={{1,2},{3,4},{5,6},{7,8},{9,10},{11,12},{13,14},{2,1},{4,3},{6,5},{... | collective-permute-start | bytes 393224 | tf_op jit(solution)/shard_map/ppermute | solution.py:202
  4.8 2.3 %copy.7 = bf16[2,1,384,2,256]{2,4,3,0,1:T(8,128)(2,1)S(1)} copy(bf16[2,1,384,2,256]{4,3,2,1,0:T(2,128)(2,1)} %param.6) | data formatting | bytes 1572864 | tf_op args[0]
  7.7 0.0 copy-done
  7.7 0.0 copy-done.1
  7.7 0.0 copy-done.2
  7.7 0.0 copy-done.3
  7.7 3.7 %local_terms.1 = (f32[3,8,128]{2,1,0:T(8,128)S(1)}, bf16[2,2,256,1024]{3,2,1,0:T(8,128)(2,1)S(1)}, f32[2,1,1024]{2,1,0:T(1,128)S(1)}) custom-call(s32[2]{0:T(128)S(1)} %copy-done.3, f32[1]{0:T(128)S(6)} %copy.8.profile_ref, s32[1,1024]{1,0:T(1,128)S(1)} %bitcast.22, s32[1,1024]{1,0:T(1,128)S(1)} %bitcast.18, bf16[2,2,256,384]{3,2,1,0:T(8,128)(2,1)S(1)} %bitcast.13, ...), custom_call_target="tpu_custom_call" | custom-call | flops 905969664 | bytes 2097152 | tf_op jit(solution)/shard_map/local_terms/pallas_call | solution.py:224
  11.4 0.0 collective-permute-done.2.near_r
  11.4 0.3 %half_term.1.half_ref = f32[8,128]{1,0:T(8,128)S(1)} custom-call(f32[2,1,1024]{2,1,0:T(1,128)S(1)} %get-tuple-element.8.weight_ref, s32[1,1024]{1,0:T(1,128)S(1)} %bitcast.19, bf16[2,2,256,1024]{3,2,1,0:T(8,128)(2,1)S(1)} %get-tuple-element.9.column_ref, bf16[1,128,2,256]{3,2,1,0:T(2,128)(2,1)S(1)} %collective-permute-done.2.near_r), custom_call_target="tpu_custom_call" | custom-call | flops 150994944 | bytes 2097152 | tf_op jit(solution)/shard_map/half_term/pallas_call | solution.py:240
  11.8 2.8 %collective-permute-done.1.near_r = bf16[2,128,2,256]{3,2,1,0:T(2,128)(2,1)S(1)} collective-permute-done((bf16[2,128,2,256]{3,2,1,0:T(2,128)(2,1)}, bf16[2,128,2,256]{3,2,1,0:T(2,128)(2,1)S(1)}, u32[]{:S(2)}, u32[]{:S(2)}) %collective-permute-start.1) | collective-permute-done | bytes 262176 | tf_op jit(solution)/shard_map/ppermute | solution.py:199
  14.5 0.6 %base_rows.1.base = f32[8,8,128]{2,1,0:T(8,128)S(1)} custom-call(f32[2,1,1024]{2,1,0:T(1,128)S(1)} %get-tuple-element.8.weight_ref, s32[1,1024]{1,0:T(1,128)S(1)} %bitcast.20, bf16[2,2,256,1024]{3,2,1,0:T(8,128)(2,1)S(1)} %get-tuple-element.9.column_ref, bf16[2,128,2,256]{3,2,1,0:T(2,128)(2,1)S(1)} %collective-permute-done.1.near_r, ...), custom_call_target="tpu_custom_call" | custom-call | flops 301989888 | bytes 2097152 | tf_op jit(solution)/shard_map/base_rows/pallas_call | solution.py:234
  15.1 0.0 collective-permute-done.far_r
  15.1 0.4 %far_term.1 = f32[64,128]{1,0:T(8,128)S(1)} custom-call(f32[2,1,1024]{2,1,0:T(1,128)S(1)} %get-tuple-element.8.weight_ref, s32[1,1024]{1,0:T(1,128)S(1)} %bitcast.21, bf16[2,2,256,1024]{3,2,1,0:T(8,128)(2,1)S(1)} %get-tuple-element.9.column_ref, bf16[1,128,2,256]{3,2,1,0:T(2,128)(2,1)S(1)} %collective-permute-done.far_r, f32[8,8,128]{2,1,0:T(8,128)S(1)} %base_rows.1.base, ...), custom_call_target="tpu_custom_call" | custom-call | flops 301989888 | bytes 2097152 | tf_op jit(solution)/shard_map/far_term/pallas_call | solution.py:243
  15.5 13.1 %all_to_all.11 = f32[32,2,128]{2,1,0:T(2,128)S(1)} all-to-all(f32[32,2,128]{2,1,0:T(2,128)S(1)} %bitcast.16), channel_id=1, replica_groups=mesh['freq'=2,'depth'=16] {'freq','depth'}, dimensions={0} | all-to-all | bytes 65536 | tf_op jit(solution)/shard_map/all_to_all | solution.py:249
  28.7 0.7 %combine.1 = f32[4,16,32]{2,1,0:T(8,128)} custom-call(f32[64,128]{1,0:T(8,128)S(1)} %bitcast.17), custom_call_target="tpu_custom_call" | custom-call | bytes 2097152 | tf_op jit(solution)/shard_map/combine/pallas_call | solution.py:250
Async XLA Ops:
  0.0 7.7 %copy-start = (bf16[2,1,128,2,256]{4,3,2,1,0:T(2,128)(2,1)S(1)}, bf16[2,1,128,2,256]{4,3,2,1,0:T(2,128)(2,1)}, u32[]{:S(2)}) copy-start(bf16[2,1,128,2,256]{4,3,2,1,0:T(2,128)(2,1)} %param.7) | copy-start | bytes 786436
  0.0 7.7 %copy-start.1 = (s32[1024]{0:T(1024)S(1)}, s32[1024]{0:T(1024)}, u32[]{:S(2)}) copy-start(s32[1024]{0:T(1024)} %param.9) | copy-start | bytes 12292
  0.0 7.7 %copy-start.2 = (s32[1024]{0:T(1024)S(1)}, s32[1024]{0:T(1024)}, u32[]{:S(2)}) copy-start(s32[1024]{0:T(1024)} %param.8) | copy-start | bytes 12292
  0.0 7.7 %copy-start.3 = (s32[2]{0:T(128)S(1)}, s32[2]{0:T(128)}, u32[]{:S(2)}) copy-start(s32[2]{0:T(128)} %bins_ref.1) | copy-start | bytes 28
  0.0 14.5 %collective-permute-start.1 = (bf16[2,128,2,256]{3,2,1,0:T(2,128)(2,1)}, bf16[2,128,2,256]{3,2,1,0:T(2,128)(2,1)S(1)}, u32[]{:S(2)}, u32[]{:S(2)}) collective-permute-start(bf16[2,128,2,256]{3,2,1,0:T(2,128)(2,1)} %bitcast.14), channel_id=1, source_target_pairs={{0,1},{1,0},{2,3},{3,2},{4,5},{5,4},{6,7},{7,6},{8,9},{9,8},{10,11... | collective-permute-start | bytes 786440 | tf_op jit(solution)/shard_map/ppermute | solution.py:199
  4.2 7.2 %collective-permute-start.2 = (bf16[1,128,2,256]{3,2,1,0:T(2,128)(2,1)S(1)}, bf16[1,128,2,256]{3,2,1,0:T(2,128)(2,1)S(1)}, u32[]{:S(2)}, u32[]{:S(2)}) collective-permute-start(bf16[1,128,2,256]{3,2,1,0:T(2,128)(2,1)S(1)} %get-tuple-element.11), channel_id=1, source_target_pairs={{1,2},{3,4},{5,6},{7,8},{9,10},{11,12},{13,14},{2,1},{4,3},{6,5},{... | collective-permute-start | bytes 393224 | tf_op jit(solution)/shard_map/ppermute | solution.py:201
  4.3 10.8 %collective-permute-start = (bf16[1,128,2,256]{3,2,1,0:T(2,128)(2,1)S(1)}, bf16[1,128,2,256]{3,2,1,0:T(2,128)(2,1)S(1)}, u32[]{:S(2)}, u32[]{:S(2)}) collective-permute-start(bf16[1,128,2,256]{3,2,1,0:T(2,128)(2,1)S(1)} %get-tuple-element.12), channel_id=1, source_target_pairs={{1,2},{3,4},{5,6},{7,8},{9,10},{11,12},{13,14},{2,1},{4,3},{6,5},{... | collective-permute-start | bytes 393224 | tf_op jit(solution)/shard_map/ppermute | solution.py:202

commit v10 on v9

--- a/solution.py
+++ b/solution.py
@@ -115,8 +115,8 @@
 def base_rows(share, weight_ref, receiver_ref, column_ref, near_r, terms, out_ref):
     near = layer_term(weight_ref, receiver_ref, column_ref, near_r)
     odd = lax.rem(lax.axis_index("depth"), 2) == 1
-    below = jnp.where(odd, near, 0.0)
-    above = jnp.where(odd, 0.0, near)
+    below = jnp.where(odd, 0.0, near)
+    above = jnp.where(odd, near, 0.0)
     tiles = near.shape[0]
     group = lax.broadcasted_iota(jnp.int32, (tiles, LANES), 1) // share
     in_tile = LANES // share
@@ -132,8 +132,8 @@
     first = column_ref.shape[0] - far_r.shape[0]
     far = half_ref[...] + layer_term(weight_ref, receiver_ref, column_ref, far_r, first)
     odd = lax.rem(lax.axis_index("depth"), 2) == 1
-    below = jnp.where(odd, 0.0, far)
-    above = jnp.where(odd, far, 0.0)
+    below = jnp.where(odd, far, 0.0)
+    above = jnp.where(odd, 0.0, far)
     tiles = far.shape[0]
     last = lax.broadcasted_iota(jnp.int32, (tiles, LANES), 1) // share == 3
     in_tile = LANES // share
@@ -196,10 +196,10 @@
         for group in range(n_freq)
         for end in (0, n_depth - 1)
     ]
-    near_r = lax.ppermute(own, "depth", paired)
     half = local_freqs // 2
-    far_a = lax.ppermute(own[:half], ("freq", "depth"), everywhere)
-    far_b = lax.ppermute(own[half:], ("freq", "depth"), everywhere)
+    far_r = lax.ppermute(own, ("freq", "depth"), everywhere)
+    near_a = lax.ppermute(own[:half], "depth", paired)
+    near_b = lax.ppermute(own[half:], "depth", paired)
 
     green_s = jnp.transpose(green_source[:, 0], (0, 2, 3, 1))
     source_row = source_index.reshape(1, pairs)
@@ -236,16 +236,16 @@
         "base_rows",
         jax.ShapeDtypeStruct((2 * LANES // share, tiles, LANES), jnp.float32),
         0, 5, 1,
-    )(weights, receiver_row, columns, near_r, terms)
+    )(weights, receiver_row, columns, far_r, terms)
     halved = call(half_term, "half_term", term_shape, 0, 4, 0.5)(
-        weights, receiver_row, columns, far_a
+        weights, receiver_row, columns, near_a
     )
     parts = call(
         functools.partial(far_term, share),
         "far_term",
         jax.ShapeDtypeStruct((2 * owners, LANES), jnp.float32),
         0, 6, 1,
-    )(weights, receiver_row, columns, far_b, base, halved)
+    )(weights, receiver_row, columns, near_b, base, halved)
     parts = lax.all_to_all(parts, ("freq", "depth"), split_axis=0, concat_axis=0, tiled=True)
     kernels = call(
         functools.partial(combine, n_freq, n_depth, share),

time: 29.6 us -> 29.5 us (level)
  blocking collectives: 13.1 us -> 11.8 us
  starting transfers between devices: 3.58 us -> 4.66 us
    all_to_all x1, blocking collectives: 13.1 us -> 11.8 us  [on_device(): lax.all_to_all(parts, ('freq', 'depth'), split_axis=0, concat_axis=0, til...]
    ppermute x3, starting transfers between devices: 3.58 us -> 4.66 us  [the longest x1 4.05 us: on_device(): near_a = lax.ppermute(own[:half], 'depth', paired)]
  transfers between devices with their start and end apart: 3 -> 3, of which waited for: 1 -> 2; matrix products, arithmetic and copies ran while one was open for 12% -> 12% of each run, Pallas kernels for 16% -> 16%
where the time goes in v10:
time: 29.5 us; the launch traced here: 29.3 us
  blocking collectives  11.8 us (40%)
  Pallas kernels  5.68 us (19%)
  starting transfers between devices  4.66 us (16%)
  local copies, waits for them, and re-layouts  3.44 us (12%)
  waiting for transfers between devices  2.96 us (10%)
  between operations  0.72 us (2%)
    all_to_all x1, blocking collectives, on_device(): lax.all_to_all(parts, ('freq', 'depth'), split_axis=0, concat_axis=0, til...  11.8 us
    ppermute x1, starting transfers between devices, on_device(): near_a = lax.ppermute(own[:half], 'depth', paired)  4.05 us
    pallas_call x1, Pallas kernels, on_device(): call(functools.partial(local_terms, scale), 'local_terms', [jax.ShapeDtyp...  3.66 us
    unnamed x9, local copies, waits for them, and re-layouts  2.3 us
    ppermute x1, waiting for transfers between devices, on_device(): near_a = lax.ppermute(own[:half], 'depth', paired)  2.24 us
    slice x1, local copies, waits for them, and re-layouts, on_device(): near_a = lax.ppermute(own[:half], 'depth', paired)  1.15 us
    ppermute x1, waiting for transfers between devices, on_device(): near_b = lax.ppermute(own[half:], 'depth', paired)  0.72 us
    pallas_call x1, Pallas kernels, on_device(): call(functools.partial(combine, n_freq, n_depth, share), 'combine', jax.S...  0.69 us
  transfers between devices with their start and end apart: 3, of which 2 were waited for; matrix products, arithmetic and copies ran while one was open for 12% of the time, Pallas kernels for 16%

profile of v10, /device:TPU:0, one launch (start us, length us, event | category | flops | bytes accessed | tf_op | source)
XLA Modules:
  0.0 29.3 jit_solution(9661193767246775470)
XLA Ops:
  0.0 0.0 copy-start
  0.0 0.0 copy-start.1
  0.0 0.0 copy-start.2
  0.0 0.0 copy-start.3
  0.0 0.5 %collective-permute-start.1 = (bf16[2,128,2,256]{3,2,1,0:T(2,128)(2,1)}, bf16[2,128,2,256]{3,2,1,0:T(2,128)(2,1)S(1)}, u32[]{:S(2)}, u32[]{:S(2)}) collective-permute-start(bf16[2,128,2,256]{3,2,1,0:T(2,128)(2,1)} %bitcast.14), channel_id=1, source_target_pairs={{1,2},{3,4},{5,6},{7,8},{9,10},{11,12},{13,14},{2,1},{4,3},{6,5},{... | collective-permute-start | bytes 786440 | tf_op jit(solution)/shard_map/ppermute | solution.py:200
  0.5 1.1 %slice_bitcast_fusion = (bf16[1,128,2,256]{3,2,1,0:T(2,128)(2,1)S(1)}, bf16[1,128,2,256]{3,2,1,0:T(2,128)(2,1)S(1)}) fusion(bf16[2,1,128,2,256]{4,3,2,1,0:T(2,128)(2,1)} %param.7), kind=kLoop, calls=%fused_computation | loop fusion | bytes 524288 | tf_op jit(solution)/shard_map/slice | solution.py:201
  1.7 4.1 %collective-permute-start.2 = (bf16[1,128,2,256]{3,2,1,0:T(2,128)(2,1)S(1)}, bf16[1,128,2,256]{3,2,1,0:T(2,128)(2,1)S(1)}, u32[]{:S(2)}, u32[]{:S(2)}) collective-permute-start(bf16[1,128,2,256]{3,2,1,0:T(2,128)(2,1)S(1)} %get-tuple-element.11), channel_id=1, source_target_pairs={{0,1},{1,0},{2,3},{3,2},{4,5},{5,4},{6,7},{7,6},{8,9},{9,8},{10,11... | collective-permute-start | bytes 393224 | tf_op jit(solution)/shard_map/ppermute | solution.py:201
  5.7 0.1 collective-permute-start
  5.8 2.3 %copy.7 = bf16[2,1,384,2,256]{2,4,3,0,1:T(8,128)(2,1)S(1)} copy(bf16[2,1,384,2,256]{4,3,2,1,0:T(2,128)(2,1)} %param.6) | data formatting | bytes 1572864 | tf_op args[0]
  8.8 0.0 copy-done
  8.8 0.0 copy-done.1
  8.8 0.0 copy-done.2
  8.8 0.0 copy-done.3
  8.8 3.7 %local_terms.1 = (f32[3,8,128]{2,1,0:T(8,128)S(1)}, bf16[2,2,256,1024]{3,2,1,0:T(8,128)(2,1)S(1)}, f32[2,1,1024]{2,1,0:T(1,128)S(1)}) custom-call(s32[2]{0:T(128)S(1)} %copy-done.3, f32[1]{0:T(128)S(6)} %copy.8.profile_ref, s32[1,1024]{1,0:T(1,128)S(1)} %bitcast.22, s32[1,1024]{1,0:T(1,128)S(1)} %bitcast.18, bf16[2,2,256,384]{3,2,1,0:T(8,128)(2,1)S(1)} %bitcast.13, ...), custom_call_target="tpu_custom_call" | custom-call | flops 905969664 | bytes 2097152 | tf_op jit(solution)/shard_map/local_terms/pallas_call | solution.py:224
  12.5 2.2 %collective-permute-done.2.near_r = bf16[1,128,2,256]{3,2,1,0:T(2,128)(2,1)S(1)} collective-permute-done((bf16[1,128,2,256]{3,2,1,0:T(2,128)(2,1)S(1)}, bf16[1,128,2,256]{3,2,1,0:T(2,128)(2,1)S(1)}, u32[]{:S(2)}, u32[]{:S(2)}) %collective-permute-start.2) | collective-permute-done | bytes 131104 | tf_op jit(solution)/shard_map/ppermute | solution.py:201
  14.7 0.3 %half_term.1.half_ref = f32[8,128]{1,0:T(8,128)S(1)} custom-call(f32[2,1,1024]{2,1,0:T(1,128)S(1)} %get-tuple-element.8.weight_ref, s32[1,1024]{1,0:T(1,128)S(1)} %bitcast.19, bf16[2,2,256,1024]{3,2,1,0:T(8,128)(2,1)S(1)} %get-tuple-element.9.column_ref, bf16[1,128,2,256]{3,2,1,0:T(2,128)(2,1)S(1)} %collective-permute-done.2.near_r), custom_call_target="tpu_custom_call" | custom-call | flops 150994944 | bytes 2097152 | tf_op jit(solution)/shard_map/half_term/pallas_call | solution.py:240
  15.0 0.0 collective-permute-done.1.near_r
  15.1 0.6 %base_rows.1.base = f32[8,8,128]{2,1,0:T(8,128)S(1)} custom-call(f32[2,1,1024]{2,1,0:T(1,128)S(1)} %get-tuple-element.8.weight_ref, s32[1,1024]{1,0:T(1,128)S(1)} %bitcast.20, bf16[2,2,256,1024]{3,2,1,0:T(8,128)(2,1)S(1)} %get-tuple-element.9.column_ref, bf16[2,128,2,256]{3,2,1,0:T(2,128)(2,1)S(1)} %collective-permute-done.1.near_r, ...), custom_call_target="tpu_custom_call" | custom-call | flops 301989888 | bytes 2097152 | tf_op jit(solution)/shard_map/base_rows/pallas_call | solution.py:234
  15.6 0.7 %collective-permute-done.far_r = bf16[1,128,2,256]{3,2,1,0:T(2,128)(2,1)S(1)} collective-permute-done((bf16[1,128,2,256]{3,2,1,0:T(2,128)(2,1)S(1)}, bf16[1,128,2,256]{3,2,1,0:T(2,128)(2,1)S(1)}, u32[]{:S(2)}, u32[]{:S(2)}) %collective-permute-start) | collective-permute-done | bytes 131104 | tf_op jit(solution)/shard_map/ppermute | solution.py:202
  16.4 0.4 %far_term.1 = f32[64,128]{1,0:T(8,128)S(1)} custom-call(f32[2,1,1024]{2,1,0:T(1,128)S(1)} %get-tuple-element.8.weight_ref, s32[1,1024]{1,0:T(1,128)S(1)} %bitcast.21, bf16[2,2,256,1024]{3,2,1,0:T(8,128)(2,1)S(1)} %get-tuple-element.9.column_ref, bf16[1,128,2,256]{3,2,1,0:T(2,128)(2,1)S(1)} %collective-permute-done.far_r, f32[8,8,128]{2,1,0:T(8,128)S(1)} %base_rows.1.base, ...), custom_call_target="tpu_custom_call" | custom-call | flops 301989888 | bytes 2097152 | tf_op jit(solution)/shard_map/far_term/pallas_call | solution.py:243
  16.8 11.8 %all_to_all.11 = f32[32,2,128]{2,1,0:T(2,128)S(1)} all-to-all(f32[32,2,128]{2,1,0:T(2,128)S(1)} %bitcast.16), channel_id=1, replica_groups=mesh['freq'=2,'depth'=16] {'freq','depth'}, dimensions={0} | all-to-all | bytes 65536 | tf_op jit(solution)/shard_map/all_to_all | solution.py:249
  28.6 0.7 %combine.1 = f32[4,16,32]{2,1,0:T(8,128)} custom-call(f32[64,128]{1,0:T(8,128)S(1)} %bitcast.17), custom_call_target="tpu_custom_call" | custom-call | bytes 2097152 | tf_op jit(solution)/shard_map/combine/pallas_call | solution.py:250
Async XLA Ops:
  0.0 8.8 %copy-start = (bf16[2,1,128,2,256]{4,3,2,1,0:T(2,128)(2,1)S(1)}, bf16[2,1,128,2,256]{4,3,2,1,0:T(2,128)(2,1)}, u32[]{:S(2)}) copy-start(bf16[2,1,128,2,256]{4,3,2,1,0:T(2,128)(2,1)} %param.7) | copy-start | bytes 786436
  0.0 8.8 %copy-start.1 = (s32[1024]{0:T(1024)S(1)}, s32[1024]{0:T(1024)}, u32[]{:S(2)}) copy-start(s32[1024]{0:T(1024)} %param.9) | copy-start | bytes 12292
  0.0 8.8 %copy-start.2 = (s32[1024]{0:T(1024)S(1)}, s32[1024]{0:T(1024)}, u32[]{:S(2)}) copy-start(s32[1024]{0:T(1024)} %param.8) | copy-start | bytes 12292
  0.0 8.8 %copy-start.3 = (s32[2]{0:T(128)S(1)}, s32[2]{0:T(128)}, u32[]{:S(2)}) copy-start(s32[2]{0:T(128)} %bins_ref.1) | copy-start | bytes 28
  0.0 15.0 %collective-permute-start.1 = (bf16[2,128,2,256]{3,2,1,0:T(2,128)(2,1)}, bf16[2,128,2,256]{3,2,1,0:T(2,128)(2,1)S(1)}, u32[]{:S(2)}, u32[]{:S(2)}) collective-permute-start(bf16[2,128,2,256]{3,2,1,0:T(2,128)(2,1)} %bitcast.14), channel_id=1, source_target_pairs={{1,2},{3,4},{5,6},{7,8},{9,10},{11,12},{13,14},{2,1},{4,3},{6,5},{... | collective-permute-start | bytes 786440 | tf_op jit(solution)/shard_map/ppermute | solution.py:200
  1.7 13.0 %collective-permute-start.2 = (bf16[1,128,2,256]{3,2,1,0:T(2,128)(2,1)S(1)}, bf16[1,128,2,256]{3,2,1,0:T(2,128)(2,1)S(1)}, u32[]{:S(2)}, u32[]{:S(2)}) collective-permute-start(bf16[1,128,2,256]{3,2,1,0:T(2,128)(2,1)S(1)} %get-tuple-element.11), channel_id=1, source_target_pairs={{0,1},{1,0},{2,3},{3,2},{4,5},{5,4},{6,7},{7,6},{8,9},{9,8},{10,11... | collective-permute-start | bytes 393224 | tf_op jit(solution)/shard_map/ppermute | solution.py:201
  5.7 10.6 %collective-permute-start = (bf16[1,128,2,256]{3,2,1,0:T(2,128)(2,1)S(1)}, bf16[1,128,2,256]{3,2,1,0:T(2,128)(2,1)S(1)}, u32[]{:S(2)}, u32[]{:S(2)}) collective-permute-start(bf16[1,128,2,256]{3,2,1,0:T(2,128)(2,1)S(1)} %get-tuple-element.12), channel_id=1, source_target_pairs={{0,1},{1,0},{2,3},{3,2},{4,5},{5,4},{6,7},{7,6},{8,9},{9,8},{10,11... | collective-permute-start | bytes 393224 | tf_op jit(solution)/shard_map/ppermute | solution.py:202

commit v11 on v10

--- a/solution.py
+++ b/solution.py
@@ -100,8 +100,9 @@
     for slot in range(first, first + other_r.shape[0]):
         real, imag = parts_of(other_r[slot - first])
         both = dot(imag, column_ref[slot, 0]) + dot(real, column_ref[slot, 1])
-        total = total + both * weight_ref[slot]
-    return pick_receivers(total, receiver_ref)
+        total = total + (both * weight_ref[slot] if other_r.shape[0] > 1 else both)
+    picked = pick_receivers(total, receiver_ref)
+    return picked if other_r.shape[0] > 1 else picked * weight_ref[first, :, :LANES]
 
 
 def half_term(weight_ref, receiver_ref, column_ref, near_r, out_ref):
@@ -112,12 +113,12 @@
     return pltpu.roll(value, (to - part) * share % LANES, 1) if to != part else value
 
 
-def base_rows(share, weight_ref, receiver_ref, column_ref, near_r, terms, out_ref):
-    near = layer_term(weight_ref, receiver_ref, column_ref, near_r)
+def base_rows(share, weight_ref, receiver_ref, column_ref, far_r, terms, out_ref):
+    far = layer_term(weight_ref, receiver_ref, column_ref, far_r)
     odd = lax.rem(lax.axis_index("depth"), 2) == 1
-    below = jnp.where(odd, 0.0, near)
-    above = jnp.where(odd, near, 0.0)
-    tiles = near.shape[0]
+    below = jnp.where(odd, 0.0, far)
+    above = jnp.where(odd, far, 0.0)
+    tiles = far.shape[0]
     group = lax.broadcasted_iota(jnp.int32, (tiles, LANES), 1) // share
     in_tile = LANES // share
     for part in range(in_tile):
@@ -128,13 +129,13 @@
         out_ref[in_tile + part] = moved(above, share, 0, part)
 
 
-def far_term(share, weight_ref, receiver_ref, column_ref, far_r, base, half_ref, out_ref):
-    first = column_ref.shape[0] - far_r.shape[0]
-    far = half_ref[...] + layer_term(weight_ref, receiver_ref, column_ref, far_r, first)
+def near_term(share, weight_ref, receiver_ref, column_ref, near_r, base, half_ref, out_ref):
+    first = column_ref.shape[0] - near_r.shape[0]
+    near = half_ref[...] + layer_term(weight_ref, receiver_ref, column_ref, near_r, first)
     odd = lax.rem(lax.axis_index("depth"), 2) == 1
-    below = jnp.where(odd, far, 0.0)
-    above = jnp.where(odd, 0.0, far)
-    tiles = far.shape[0]
+    below = jnp.where(odd, near, 0.0)
+    above = jnp.where(odd, 0.0, near)
+    tiles = near.shape[0]
     last = lax.broadcasted_iota(jnp.int32, (tiles, LANES), 1) // share == 3
     in_tile = LANES // share
     for part in range(in_tile):
@@ -241,8 +242,8 @@
         weights, receiver_row, columns, near_a
     )
     parts = call(
-        functools.partial(far_term, share),
-        "far_term",
+        functools.partial(near_term, share),
+        "near_term",
         jax.ShapeDtypeStruct((2 * owners, LANES), jnp.float32),
         0, 6, 1,
     )(weights, receiver_row, columns, near_b, base, halved)

time: 29.5 us -> 29.5 us (level)
  no operation moved by 1% of the time
where the time goes in v11:
time: 29.5 us; the launch traced here: 29.3 us
  blocking collectives  11.8 us (40%)
  Pallas kernels  5.67 us (19%)
  starting transfers between devices  4.66 us (16%)
  local copies, waits for them, and re-layouts  3.44 us (12%)
  waiting for transfers between devices  2.97 us (10%)
  between operations  0.72 us (2%)
    all_to_all x1, blocking collectives, on_device(): lax.all_to_all(parts, ('freq', 'depth'), split_axis=0, concat_axis=0, til...  11.8 us
    ppermute x1, starting transfers between devices, on_device(): near_a = lax.ppermute(own[:half], 'depth', paired)  4.05 us
    pallas_call x1, Pallas kernels, on_device(): call(functools.partial(local_terms, scale), 'local_terms', [jax.ShapeDtyp...  3.66 us
    unnamed x9, local copies, waits for them, and re-layouts  2.3 us
    ppermute x1, waiting for transfers between devices, on_device(): near_a = lax.ppermute(own[:half], 'depth', paired)  2.24 us
    slice x1, local copies, waits for them, and re-layouts, on_device(): near_a = lax.ppermute(own[:half], 'depth', paired)  1.15 us
    ppermute x1, waiting for transfers between devices, on_device(): near_b = lax.ppermute(own[half:], 'depth', paired)  0.73 us
    pallas_call x1, Pallas kernels, on_device(): call(functools.partial(combine, n_freq, n_depth, share), 'combine', jax.S...  0.69 us
  transfers between devices with their start and end apart: 3, of which 2 were waited for; matrix products, arithmetic and copies ran while one was open for 12% of the time, Pallas kernels for 16%

profile of v11, /device:TPU:0, one launch (start us, length us, event | category | flops | bytes accessed | tf_op | source)
XLA Modules:
  0.0 29.3 jit_solution(13762095600513926541)
XLA Ops:
  0.0 0.0 copy-start
  0.0 0.0 copy-start.1
  0.0 0.0 copy-start.2
  0.0 0.0 copy-start.3
  0.0 0.5 %collective-permute-start.1 = (bf16[2,128,2,256]{3,2,1,0:T(2,128)(2,1)}, bf16[2,128,2,256]{3,2,1,0:T(2,128)(2,1)S(1)}, u32[]{:S(2)}, u32[]{:S(2)}) collective-permute-start(bf16[2,128,2,256]{3,2,1,0:T(2,128)(2,1)} %bitcast.14), channel_id=1, source_target_pairs={{1,2},{3,4},{5,6},{7,8},{9,10},{11,12},{13,14},{2,1},{4,3},{6,5},{... | collective-permute-start | bytes 786440 | tf_op jit(solution)/shard_map/ppermute | solution.py:201
  0.5 1.1 %slice_bitcast_fusion = (bf16[1,128,2,256]{3,2,1,0:T(2,128)(2,1)S(1)}, bf16[1,128,2,256]{3,2,1,0:T(2,128)(2,1)S(1)}) fusion(bf16[2,1,128,2,256]{4,3,2,1,0:T(2,128)(2,1)} %param.7), kind=kLoop, calls=%fused_computation | loop fusion | bytes 524288 | tf_op jit(solution)/shard_map/slice | solution.py:202
  1.7 4.1 %collective-permute-start.2 = (bf16[1,128,2,256]{3,2,1,0:T(2,128)(2,1)S(1)}, bf16[1,128,2,256]{3,2,1,0:T(2,128)(2,1)S(1)}, u32[]{:S(2)}, u32[]{:S(2)}) collective-permute-start(bf16[1,128,2,256]{3,2,1,0:T(2,128)(2,1)S(1)} %get-tuple-element.11), channel_id=1, source_target_pairs={{0,1},{1,0},{2,3},{3,2},{4,5},{5,4},{6,7},{7,6},{8,9},{9,8},{10,11... | collective-permute-start | bytes 393224 | tf_op jit(solution)/shard_map/ppermute | solution.py:202
  5.7 0.1 collective-permute-start
  5.8 2.3 %copy.7 = bf16[2,1,384,2,256]{2,4,3,0,1:T(8,128)(2,1)S(1)} copy(bf16[2,1,384,2,256]{4,3,2,1,0:T(2,128)(2,1)} %param.6) | data formatting | bytes 1572864 | tf_op args[0]
  8.8 0.0 copy-done
  8.8 0.0 copy-done.1
  8.8 0.0 copy-done.2
  8.8 0.0 copy-done.3
  8.8 3.7 %local_terms.1 = (f32[3,8,128]{2,1,0:T(8,128)S(1)}, bf16[2,2,256,1024]{3,2,1,0:T(8,128)(2,1)S(1)}, f32[2,1,1024]{2,1,0:T(1,128)S(1)}) custom-call(s32[2]{0:T(128)S(1)} %copy-done.3, f32[1]{0:T(128)S(6)} %copy.8.profile_ref, s32[1,1024]{1,0:T(1,128)S(1)} %bitcast.22, s32[1,1024]{1,0:T(1,128)S(1)} %bitcast.18, bf16[2,2,256,384]{3,2,1,0:T(8,128)(2,1)S(1)} %bitcast.13, ...), custom_call_target="tpu_custom_call" | custom-call | flops 905969664 | bytes 2097152 | tf_op jit(solution)/shard_map/local_terms/pallas_call | solution.py:225
  12.5 2.2 %collective-permute-done.2.near_r = bf16[1,128,2,256]{3,2,1,0:T(2,128)(2,1)S(1)} collective-permute-done((bf16[1,128,2,256]{3,2,1,0:T(2,128)(2,1)S(1)}, bf16[1,128,2,256]{3,2,1,0:T(2,128)(2,1)S(1)}, u32[]{:S(2)}, u32[]{:S(2)}) %collective-permute-start.2) | collective-permute-done | bytes 131104 | tf_op jit(solution)/shard_map/ppermute | solution.py:202
  14.7 0.3 %half_term.1.half_ref = f32[8,128]{1,0:T(8,128)S(1)} custom-call(f32[2,1,1024]{2,1,0:T(1,128)S(1)} %get-tuple-element.8.weight_ref, s32[1,1024]{1,0:T(1,128)S(1)} %bitcast.19, bf16[2,2,256,1024]{3,2,1,0:T(8,128)(2,1)S(1)} %get-tuple-element.9.column_ref, bf16[1,128,2,256]{3,2,1,0:T(2,128)(2,1)S(1)} %collective-permute-done.2.near_r), custom_call_target="tpu_custom_call" | custom-call | flops 150994944 | bytes 2097152 | tf_op jit(solution)/shard_map/half_term/pallas_call | solution.py:241
  15.0 0.0 collective-permute-done.1.far_r
  15.0 0.6 %base_rows.1.base = f32[8,8,128]{2,1,0:T(8,128)S(1)} custom-call(f32[2,1,1024]{2,1,0:T(1,128)S(1)} %get-tuple-element.8.weight_ref, s32[1,1024]{1,0:T(1,128)S(1)} %bitcast.20, bf16[2,2,256,1024]{3,2,1,0:T(8,128)(2,1)S(1)} %get-tuple-element.9.column_ref, bf16[2,128,2,256]{3,2,1,0:T(2,128)(2,1)S(1)} %collective-permute-done.1.far_r, ...), custom_call_target="tpu_custom_call" | custom-call | flops 301989888 | bytes 2097152 | tf_op jit(solution)/shard_map/base_rows/pallas_call | solution.py:235
  15.6 0.7 %collective-permute-done.near_r = bf16[1,128,2,256]{3,2,1,0:T(2,128)(2,1)S(1)} collective-permute-done((bf16[1,128,2,256]{3,2,1,0:T(2,128)(2,1)S(1)}, bf16[1,128,2,256]{3,2,1,0:T(2,128)(2,1)S(1)}, u32[]{:S(2)}, u32[]{:S(2)}) %collective-permute-start) | collective-permute-done | bytes 131104 | tf_op jit(solution)/shard_map/ppermute | solution.py:203
  16.4 0.4 %near_term.1 = f32[64,128]{1,0:T(8,128)S(1)} custom-call(f32[2,1,1024]{2,1,0:T(1,128)S(1)} %get-tuple-element.8.weight_ref, s32[1,1024]{1,0:T(1,128)S(1)} %bitcast.21, bf16[2,2,256,1024]{3,2,1,0:T(8,128)(2,1)S(1)} %get-tuple-element.9.column_ref, bf16[1,128,2,256]{3,2,1,0:T(2,128)(2,1)S(1)} %collective-permute-done.near_r, f32[8,8,128]{2,1,0:T(8,128)S(1)} %base_rows.1.base, ...), custom_call_target="tpu_custom_call" | custom-call | flops 301989888 | bytes 2097152 | tf_op jit(solution)/shard_map/near_term/pallas_call | solution.py:244
  16.8 11.8 %all_to_all.11 = f32[32,2,128]{2,1,0:T(2,128)S(1)} all-to-all(f32[32,2,128]{2,1,0:T(2,128)S(1)} %bitcast.16), channel_id=1, replica_groups=mesh['freq'=2,'depth'=16] {'freq','depth'}, dimensions={0} | all-to-all | bytes 65536 | tf_op jit(solution)/shard_map/all_to_all | solution.py:250
  28.6 0.7 %combine.1 = f32[4,16,32]{2,1,0:T(8,128)} custom-call(f32[64,128]{1,0:T(8,128)S(1)} %bitcast.17), custom_call_target="tpu_custom_call" | custom-call | bytes 2097152 | tf_op jit(solution)/shard_map/combine/pallas_call | solution.py:251
Async XLA Ops:
  0.0 8.8 %copy-start = (bf16[2,1,128,2,256]{4,3,2,1,0:T(2,128)(2,1)S(1)}, bf16[2,1,128,2,256]{4,3,2,1,0:T(2,128)(2,1)}, u32[]{:S(2)}) copy-start(bf16[2,1,128,2,256]{4,3,2,1,0:T(2,128)(2,1)} %param.7) | copy-start | bytes 786436
  0.0 8.8 %copy-start.1 = (s32[1024]{0:T(1024)S(1)}, s32[1024]{0:T(1024)}, u32[]{:S(2)}) copy-start(s32[1024]{0:T(1024)} %param.9) | copy-start | bytes 12292
  0.0 8.8 %copy-start.2 = (s32[1024]{0:T(1024)S(1)}, s32[1024]{0:T(1024)}, u32[]{:S(2)}) copy-start(s32[1024]{0:T(1024)} %param.8) | copy-start | bytes 12292
  0.0 8.8 %copy-start.3 = (s32[2]{0:T(128)S(1)}, s32[2]{0:T(128)}, u32[]{:S(2)}) copy-start(s32[2]{0:T(128)} %bins_ref.1) | copy-start | bytes 28
  0.0 15.0 %collective-permute-start.1 = (bf16[2,128,2,256]{3,2,1,0:T(2,128)(2,1)}, bf16[2,128,2,256]{3,2,1,0:T(2,128)(2,1)S(1)}, u32[]{:S(2)}, u32[]{:S(2)}) collective-permute-start(bf16[2,128,2,256]{3,2,1,0:T(2,128)(2,1)} %bitcast.14), channel_id=1, source_target_pairs={{1,2},{3,4},{5,6},{7,8},{9,10},{11,12},{13,14},{2,1},{4,3},{6,5},{... | collective-permute-start | bytes 786440 | tf_op jit(solution)/shard_map/ppermute | solution.py:201
  1.7 13.0 %collective-permute-start.2 = (bf16[1,128,2,256]{3,2,1,0:T(2,128)(2,1)S(1)}, bf16[1,128,2,256]{3,2,1,0:T(2,128)(2,1)S(1)}, u32[]{:S(2)}, u32[]{:S(2)}) collective-permute-start(bf16[1,128,2,256]{3,2,1,0:T(2,128)(2,1)S(1)} %get-tuple-element.11), channel_id=1, source_target_pairs={{0,1},{1,0},{2,3},{3,2},{4,5},{5,4},{6,7},{7,6},{8,9},{9,8},{10,11... | collective-permute-start | bytes 393224 | tf_op jit(solution)/shard_map/ppermute | solution.py:202
  5.7 10.6 %collective-permute-start = (bf16[1,128,2,256]{3,2,1,0:T(2,128)(2,1)S(1)}, bf16[1,128,2,256]{3,2,1,0:T(2,128)(2,1)S(1)}, u32[]{:S(2)}, u32[]{:S(2)}) collective-permute-start(bf16[1,128,2,256]{3,2,1,0:T(2,128)(2,1)S(1)} %get-tuple-element.12), channel_id=1, source_target_pairs={{0,1},{1,0},{2,3},{3,2},{4,5},{5,4},{6,7},{7,6},{8,9},{9,8},{10,11... | collective-permute-start | bytes 393224 | tf_op jit(solution)/shard_map/ppermute | solution.py:203

commit v12 on v10

--- a/solution.py
+++ b/solution.py
@@ -12,7 +12,7 @@
 WX = 16
 WY = 16
 LANES = 128
-VMEM_BYTES = 48 * 1024 * 1024
+VMEM_BYTES = 24 * 1024 * 1024
 
 
 def dot(left, right):

time: 29.5 us -> 29.5 us (level)
  no operation moved by 1% of the time
where the time goes in v12:
time: 29.5 us; the launch traced here: 29.3 us
  blocking collectives  11.8 us (40%)
  Pallas kernels  5.68 us (19%)
  starting transfers between devices  4.66 us (16%)
  local copies, waits for them, and re-layouts  3.44 us (12%)
  waiting for transfers between devices  2.96 us (10%)
  between operations  0.72 us (2%)
    all_to_all x1, blocking collectives, on_device(): lax.all_to_all(parts, ('freq', 'depth'), split_axis=0, concat_axis=0, til...  11.8 us
    ppermute x1, starting transfers between devices, on_device(): near_a = lax.ppermute(own[:half], 'depth', paired)  4.05 us
    pallas_call x1, Pallas kernels, on_device(): call(functools.partial(local_terms, scale), 'local_terms', [jax.ShapeDtyp...  3.66 us
    unnamed x9, local copies, waits for them, and re-layouts  2.3 us
    ppermute x1, waiting for transfers between devices, on_device(): near_a = lax.ppermute(own[:half], 'depth', paired)  2.24 us
    slice x1, local copies, waits for them, and re-layouts, on_device(): near_a = lax.ppermute(own[:half], 'depth', paired)  1.15 us
    ppermute x1, waiting for transfers between devices, on_device(): near_b = lax.ppermute(own[half:], 'depth', paired)  0.72 us
    pallas_call x1, Pallas kernels, on_device(): call(functools.partial(combine, n_freq, n_depth, share), 'combine', jax.S...  0.69 us
  transfers between devices with their start and end apart: 3, of which 2 were waited for; matrix products, arithmetic and copies ran while one was open for 12% of the time, Pallas kernels for 16%

profile of v12, /device:TPU:0, one launch (start us, length us, event | category | flops | bytes accessed | tf_op | source)
XLA Modules:
  0.0 29.3 jit_solution(10993901328563754220)
XLA Ops:
  0.0 0.0 copy-start
  0.0 0.0 copy-start.1
  0.0 0.0 copy-start.2
  0.0 0.0 copy-start.3
  0.0 0.5 %collective-permute-start.1 = (bf16[2,128,2,256]{3,2,1,0:T(2,128)(2,1)}, bf16[2,128,2,256]{3,2,1,0:T(2,128)(2,1)S(1)}, u32[]{:S(2)}, u32[]{:S(2)}) collective-permute-start(bf16[2,128,2,256]{3,2,1,0:T(2,128)(2,1)} %bitcast.14), channel_id=1, source_target_pairs={{1,2},{3,4},{5,6},{7,8},{9,10},{11,12},{13,14},{2,1},{4,3},{6,5},{... | collective-permute-start | bytes 786440 | tf_op jit(solution)/shard_map/ppermute | solution.py:200
  0.5 1.1 %slice_bitcast_fusion = (bf16[1,128,2,256]{3,2,1,0:T(2,128)(2,1)S(1)}, bf16[1,128,2,256]{3,2,1,0:T(2,128)(2,1)S(1)}) fusion(bf16[2,1,128,2,256]{4,3,2,1,0:T(2,128)(2,1)} %param.7), kind=kLoop, calls=%fused_computation | loop fusion | bytes 524288 | tf_op jit(solution)/shard_map/slice | solution.py:201
  1.7 4.1 %collective-permute-start.2 = (bf16[1,128,2,256]{3,2,1,0:T(2,128)(2,1)S(1)}, bf16[1,128,2,256]{3,2,1,0:T(2,128)(2,1)S(1)}, u32[]{:S(2)}, u32[]{:S(2)}) collective-permute-start(bf16[1,128,2,256]{3,2,1,0:T(2,128)(2,1)S(1)} %get-tuple-element.11), channel_id=1, source_target_pairs={{0,1},{1,0},{2,3},{3,2},{4,5},{5,4},{6,7},{7,6},{8,9},{9,8},{10,11... | collective-permute-start | bytes 393224 | tf_op jit(solution)/shard_map/ppermute | solution.py:201
  5.7 0.1 collective-permute-start
  5.8 2.3 %copy.7 = bf16[2,1,384,2,256]{2,4,3,0,1:T(8,128)(2,1)S(1)} copy(bf16[2,1,384,2,256]{4,3,2,1,0:T(2,128)(2,1)} %param.6) | data formatting | bytes 1572864 | tf_op args[0]
  8.8 0.0 copy-done
  8.8 0.0 copy-done.1
  8.8 0.0 copy-done.2
  8.8 0.0 copy-done.3
  8.8 3.7 %local_terms.1 = (f32[3,8,128]{2,1,0:T(8,128)S(1)}, bf16[2,2,256,1024]{3,2,1,0:T(8,128)(2,1)S(1)}, f32[2,1,1024]{2,1,0:T(1,128)S(1)}) custom-call(s32[2]{0:T(128)S(1)} %copy-done.3, f32[1]{0:T(128)S(6)} %copy.8.profile_ref, s32[1,1024]{1,0:T(1,128)S(1)} %bitcast.22, s32[1,1024]{1,0:T(1,128)S(1)} %bitcast.18, bf16[2,2,256,384]{3,2,1,0:T(8,128)(2,1)S(1)} %bitcast.13, ...), custom_call_target="tpu_custom_call" | custom-call | flops 905969664 | bytes 2097152 | tf_op jit(solution)/shard_map/local_terms/pallas_call | solution.py:224
  12.5 2.2 %collective-permute-done.2.near_r = bf16[1,128,2,256]{3,2,1,0:T(2,128)(2,1)S(1)} collective-permute-done((bf16[1,128,2,256]{3,2,1,0:T(2,128)(2,1)S(1)}, bf16[1,128,2,256]{3,2,1,0:T(2,128)(2,1)S(1)}, u32[]{:S(2)}, u32[]{:S(2)}) %collective-permute-start.2) | collective-permute-done | bytes 131104 | tf_op jit(solution)/shard_map/ppermute | solution.py:201
  14.7 0.3 %half_term.1.half_ref = f32[8,128]{1,0:T(8,128)S(1)} custom-call(f32[2,1,1024]{2,1,0:T(1,128)S(1)} %get-tuple-element.8.weight_ref, s32[1,1024]{1,0:T(1,128)S(1)} %bitcast.19, bf16[2,2,256,1024]{3,2,1,0:T(8,128)(2,1)S(1)} %get-tuple-element.9.column_ref, bf16[1,128,2,256]{3,2,1,0:T(2,128)(2,1)S(1)} %collective-permute-done.2.near_r), custom_call_target="tpu_custom_call" | custom-call | flops 150994944 | bytes 2097152 | tf_op jit(solution)/shard_map/half_term/pallas_call | solution.py:240
  15.0 0.0 collective-permute-done.1.near_r
  15.1 0.6 %base_rows.1.base = f32[8,8,128]{2,1,0:T(8,128)S(1)} custom-call(f32[2,1,1024]{2,1,0:T(1,128)S(1)} %get-tuple-element.8.weight_ref, s32[1,1024]{1,0:T(1,128)S(1)} %bitcast.20, bf16[2,2,256,1024]{3,2,1,0:T(8,128)(2,1)S(1)} %get-tuple-element.9.column_ref, bf16[2,128,2,256]{3,2,1,0:T(2,128)(2,1)S(1)} %collective-permute-done.1.near_r, ...), custom_call_target="tpu_custom_call" | custom-call | flops 301989888 | bytes 2097152 | tf_op jit(solution)/shard_map/base_rows/pallas_call | solution.py:234
  15.6 0.7 %collective-permute-done.far_r = bf16[1,128,2,256]{3,2,1,0:T(2,128)(2,1)S(1)} collective-permute-done((bf16[1,128,2,256]{3,2,1,0:T(2,128)(2,1)S(1)}, bf16[1,128,2,256]{3,2,1,0:T(2,128)(2,1)S(1)}, u32[]{:S(2)}, u32[]{:S(2)}) %collective-permute-start) | collective-permute-done | bytes 131104 | tf_op jit(solution)/shard_map/ppermute | solution.py:202
  16.4 0.4 %far_term.1 = f32[64,128]{1,0:T(8,128)S(1)} custom-call(f32[2,1,1024]{2,1,0:T(1,128)S(1)} %get-tuple-element.8.weight_ref, s32[1,1024]{1,0:T(1,128)S(1)} %bitcast.21, bf16[2,2,256,1024]{3,2,1,0:T(8,128)(2,1)S(1)} %get-tuple-element.9.column_ref, bf16[1,128,2,256]{3,2,1,0:T(2,128)(2,1)S(1)} %collective-permute-done.far_r, f32[8,8,128]{2,1,0:T(8,128)S(1)} %base_rows.1.base, ...), custom_call_target="tpu_custom_call" | custom-call | flops 301989888 | bytes 2097152 | tf_op jit(solution)/shard_map/far_term/pallas_call | solution.py:243
  16.8 11.8 %all_to_all.11 = f32[32,2,128]{2,1,0:T(2,128)S(1)} all-to-all(f32[32,2,128]{2,1,0:T(2,128)S(1)} %bitcast.16), channel_id=1, replica_groups=mesh['freq'=2,'depth'=16] {'freq','depth'}, dimensions={0} | all-to-all | bytes 65536 | tf_op jit(solution)/shard_map/all_to_all | solution.py:249
  28.6 0.7 %combine.1 = f32[4,16,32]{2,1,0:T(8,128)} custom-call(f32[64,128]{1,0:T(8,128)S(1)} %bitcast.17), custom_call_target="tpu_custom_call" | custom-call | bytes 2097152 | tf_op jit(solution)/shard_map/combine/pallas_call | solution.py:250
Async XLA Ops:
  0.0 8.8 %copy-start = (bf16[2,1,128,2,256]{4,3,2,1,0:T(2,128)(2,1)S(1)}, bf16[2,1,128,2,256]{4,3,2,1,0:T(2,128)(2,1)}, u32[]{:S(2)}) copy-start(bf16[2,1,128,2,256]{4,3,2,1,0:T(2,128)(2,1)} %param.7) | copy-start | bytes 786436
  0.0 8.8 %copy-start.1 = (s32[1024]{0:T(1024)S(1)}, s32[1024]{0:T(1024)}, u32[]{:S(2)}) copy-start(s32[1024]{0:T(1024)} %param.9) | copy-start | bytes 12292
  0.0 8.8 %copy-start.2 = (s32[1024]{0:T(1024)S(1)}, s32[1024]{0:T(1024)}, u32[]{:S(2)}) copy-start(s32[1024]{0:T(1024)} %param.8) | copy-start | bytes 12292
  0.0 8.8 %copy-start.3 = (s32[2]{0:T(128)S(1)}, s32[2]{0:T(128)}, u32[]{:S(2)}) copy-start(s32[2]{0:T(128)} %bins_ref.1) | copy-start | bytes 28
  0.0 15.0 %collective-permute-start.1 = (bf16[2,128,2,256]{3,2,1,0:T(2,128)(2,1)}, bf16[2,128,2,256]{3,2,1,0:T(2,128)(2,1)S(1)}, u32[]{:S(2)}, u32[]{:S(2)}) collective-permute-start(bf16[2,128,2,256]{3,2,1,0:T(2,128)(2,1)} %bitcast.14), channel_id=1, source_target_pairs={{1,2},{3,4},{5,6},{7,8},{9,10},{11,12},{13,14},{2,1},{4,3},{6,5},{... | collective-permute-start | bytes 786440 | tf_op jit(solution)/shard_map/ppermute | solution.py:200
  1.7 13.0 %collective-permute-start.2 = (bf16[1,128,2,256]{3,2,1,0:T(2,128)(2,1)S(1)}, bf16[1,128,2,256]{3,2,1,0:T(2,128)(2,1)S(1)}, u32[]{:S(2)}, u32[]{:S(2)}) collective-permute-start(bf16[1,128,2,256]{3,2,1,0:T(2,128)(2,1)S(1)} %get-tuple-element.11), channel_id=1, source_target_pairs={{0,1},{1,0},{2,3},{3,2},{4,5},{5,4},{6,7},{7,6},{8,9},{9,8},{10,11... | collective-permute-start | bytes 393224 | tf_op jit(solution)/shard_map/ppermute | solution.py:201
  5.7 10.6 %collective-permute-start = (bf16[1,128,2,256]{3,2,1,0:T(2,128)(2,1)S(1)}, bf16[1,128,2,256]{3,2,1,0:T(2,128)(2,1)S(1)}, u32[]{:S(2)}, u32[]{:S(2)}) collective-permute-start(bf16[1,128,2,256]{3,2,1,0:T(2,128)(2,1)S(1)} %get-tuple-element.12), channel_id=1, source_target_pairs={{0,1},{1,0},{2,3},{3,2},{4,5},{5,4},{6,7},{7,6},{8,9},{9,8},{10,11... | collective-permute-start | bytes 393224 | tf_op jit(solution)/shard_map/ppermute | solution.py:202

commit v13 on v10

--- a/solution.py
+++ b/solution.py
@@ -125,7 +125,7 @@
         for k in range(3):
             first = jnp.where(group == k, moved(terms[k], share, k, part), first)
         out_ref[part] = first
-        out_ref[in_tile + part] = moved(above, share, 0, part)
+        out_ref[in_tile + part] = moved(above, share, 3, part)
 
 
 def far_term(share, weight_ref, receiver_ref, column_ref, far_r, base, half_ref, out_ref):
@@ -142,7 +142,7 @@
         out_ref[pl.ds(2 * part, tiles, stride=2 * in_tile), :] = base[part] + own
         out_ref[pl.ds(2 * part + 1, tiles, stride=2 * in_tile), :] = base[
             in_tile + part
-        ] + moved(above, share, 0, part)
+        ] + moved(above, share, 3, part)
 
 
 def combine(freqs, depths, share, parts_ref, out_ref):
@@ -158,7 +158,7 @@
     below = jnp.where(depth == 0, 0.0, pltpu.roll(second, 1, 0))
     for k in range(3):
         out_ref[k] = pltpu.roll(first, (LANES - k * share) % LANES, 1)[:, :share]
-    out_ref[3] = (pltpu.roll(above, LANES - 3 * share, 1) - below)[:, :share]
+    out_ref[3] = pltpu.roll(above - below, LANES - 3 * share, 1)[:, :share]
 
 
 def vmem(count):

time: 29.5 us -> 29.5 us (level)
  no operation moved by 1% of the time
where the time goes in v13:
time: 29.5 us; the launch traced here: 29.3 us
  blocking collectives  11.8 us (40%)
  Pallas kernels  5.68 us (19%)
  starting transfers between devices  4.66 us (16%)
  local copies, waits for them, and re-layouts  3.44 us (12%)
  waiting for transfers between devices  2.96 us (10%)
  between operations  0.72 us (2%)
    all_to_all x1, blocking collectives, on_device(): lax.all_to_all(parts, ('freq', 'depth'), split_axis=0, concat_axis=0, til...  11.8 us
    ppermute x1, starting transfers between devices, on_device(): near_a = lax.ppermute(own[:half], 'depth', paired)  4.05 us
    pallas_call x1, Pallas kernels, on_device(): call(functools.partial(local_terms, scale), 'local_terms', [jax.ShapeDtyp...  3.66 us
    unnamed x9, local copies, waits for them, and re-layouts  2.3 us
    ppermute x1, waiting for transfers between devices, on_device(): near_a = lax.ppermute(own[:half], 'depth', paired)  2.24 us
    slice x1, local copies, waits for them, and re-layouts, on_device(): near_a = lax.ppermute(own[:half], 'depth', paired)  1.15 us
    ppermute x1, waiting for transfers between devices, on_device(): near_b = lax.ppermute(own[half:], 'depth', paired)  0.72 us
    pallas_call x1, Pallas kernels, on_device(): call(functools.partial(combine, n_freq, n_depth, share), 'combine', jax.S...  0.69 us
  transfers between devices with their start and end apart: 3, of which 2 were waited for; matrix products, arithmetic and copies ran while one was open for 12% of the time, Pallas kernels for 16%

profile of v13, /device:TPU:0, one launch (start us, length us, event | category | flops | bytes accessed | tf_op | source)
XLA Modules:
  0.0 29.3 jit_solution(16510679301511444744)
XLA Ops:
  0.0 0.0 copy-start
  0.0 0.0 copy-start.1
  0.0 0.0 copy-start.2
  0.0 0.0 copy-start.3
  0.0 0.5 %collective-permute-start.1 = (bf16[2,128,2,256]{3,2,1,0:T(2,128)(2,1)}, bf16[2,128,2,256]{3,2,1,0:T(2,128)(2,1)S(1)}, u32[]{:S(2)}, u32[]{:S(2)}) collective-permute-start(bf16[2,128,2,256]{3,2,1,0:T(2,128)(2,1)} %bitcast.14), channel_id=1, source_target_pairs={{1,2},{3,4},{5,6},{7,8},{9,10},{11,12},{13,14},{2,1},{4,3},{6,5},{... | collective-permute-start | bytes 786440 | tf_op jit(solution)/shard_map/ppermute | solution.py:200
  0.5 1.1 %slice_bitcast_fusion = (bf16[1,128,2,256]{3,2,1,0:T(2,128)(2,1)S(1)}, bf16[1,128,2,256]{3,2,1,0:T(2,128)(2,1)S(1)}) fusion(bf16[2,1,128,2,256]{4,3,2,1,0:T(2,128)(2,1)} %param.7), kind=kLoop, calls=%fused_computation | loop fusion | bytes 524288 | tf_op jit(solution)/shard_map/slice | solution.py:201
  1.7 4.1 %collective-permute-start.2 = (bf16[1,128,2,256]{3,2,1,0:T(2,128)(2,1)S(1)}, bf16[1,128,2,256]{3,2,1,0:T(2,128)(2,1)S(1)}, u32[]{:S(2)}, u32[]{:S(2)}) collective-permute-start(bf16[1,128,2,256]{3,2,1,0:T(2,128)(2,1)S(1)} %get-tuple-element.11), channel_id=1, source_target_pairs={{0,1},{1,0},{2,3},{3,2},{4,5},{5,4},{6,7},{7,6},{8,9},{9,8},{10,11... | collective-permute-start | bytes 393224 | tf_op jit(solution)/shard_map/ppermute | solution.py:201
  5.7 0.1 collective-permute-start
  5.8 2.3 %copy.7 = bf16[2,1,384,2,256]{2,4,3,0,1:T(8,128)(2,1)S(1)} copy(bf16[2,1,384,2,256]{4,3,2,1,0:T(2,128)(2,1)} %param.6) | data formatting | bytes 1572864 | tf_op args[0]
  8.8 0.0 copy-done
  8.8 0.0 copy-done.1
  8.8 0.0 copy-done.2
  8.8 0.0 copy-done.3
  8.8 3.7 %local_terms.1 = (f32[3,8,128]{2,1,0:T(8,128)S(1)}, bf16[2,2,256,1024]{3,2,1,0:T(8,128)(2,1)S(1)}, f32[2,1,1024]{2,1,0:T(1,128)S(1)}) custom-call(s32[2]{0:T(128)S(1)} %copy-done.3, f32[1]{0:T(128)S(6)} %copy.8.profile_ref, s32[1,1024]{1,0:T(1,128)S(1)} %bitcast.22, s32[1,1024]{1,0:T(1,128)S(1)} %bitcast.18, bf16[2,2,256,384]{3,2,1,0:T(8,128)(2,1)S(1)} %bitcast.13, ...), custom_call_target="tpu_custom_call" | custom-call | flops 905969664 | bytes 2097152 | tf_op jit(solution)/shard_map/local_terms/pallas_call | solution.py:224
  12.5 2.2 %collective-permute-done.2.near_r = bf16[1,128,2,256]{3,2,1,0:T(2,128)(2,1)S(1)} collective-permute-done((bf16[1,128,2,256]{3,2,1,0:T(2,128)(2,1)S(1)}, bf16[1,128,2,256]{3,2,1,0:T(2,128)(2,1)S(1)}, u32[]{:S(2)}, u32[]{:S(2)}) %collective-permute-start.2) | collective-permute-done | bytes 131104 | tf_op jit(solution)/shard_map/ppermute | solution.py:201
  14.7 0.3 %half_term.1.half_ref = f32[8,128]{1,0:T(8,128)S(1)} custom-call(f32[2,1,1024]{2,1,0:T(1,128)S(1)} %get-tuple-element.8.weight_ref, s32[1,1024]{1,0:T(1,128)S(1)} %bitcast.19, bf16[2,2,256,1024]{3,2,1,0:T(8,128)(2,1)S(1)} %get-tuple-element.9.column_ref, bf16[1,128,2,256]{3,2,1,0:T(2,128)(2,1)S(1)} %collective-permute-done.2.near_r), custom_call_target="tpu_custom_call" | custom-call | flops 150994944 | bytes 2097152 | tf_op jit(solution)/shard_map/half_term/pallas_call | solution.py:240
  15.0 0.0 collective-permute-done.1.near_r
  15.1 0.6 %base_rows.1.base = f32[8,8,128]{2,1,0:T(8,128)S(1)} custom-call(f32[2,1,1024]{2,1,0:T(1,128)S(1)} %get-tuple-element.8.weight_ref, s32[1,1024]{1,0:T(1,128)S(1)} %bitcast.20, bf16[2,2,256,1024]{3,2,1,0:T(8,128)(2,1)S(1)} %get-tuple-element.9.column_ref, bf16[2,128,2,256]{3,2,1,0:T(2,128)(2,1)S(1)} %collective-permute-done.1.near_r, ...), custom_call_target="tpu_custom_call" | custom-call | flops 301989888 | bytes 2097152 | tf_op jit(solution)/shard_map/base_rows/pallas_call | solution.py:234
  15.6 0.7 %collective-permute-done.far_r = bf16[1,128,2,256]{3,2,1,0:T(2,128)(2,1)S(1)} collective-permute-done((bf16[1,128,2,256]{3,2,1,0:T(2,128)(2,1)S(1)}, bf16[1,128,2,256]{3,2,1,0:T(2,128)(2,1)S(1)}, u32[]{:S(2)}, u32[]{:S(2)}) %collective-permute-start) | collective-permute-done | bytes 131104 | tf_op jit(solution)/shard_map/ppermute | solution.py:202
  16.4 0.4 %far_term.1 = f32[64,128]{1,0:T(8,128)S(1)} custom-call(f32[2,1,1024]{2,1,0:T(1,128)S(1)} %get-tuple-element.8.weight_ref, s32[1,1024]{1,0:T(1,128)S(1)} %bitcast.21, bf16[2,2,256,1024]{3,2,1,0:T(8,128)(2,1)S(1)} %get-tuple-element.9.column_ref, bf16[1,128,2,256]{3,2,1,0:T(2,128)(2,1)S(1)} %collective-permute-done.far_r, f32[8,8,128]{2,1,0:T(8,128)S(1)} %base_rows.1.base, ...), custom_call_target="tpu_custom_call" | custom-call | flops 301989888 | bytes 2097152 | tf_op jit(solution)/shard_map/far_term/pallas_call | solution.py:243
  16.8 11.8 %all_to_all.11 = f32[32,2,128]{2,1,0:T(2,128)S(1)} all-to-all(f32[32,2,128]{2,1,0:T(2,128)S(1)} %bitcast.16), channel_id=1, replica_groups=mesh['freq'=2,'depth'=16] {'freq','depth'}, dimensions={0} | all-to-all | bytes 65536 | tf_op jit(solution)/shard_map/all_to_all | solution.py:249
  28.6 0.7 %combine.1 = f32[4,16,32]{2,1,0:T(8,128)} custom-call(f32[64,128]{1,0:T(8,128)S(1)} %bitcast.17), custom_call_target="tpu_custom_call" | custom-call | bytes 2097152 | tf_op jit(solution)/shard_map/combine/pallas_call | solution.py:250
Async XLA Ops:
  0.0 8.8 %copy-start = (bf16[2,1,128,2,256]{4,3,2,1,0:T(2,128)(2,1)S(1)}, bf16[2,1,128,2,256]{4,3,2,1,0:T(2,128)(2,1)}, u32[]{:S(2)}) copy-start(bf16[2,1,128,2,256]{4,3,2,1,0:T(2,128)(2,1)} %param.7) | copy-start | bytes 786436
  0.0 8.8 %copy-start.1 = (s32[1024]{0:T(1024)S(1)}, s32[1024]{0:T(1024)}, u32[]{:S(2)}) copy-start(s32[1024]{0:T(1024)} %param.9) | copy-start | bytes 12292
  0.0 8.8 %copy-start.2 = (s32[1024]{0:T(1024)S(1)}, s32[1024]{0:T(1024)}, u32[]{:S(2)}) copy-start(s32[1024]{0:T(1024)} %param.8) | copy-start | bytes 12292
  0.0 8.8 %copy-start.3 = (s32[2]{0:T(128)S(1)}, s32[2]{0:T(128)}, u32[]{:S(2)}) copy-start(s32[2]{0:T(128)} %bins_ref.1) | copy-start | bytes 28
  0.0 15.0 %collective-permute-start.1 = (bf16[2,128,2,256]{3,2,1,0:T(2,128)(2,1)}, bf16[2,128,2,256]{3,2,1,0:T(2,128)(2,1)S(1)}, u32[]{:S(2)}, u32[]{:S(2)}) collective-permute-start(bf16[2,128,2,256]{3,2,1,0:T(2,128)(2,1)} %bitcast.14), channel_id=1, source_target_pairs={{1,2},{3,4},{5,6},{7,8},{9,10},{11,12},{13,14},{2,1},{4,3},{6,5},{... | collective-permute-start | bytes 786440 | tf_op jit(solution)/shard_map/ppermute | solution.py:200
  1.7 13.0 %collective-permute-start.2 = (bf16[1,128,2,256]{3,2,1,0:T(2,128)(2,1)S(1)}, bf16[1,128,2,256]{3,2,1,0:T(2,128)(2,1)S(1)}, u32[]{:S(2)}, u32[]{:S(2)}) collective-permute-start(bf16[1,128,2,256]{3,2,1,0:T(2,128)(2,1)S(1)} %get-tuple-element.11), channel_id=1, source_target_pairs={{0,1},{1,0},{2,3},{3,2},{4,5},{5,4},{6,7},{7,6},{8,9},{9,8},{10,11... | collective-permute-start | bytes 393224 | tf_op jit(solution)/shard_map/ppermute | solution.py:201
  5.7 10.6 %collective-permute-start = (bf16[1,128,2,256]{3,2,1,0:T(2,128)(2,1)S(1)}, bf16[1,128,2,256]{3,2,1,0:T(2,128)(2,1)S(1)}, u32[]{:S(2)}, u32[]{:S(2)}) collective-permute-start(bf16[1,128,2,256]{3,2,1,0:T(2,128)(2,1)S(1)} %get-tuple-element.12), channel_id=1, source_target_pairs={{0,1},{1,0},{2,3},{3,2},{4,5},{5,4},{6,7},{7,6},{8,9},{9,8},{10,11... | collective-permute-start | bytes 393224 | tf_op jit(solution)/shard_map/ppermute | solution.py:202
